TPU v7x, 32 devices: a whole 2x2x4 slice. The times are simulated.
32 devices in a mesh: fsdp: 8 (over y, x, core), tensor: 4 (over z).
Axes of the slice: x: 2, y: 2, z: 4, core: 2. Of those that a mesh axis runs over, the one named last changes fastest.
Arguments:
- hidden: bfloat16 [2, 8192, 768], P(None, ('fsdp', 'tensor')), may hold values from -6 to 6
- passages: bfloat16 [2, 20480, 768], P(None, ('fsdp', 'tensor')), may hold values from -6 to 6
- block_ids: int32 [2, 8192], P(None, 'fsdp'), may hold values from 0 to 8191, as said below
- buckets: int32 [256, 256], replicated, may hold values from 0 to 31
- norm_gains: bfloat16 [768, 3], P('fsdp'), may hold values from 0.099609375 to 1.8984375
- self_query: bfloat16 [768, 768], P('fsdp', 'tensor'), may hold values from -0.109375 to 0.109375
- self_key: bfloat16 [768, 768], P('fsdp', 'tensor'), may hold values from -0.109375 to 0.109375
- self_value: bfloat16 [768, 768], P('fsdp', 'tensor'), may hold values from -0.21875 to 0.21875
- self_out: bfloat16 [768, 768], P('fsdp', 'tensor'), may hold values from -0.4375 to 0.4375
- cross_query: bfloat16 [768, 768], P('fsdp', 'tensor'), may hold values from -0.109375 to 0.109375
- cross_key: bfloat16 [768, 768], P('fsdp', 'tensor'), may hold values from -0.109375 to 0.109375
- cross_value: bfloat16 [768, 768], P('fsdp', 'tensor'), may hold values from -0.21875 to 0.21875
- cross_out: bfloat16 [768, 768], P('fsdp', 'tensor'), may hold values from -0.4375 to 0.4375
- ffn_in: bfloat16 [768, 3072], P('fsdp', 'tensor'), may hold values from -0.21875 to 0.21875
- ffn_out: bfloat16 [768, 3072], P('fsdp', 'tensor'), may hold values from -0.15625 to 0.15625
- rel_bias: float32 [32, 12], replicated, may hold values from -4 to 4
- out_grad: bfloat16 [2, 8192, 768], P(None, ('fsdp', 'tensor')), may hold values from -6 to 6
Outputs:
- output: bfloat16 [2, 8192, 768], P(None, ('fsdp', 'tensor'))
- hidden_grad: float32 [2, 8192, 768], P(None, ('fsdp', 'tensor'))
- passages_grad: float32 [2, 20480, 768], P(None, ('fsdp', 'tensor'))
- norm_gains_grad: float32 [768, 3], replicated
- self_query_grad: float32 [768, 768], P('fsdp', 'tensor')
- self_key_grad: float32 [768, 768], P('fsdp', 'tensor')
- self_value_grad: float32 [768, 768], P('fsdp', 'tensor')
- self_out_grad: float32 [768, 768], P('fsdp', 'tensor')
- cross_query_grad: float32 [768, 768], P('fsdp', 'tensor')
- cross_key_grad: float32 [768, 768], P('fsdp', 'tensor')
- cross_value_grad: float32 [768, 768], P('fsdp', 'tensor')
- cross_out_grad: float32 [768, 768], P('fsdp', 'tensor')
- ffn_in_grad: float32 [768, 3072], P('fsdp', 'tensor')
- ffn_out_grad: float32 [768, 3072], P('fsdp', 'tensor')
- rel_bias_grad: float32 [32, 12], replicated
Inputs may be any that keep to these rules, and one draw needn't show every extreme that they name: `block_ids`: along each row a token's id is 256 times the index of its aligned window plus the position, inside that window, of the first token of its segment; so ids never fall and a segment never crosses aligned windows of 256 tokens.
All inputs are finite; a program needn't handle non-finite values.
Results may differ from a plain program's by a relative error of at most 0.024.
The roundings to bfloat16 on the way count: a program that leaves them out, or rounds other values in their place, can miss the bound.
Values may be sent and summed in bfloat16 or wider, within the bound.
No kernel may reach another device: no remote copies, remote signals or barrier semaphores. Data moves between devices by JAX's collectives and lax.ppermute only.
A program may use at most 256 MiB of HBM per device.

v0:
```python
import jax
import jax.numpy as jnp
from jax import lax
from jax.sharding import PartitionSpec as P

DH = 64
WIN = 256


EPSILON = 1e-06
MASKED = -1000000000.0
HIGHEST = lax.Precision.HIGHEST


def for_sending(shard):
    return jax.tree.map(lambda a: a.astype(jnp.bfloat16) if a.dtype == jnp.float32 else a, shard)


def times_plain(left, weight):
    return jnp.dot(left, weight, preferred_element_type=jnp.float32)


def times_back(left, weight):
    return lax.dot_general(
        left, weight, (((1,), (1,)), ((), ())), preferred_element_type=jnp.float32
    )


def weight_grad(inputs, grads):
    return lax.dot_general(
        inputs, grads, (((0,), (0,)), ((), ())), preferred_element_type=jnp.float32
    )


def smooth_gate(values):
    return jax.nn.gelu(values, approximate=True)


def gate_back(pre_values, incoming):
    _, pullback = jax.vjp(smooth_gate, pre_values)
    return pullback(incoming)[0]


def norm_rows(stream, gain):
    scale = lax.rsqrt(jnp.mean(stream * stream, axis=-1, keepdims=True) + EPSILON)
    return ((stream * scale * gain).astype(jnp.bfloat16), scale)


def norm_back(stream, scale, gain, incoming):
    scaled = incoming * gain
    along = jnp.mean(scaled * stream, axis=-1, keepdims=True)
    return (
        scale * scaled - stream * (scale * scale * scale) * along,
        jnp.sum(incoming * stream * scale, axis=0),
    )


def spread_rows(normed):
    return lax.all_gather(normed, "tensor", axis=0, tiled=True)


def spread_grads(branch_grad):
    return lax.all_gather(branch_grad, "tensor", axis=0, tiled=True)


def combine_rows(values, weight, row_count):

    def row_term(first_row, row_total):
        return times_back(values, weight)

    return lax.psum_scatter(
        row_term(jnp.int32(0), row_count * lax.axis_size("tensor")),
        "tensor",
        scatter_dimension=0,
        tiled=True,
    )


def combine_grads(values, weight, row_count):

    def row_term(first_row, row_total):
        return times_back(values, weight)

    return lax.psum_scatter(
        row_term(jnp.int32(0), row_count * lax.axis_size("tensor")),
        "tensor",
        scatter_dimension=0,
        tiled=True,
    )


def self_scores(query_tile, key_tile, segment_tile, tile_bias):
    raw_scores = (
        jnp.einsum("qhd,khd->hqk", query_tile, key_tile, preferred_element_type=jnp.float32)
        + tile_bias
    )
    positions = jnp.arange(segment_tile.shape[0], dtype=jnp.int32)
    allowed = (segment_tile[:, None] == segment_tile[None, :]) & (
        positions[None, :] <= positions[:, None]
    )
    return jnp.where(allowed[None], raw_scores, MASKED)


def soft_forward(scores, value_tile):
    row_max = jnp.max(scores, axis=-1, keepdims=True)
    exponent = jnp.exp(scores - row_max)
    row_sum = jnp.sum(exponent, axis=-1, keepdims=True)
    probability = (exponent / row_sum).astype(jnp.bfloat16)
    context = jnp.einsum(
        "hqk,khd->qhd", probability, value_tile, preferred_element_type=jnp.float32
    )
    return (context.astype(jnp.bfloat16), (row_max + jnp.log(row_sum))[..., 0])


def soft_backward(scores, log_total, query_tile, key_tile, value_tile, context_grad):
    probability = jnp.exp(scores - log_total[..., None])
    prob_grad = jnp.einsum(
        "qhd,khd->hqk", context_grad, value_tile, preferred_element_type=jnp.float32
    )
    inner_sum = jnp.sum(prob_grad * probability, axis=-1, keepdims=True)
    score_grad = (probability * (prob_grad - inner_sum)).astype(jnp.bfloat16)
    query_grad = jnp.einsum(
        "hqk,khd->qhd", score_grad, key_tile, preferred_element_type=jnp.float32
    )
    key_grad = jnp.einsum(
        "hqk,qhd->khd", score_grad, query_tile, preferred_element_type=jnp.float32
    )
    value_grad = jnp.einsum(
        "hqk,qhd->khd",
        probability.astype(jnp.bfloat16),
        context_grad,
        preferred_element_type=jnp.float32,
    )
    return (query_grad, key_grad, value_grad, score_grad)


def self_attention(queries, key_rows, value_rows, segment_ids, tile_bias):
    tile_rows = tile_bias.shape[-1]
    tile_count = queries.shape[0] // tile_rows
    tile_shape = (tile_count, tile_rows, queries.shape[1] // DH, DH)

    def one_tile(inputs_now):
        query_tile, key_tile, value_tile, segment_tile = inputs_now
        return soft_forward(self_scores(query_tile, key_tile, segment_tile, tile_bias), value_tile)

    context, log_total = lax.map(
        one_tile,
        (
            queries.reshape(tile_shape),
            key_rows.reshape(tile_shape),
            value_rows.reshape(tile_shape),
            segment_ids.reshape(tile_count, tile_rows),
        ),
    )
    return (context.reshape(queries.shape), log_total)


def self_backward(queries, key_rows, value_rows, segment_ids, tile_bias, log_total, context_grad):
    tile_rows = tile_bias.shape[-1]
    tile_count = queries.shape[0] // tile_rows
    head_count = queries.shape[1] // DH
    tile_shape = (tile_count, tile_rows, head_count, DH)

    def one_tile(bias_sum, inputs_now):
        query_tile, key_tile, value_tile, segment_tile, tile_total, grad_tile = inputs_now
        scores = self_scores(query_tile, key_tile, segment_tile, tile_bias)
        query_grad, key_grad, value_grad, score_grad = soft_backward(
            scores, tile_total, query_tile, key_tile, value_tile, grad_tile
        )
        joined = jnp.concatenate(
            [
                query_grad.reshape(tile_rows, -1),
                key_grad.reshape(tile_rows, -1),
                value_grad.reshape(tile_rows, -1),
            ],
            axis=1,
        )
        return (bias_sum + score_grad.astype(jnp.float32), joined.astype(jnp.bfloat16))

    bias_sum, joined = lax.scan(
        one_tile,
        jnp.zeros((head_count, tile_rows, tile_rows), jnp.float32),
        (
            queries.reshape(tile_shape),
            key_rows.reshape(tile_shape),
            value_rows.reshape(tile_shape),
            segment_ids.reshape(tile_count, tile_rows),
            log_total,
            context_grad.reshape(tile_shape),
        ),
    )
    return (bias_sum, joined.reshape(queries.shape[0], 3 * queries.shape[1]))


def cross_attention(queries, key_rows, value_rows, tile_rows):
    tile_shape = (queries.shape[0] // tile_rows, tile_rows, key_rows.shape[1], DH)

    def one_tile(query_tile):
        scores = jnp.einsum(
            "qhd,khd->hqk", query_tile, key_rows, preferred_element_type=jnp.float32
        )
        return soft_forward(scores, value_rows)

    context, log_total = lax.map(one_tile, queries.reshape(tile_shape))
    return (context.reshape(queries.shape), log_total)


def cross_backward(queries, key_rows, value_rows, tile_rows, log_total, context_grad):
    tile_shape = (queries.shape[0] // tile_rows, tile_rows, key_rows.shape[1], DH)

    def one_tile(sums, inputs_now):
        query_tile, tile_total, grad_tile = inputs_now
        scores = jnp.einsum(
            "qhd,khd->hqk", query_tile, key_rows, preferred_element_type=jnp.float32
        )
        query_grad, key_grad, value_grad, score_grad = soft_backward(
            scores, tile_total, query_tile, key_rows, value_rows, grad_tile
        )
        return (
            (sums[0] + key_grad, sums[1] + value_grad),
            query_grad.reshape(tile_rows, -1).astype(jnp.bfloat16),
        )

    empty = jnp.zeros(key_rows.shape, jnp.float32)
    (key_sum, value_sum), query_grads = lax.scan(
        one_tile,
        (empty, empty),
        (queries.reshape(tile_shape), log_total, context_grad.reshape(tile_shape)),
    )
    return (query_grads.reshape(queries.shape), key_sum, value_sum)


def collect_weights(shards):
    gathered = jax.tree.map(
        lambda part, own: part.astype(own.dtype),
        lax.all_gather(for_sending(shards), "fsdp", axis=0, tiled=True),
        shards,
    )
    (
        norm_gains,
        self_query,
        self_key,
        self_value,
        self_out,
        cross_query,
        cross_key,
        cross_value,
        cross_out,
        ffn_in,
        ffn_out,
    ) = gathered
    ffn_in, ffn_out = (
        lax.all_gather(ffn_in, "tensor", axis=1, tiled=True),
        lax.all_gather(ffn_out, "tensor", axis=1, tiled=True),
    )
    cross_key, cross_value = (
        lax.all_gather(cross_key, "tensor", axis=1, tiled=True),
        lax.all_gather(cross_value, "tensor", axis=1, tiled=True),
    )
    return (
        norm_gains.astype(jnp.float32),
        jnp.concatenate([self_query, self_key, self_value], axis=1),
        self_out,
        cross_query,
        jnp.concatenate([cross_key, cross_value], axis=1),
        cross_out,
        ffn_in,
        ffn_out,
    )


def forward_pass(stream, encoded_rows, segment_ids, weights, tile_bias):
    gains, qkv_weight, self_out, cross_query, kv_weight, cross_out, ffn_in, ffn_out = weights
    head_width = self_out.shape[1]
    head_count = head_width // DH
    row_count = stream.shape[0]
    tile_rows = tile_bias.shape[-1]
    normed_one, scale_one = norm_rows(stream, gains[:, 0])
    gathered_one = spread_rows(normed_one)
    projected = times_plain(gathered_one, qkv_weight).astype(jnp.bfloat16)
    queries = projected[:, :head_width]
    key_rows = projected[:, head_width : 2 * head_width]
    value_rows = projected[:, 2 * head_width :]
    context, log_self = self_attention(queries, key_rows, value_rows, segment_ids, tile_bias)
    after_self = stream + combine_rows(context, self_out, row_count)
    normed_two, scale_two = norm_rows(after_self, gains[:, 1])
    gathered_two = spread_rows(normed_two)
    cross_rows = times_plain(gathered_two, cross_query).astype(jnp.bfloat16)
    own_values = times_plain(encoded_rows, kv_weight).astype(jnp.bfloat16)
    shaped = own_values.reshape(encoded_rows.shape[0], 2, lax.axis_size("tensor"), head_width)
    exchanged = lax.all_to_all(shaped, "tensor", split_axis=2, concat_axis=0, tiled=True)
    enc_keys = exchanged[:, 0, 0].reshape(-1, head_count, DH)
    enc_values = exchanged[:, 1, 0].reshape(-1, head_count, DH)
    cross_context, log_cross = cross_attention(cross_rows, enc_keys, enc_values, tile_rows)
    after_cross = after_self + combine_rows(cross_context, cross_out, row_count)
    normed_three, scale_three = norm_rows(after_cross, gains[:, 2])
    pre_values = times_plain(normed_three, ffn_in)
    activated = smooth_gate(pre_values).astype(jnp.bfloat16)
    output = after_cross + times_back(activated, ffn_out)
    saved = (
        stream,
        scale_one,
        gathered_one,
        queries,
        key_rows,
        value_rows,
        segment_ids,
        context,
        log_self,
        after_self,
        scale_two,
        gathered_two,
        cross_rows,
        encoded_rows,
        enc_keys,
        enc_values,
        cross_context,
        log_cross,
        after_cross,
        scale_three,
        normed_three,
        pre_values,
        activated,
    )
    return (output, saved)


def backward_pass(saved, incoming, weights, tile_bias):
    (
        stream,
        scale_one,
        gathered_one,
        queries,
        key_rows,
        value_rows,
        segment_ids,
        context,
        log_self,
        after_self,
        scale_two,
        gathered_two,
        cross_rows,
        encoded,
        enc_keys,
        enc_values,
        cross_context,
        log_cross,
        after_cross,
        scale_three,
        ffn_rows,
        pre_values,
        activated,
    ) = saved
    gains, qkv_weight, self_out, cross_query, kv_weight, cross_out, ffn_in, ffn_out = weights
    row_count = stream.shape[0]
    head_width = self_out.shape[1]
    branch_grad = incoming.astype(jnp.bfloat16)
    hidden_part = times_plain(branch_grad, ffn_out)
    out_weight_grad = weight_grad(branch_grad, activated)
    pre_grad = gate_back(pre_values, hidden_part).astype(jnp.bfloat16)
    in_weight_grad = weight_grad(ffn_rows, pre_grad)
    normed_three_grad = times_back(pre_grad, ffn_in)
    stream_part, gain_three = norm_back(after_cross, scale_three, gains[:, 2], normed_three_grad)
    cross_grad = incoming + stream_part
    spread_two = spread_grads(cross_grad.astype(jnp.bfloat16))
    context_two_grad = times_plain(spread_two, cross_out).astype(jnp.bfloat16)
    cross_out_grad = weight_grad(spread_two, cross_context)
    query_two_grad, key_sum, value_sum = cross_backward(
        cross_rows, enc_keys, enc_values, tile_bias.shape[-1], log_cross, context_two_grad
    )
    kv_grad = jnp.concatenate(
        [key_sum.reshape(key_sum.shape[0], -1), value_sum.reshape(value_sum.shape[0], -1)], axis=1
    ).astype(jnp.bfloat16)
    cross_query_grad = weight_grad(gathered_two, query_two_grad)
    normed_two_grad = combine_grads(query_two_grad, cross_query, row_count)
    shaped = kv_grad.reshape(kv_grad.shape[0], 2, 1, head_width)
    returned = lax.all_to_all(shaped, "tensor", split_axis=0, concat_axis=2, tiled=True)
    own_grad = returned.reshape(returned.shape[0], -1)
    kv_weight_grad = weight_grad(encoded, own_grad)
    encoded_grad = times_back(own_grad, kv_weight)
    stream_part, gain_two = norm_back(after_self, scale_two, gains[:, 1], normed_two_grad)
    self_grad = cross_grad + stream_part
    spread_one = spread_grads(self_grad.astype(jnp.bfloat16))
    context_grad = times_plain(spread_one, self_out).astype(jnp.bfloat16)
    self_out_grad = weight_grad(spread_one, context)
    bias_sum, qkv_grad = self_backward(
        queries, key_rows, value_rows, segment_ids, tile_bias, log_self, context_grad
    )
    qkv_weight_grad = weight_grad(gathered_one, qkv_grad)
    normed_one_grad = combine_grads(qkv_grad, qkv_weight, row_count)
    stream_part, gain_one = norm_back(stream, scale_one, gains[:, 0], normed_one_grad)
    input_grad = self_grad + stream_part
    gain_grads = jnp.stack([gain_one, gain_two, gain_three], axis=1)
    return (
        input_grad,
        encoded_grad,
        (
            qkv_weight_grad,
            self_out_grad,
            cross_query_grad,
            kv_weight_grad,
            cross_out_grad,
            in_weight_grad,
            out_weight_grad,
            gain_grads,
            bias_sum,
        ),
    )


def local(
    hidden,
    passages,
    block_ids,
    buckets,
    norm_gains,
    self_query,
    self_key,
    self_value,
    self_out,
    cross_query,
    cross_key,
    cross_value,
    cross_out,
    ffn_in,
    ffn_out,
    rel_bias,
    out_grad,
):
    shards = (
        norm_gains,
        self_query,
        self_key,
        self_value,
        self_out,
        cross_query,
        cross_key,
        cross_value,
        cross_out,
        ffn_in,
        ffn_out,
    )
    head_width = self_query.shape[1]
    head_count = head_width // DH
    tensor_rank = lax.axis_index("tensor")
    tile_rows = 2 * WIN
    repeat = tile_rows // WIN
    local_bias = lax.dynamic_slice_in_dim(rel_bias, tensor_rank * head_count, head_count, 1)
    one_hot = (
        buckets[None, :, :] == jnp.arange(rel_bias.shape[0], dtype=jnp.int32)[:, None, None]
    ).astype(jnp.float32)
    window_bias = jnp.einsum("bij,bh->hij", one_hot, local_bias, precision=HIGHEST)
    tile_bias = jnp.tile(window_bias, (1, repeat, repeat))
    outputs = []
    input_grads = []
    encoded_grads = []
    totals = None
    for batch_index in range(hidden.shape[0]):
        weights = collect_weights(shards)
        output, saved = forward_pass(
            hidden[batch_index].astype(jnp.float32),
            passages[batch_index],
            block_ids[batch_index],
            weights,
            tile_bias,
        )
        weights = collect_weights(shards)
        input_grad, encoded_grad, grads = backward_pass(
            saved, out_grad[batch_index].astype(jnp.float32), weights, tile_bias
        )
        totals = grads if totals is None else jax.tree.map(jnp.add, totals, grads)
        outputs.append(output.astype(jnp.bfloat16))
        input_grads.append(input_grad)
        encoded_grads.append(encoded_grad)
    (
        qkv_total,
        self_out_total,
        cross_query_total,
        kv_total,
        cross_out_total,
        in_total,
        out_total,
        gain_total,
        bias_sum,
    ) = totals
    folded = bias_sum.reshape(head_count, repeat, WIN, repeat, WIN).sum(axis=(1, 3))
    bias_grad = jnp.einsum("bij,hij->bh", one_hot, folded, precision=HIGHEST)
    bias_full = lax.dynamic_update_slice_in_dim(
        jnp.zeros(rel_bias.shape, jnp.float32), bias_grad, tensor_rank * head_count, 1
    )
    in_total, out_total = (
        lax.psum_scatter(
            in_total.astype(jnp.bfloat16), "tensor", scatter_dimension=1, tiled=True
        ).astype(jnp.float32),
        lax.psum_scatter(
            out_total.astype(jnp.bfloat16), "tensor", scatter_dimension=1, tiled=True
        ).astype(jnp.float32),
    )
    summed = (
        lax.psum_scatter(qkv_total[:, :head_width], "fsdp", scatter_dimension=0, tiled=True),
        lax.psum_scatter(
            qkv_total[:, head_width : 2 * head_width], "fsdp", scatter_dimension=0, tiled=True
        ),
        lax.psum_scatter(qkv_total[:, 2 * head_width :], "fsdp", scatter_dimension=0, tiled=True),
        lax.psum_scatter(self_out_total, "fsdp", scatter_dimension=0, tiled=True),
        lax.psum_scatter(cross_query_total, "fsdp", scatter_dimension=0, tiled=True),
        lax.psum_scatter(kv_total, "fsdp", scatter_dimension=0, tiled=True),
        lax.psum_scatter(cross_out_total, "fsdp", scatter_dimension=0, tiled=True),
        lax.psum_scatter(in_total, "fsdp", scatter_dimension=0, tiled=True),
        lax.psum_scatter(out_total, "fsdp", scatter_dimension=0, tiled=True),
    )
    kv_summed = summed[5]
    shaped = kv_summed.reshape(kv_summed.shape[0], 2, lax.axis_size("tensor"), head_width)
    reduced = lax.psum_scatter(
        shaped.astype(jnp.bfloat16), "tensor", scatter_dimension=2, tiled=True
    ).astype(jnp.float32)
    key_grad_out = reduced[:, 0, 0]
    value_grad_out = reduced[:, 1, 0]
    gains_sum, bias_total = lax.psum((gain_total, bias_full), ("fsdp", "tensor"))
    return (
        jnp.stack(outputs),
        jnp.stack(input_grads),
        jnp.stack(encoded_grads),
        gains_sum,
        summed[0],
        summed[1],
        summed[2],
        summed[3],
        summed[4],
        key_grad_out,
        value_grad_out,
        summed[6],
        summed[7],
        summed[8],
        bias_total,
    )


def solution(mesh):
    in_specs = (
        P(None, ("fsdp", "tensor"), None),
        P(None, ("fsdp", "tensor"), None),
        P(None, "fsdp"),
        P(),
        P("fsdp", None),
        P("fsdp", "tensor"),
        P("fsdp", "tensor"),
        P("fsdp", "tensor"),
        P("fsdp", "tensor"),
        P("fsdp", "tensor"),
        P("fsdp", "tensor"),
        P("fsdp", "tensor"),
        P("fsdp", "tensor"),
        P("fsdp", "tensor"),
        P("fsdp", "tensor"),
        P(),
        P(None, ("fsdp", "tensor"), None),
    )
    out_specs = (
        P(None, ("fsdp", "tensor"), None),
        P(None, ("fsdp", "tensor"), None),
        P(None, ("fsdp", "tensor"), None),
        P(),
        P("fsdp", "tensor"),
        P("fsdp", "tensor"),
        P("fsdp", "tensor"),
        P("fsdp", "tensor"),
        P("fsdp", "tensor"),
        P("fsdp", "tensor"),
        P("fsdp", "tensor"),
        P("fsdp", "tensor"),
        P("fsdp", "tensor"),
        P("fsdp", "tensor"),
        P(),
    )
    return jax.shard_map(local, mesh=mesh, in_specs=in_specs, out_specs=out_specs, check_vma=False)
```

profile of v0, /device:TPU:0, one launch (start us, length us, event | category | flops | bytes accessed | tf_op | source)
XLA Modules:
  0.0 2056.6 jit_solution(4064682617066090573)
XLA Ops:
  165.0 63.0 %reduce-scatter.31.cloned.1.call-done = f32[256,768]{1,0:T(8,128)} async-done(((f32[1024,768]{1,0:T(8,128)}), f32[256,768]{1,0:T(8,128)}) %reduce-scatter.31.cloned.1.call-update) | async-done | bytes 786448 | tf_op jit(solution)/shard_map/reduce_scatter | solution.py:71
  309.6 62.1 %all-to-all-done = bf16[640,2,4,192]{0,3,1,2:T(8,128)(2,1)} async-done(((bf16[640,2,4,192]{0,3,1,2:T(8,128)(2,1)}), bf16[640,2,4,192]{0,3,1,2:T(8,128)(2,1)}, u32[]{:S(2)}, u32[]{:S(2)}) %all-to-all-start) | async-done | bytes 1966112 | tf_op jit(solution)/shard_map/all_to_all | solution.py:291
  398.8 42.8 %all-to-all-done.1 = bf16[640,2,4,192]{0,3,1,2:T(8,128)(2,1)} async-done(((bf16[640,2,4,192]{0,3,1,2:T(8,128)(2,1)}), bf16[640,2,4,192]{0,3,1,2:T(8,128)(2,1)}, u32[]{:S(2)}, u32[]{:S(2)}) %all-to-all-start.1) | async-done | bytes 1966112 | tf_op jit(solution)/shard_map/all_to_all | solution.py:291
  447.2 45.0 %while.106 = (s32[]{:T(128)}, bf16[2,512,3,64]{1,3,2,0:T(8,128)(2,1)S(1)}, f32[2,3,512]{2,1,0:T(4,128)S(1)}, bf16[2,512,3,64]{1,3,2,0:T(8,128)(2,1)S(1)}, bf16[2...) while((s32[]{:T(128)}, bf16[2,512,3,64]{1,3,2,0:T(8,128)(2,1)S(1)}, ...), condition=%wide.region_10.11_spmd, body=%wide.region_7.10_spmd.sunk | while | flops 1030322688 | bytes 49604696 | solution.py:204
  500.2 45.6 %while.107 = (s32[]{:T(128)}, bf16[2,512,3,64]{1,3,2,0:T(8,128)(2,1)S(1)}, f32[2,3,512]{2,1,0:T(4,128)S(1)}, bf16[2,512,3,64]{1,3,2,0:T(8,128)(2,1)S(1)}, bf16[2...) while((s32[]{:T(128)}, bf16[2,512,3,64]{1,3,2,0:T(8,128)(2,1)S(1)}, ...), condition=%wide.region_23.24_spmd, body=%wide.region_20.23_spmd.sunk | while | flops 1030322688 | bytes 49604696 | solution.py:204
  561.4 60.9 %reduce-scatter.37.cloned.1.call-done = f32[256,768]{1,0:T(8,128)} async-done(((f32[1024,768]{1,0:T(8,128)}), f32[256,768]{1,0:T(8,128)}) %reduce-scatter.37.cloned.1.call-update) | async-done | bytes 786448 | tf_op jit(solution)/shard_map/reduce_scatter | solution.py:71
  623.9 89.5 %all-gather.26.cloned.1.call-done = bf16[768,3072]{1,0:T(8,128)(2,1)} async-done(((bf16[768,768]{1,0:T(8,128)(2,1)}), bf16[768,3072]{1,0:T(8,128)(2,1)}) %all-gather.26.cloned.1.call-update) | async-done | bytes 4718608 | tf_op jit(solution)/shard_map/all_gather | solution.py:253
  722.3 80.4 %all-gather.30.cloned.1.call-done = bf16[768,3072]{1,0:T(8,128)(2,1)} async-done(((bf16[768,768]{1,0:T(8,128)(2,1)}), bf16[768,3072]{1,0:T(8,128)(2,1)}) %all-gather.30.cloned.1.call-update) | async-done | bytes 4718608 | tf_op jit(solution)/shard_map/all_gather | solution.py:254
  896.6 79.8 %while.112 = (s32[]{:T(128)}, f32[2560,3,64]{0,2,1:T(8,128)}, f32[2560,3,64]{0,2,1:T(8,128)}, bf16[2,512,192]{1,2,0:T(8,128)(2,1)S(1)}, bf16[2,512,3,64]{1,3,2,0...) while((s32[]{:T(128)}, f32[2560,3,64]{0,2,1:T(8,128)}, ...), condition=%wide.region_40.41_spmd.clone, body=%wide.region_38.40_spmd.clone.sunk | while | flops 2554034688 | bytes 256030928 | solution.py:225
  981.8 79.3 %while.110 = (s32[]{:T(128)}, f32[2560,3,64]{0,2,1:T(8,128)S(1)}, f32[2560,3,64]{0,2,1:T(8,128)}, bf16[2,512,192]{1,2,0:T(8,128)(2,1)}, bf16[2,512,3,64]{1,3,2,0...) while((s32[]{:T(128)}, f32[2560,3,64]{0,2,1:T(8,128)S(1)}, ...), condition=%wide.region_29.30_spmd.clone, body=%wide.region_27.29_spmd.clone.sunk | while | flops 2554034688 | bytes 266254704 | solution.py:225
  1084.2 96.6 %all-to-all-done.2 = bf16[2560,2,1,192]{3,1,2,0:T(2,128)(2,1)} async-done(((bf16[2560,2,1,192]{3,1,2,0:T(2,128)(2,1)}), bf16[2560,2,1,192]{3,1,2,0:T(2,128)(2,1)}, u32[]{:S(2)}, u32[]{:S(2)}) %all-to-all-start.2) | async-done | bytes 1966112 | tf_op jit(solution)/shard_map/all_to_all | solution.py:377
  1200.3 70.2 %all-to-all-done.3 = bf16[2560,2,1,192]{3,1,2,0:T(2,128)(2,1)} async-done(((bf16[2560,2,1,192]{3,1,2,0:T(2,128)(2,1)}), bf16[2560,2,1,192]{3,1,2,0:T(2,128)(2,1)}, u32[]{:S(2)}, u32[]{:S(2)}) %all-to-all-start.3) | async-done | bytes 1966112 | tf_op jit(solution)/shard_map/all_to_all | solution.py:377
  1316.1 41.9 %while.113 = (s32[]{:T(128)}, f32[3,512,512]{1,2,0:T(8,128)}, bf16[2,512,576]{1,2,0:T(8,128)(2,1)}, s32[2,512]{1,0:T(2,128)S(1)}, bf16[2,512,3,64]{1,3,2,0:T(8,1...) while((s32[]{:T(128)}, f32[3,512,512]{1,2,0:T(8,128)}, ...), condition=%wide.region_45.46_spmd.clone, body=%wide.region_43.45_spmd.clone.sunk | while | flops 515602944 | bytes 62693692 | solution.py:180
  1389.2 41.6 %while.111 = (s32[]{:T(128)}, f32[3,512,512]{1,2,0:T(8,128)}, bf16[2,512,576]{1,2,0:T(8,128)(2,1)}, s32[2,512]{1,0:T(2,128)S(1)}, bf16[2,512,3,64]{1,3,2,0:T(8,1...) while((s32[]{:T(128)}, f32[3,512,512]{1,2,0:T(8,128)}, ...), condition=%wide.region_34.35_spmd.clone, body=%wide.region_32.34_spmd.clone.sunk | while | flops 515602944 | bytes 62693692 | solution.py:180
  1480.3 79.4 %reduce-scatter.57.cloned.1.call-done = bf16[768,768]{0,1:T(8,128)(2,1)} async-done(((bf16[768,3072]{0,1:T(8,128)(2,1)}), bf16[768,768]{0,1:T(8,128)(2,1)}) %reduce-scatter.57.cloned.1.call-update) | async-done | bytes 1179664 | tf_op jit(solution)/shard_map/reduce_scatter | solution.py:495
  1601.8 59.9 %reduce-scatter.45.cloned.1.call-done = f32[256,768]{1,0:T(8,128)} async-done(((f32[1024,768]{1,0:T(8,128)}), f32[256,768]{1,0:T(8,128)}) %reduce-scatter.45.cloned.1.call-update) | async-done | bytes 786448 | tf_op jit(solution)/shard_map/reduce_scatter | solution.py:84
  1661.8 62.5 %reduce-scatter.41.cloned.1.call-done = f32[256,768]{1,0:T(8,128)} async-done(((f32[1024,768]{1,0:T(8,128)}), f32[256,768]{1,0:T(8,128)}) %reduce-scatter.41.cloned.1.call-update) | async-done | bytes 786448 | tf_op jit(solution)/shard_map/reduce_scatter | solution.py:84
  1726.3 40.8 %all-reduce.1 = (f32[768,3]{0,1:T(4,128)}, f32[32,12]{0,1:T(8,128)}) all-reduce(f32[768,3]{0,1:T(4,128)S(1)} %maximum_add_fusion, f32[32,12]{0,1:T(8,128)S(1)} %dynamic_update_slice.43), channel_id=1, replica_groups=mesh['fsdp'=8,'tensor'=4] {'fsdp','tensor'}, use_global_device_ids=true, to_apply=%region_54.55 | all-reduce | flops 2688 | bytes 21504 | tf_op jit(solution)/shard_map/psum | solution.py:519
  1801.6 38.8 %reduce-scatter.47.cloned.1.call-done = f32[96,192]{1,0:T(8,128)} async-done(((f32[768,192]{1,0:T(8,128)}), f32[96,192]{1,0:T(8,128)}) %reduce-scatter.47.cloned.1.call-update) | async-done | bytes 73744 | tf_op jit(solution)/shard_map/reduce_scatter | solution.py:505
  1840.4 38.6 %reduce-scatter.59.cloned.1.call-done = f32[96,192]{1,0:T(8,128)} async-done(((f32[768,192]{1,0:T(8,128)}), f32[96,192]{1,0:T(8,128)}) %reduce-scatter.59.cloned.1.call-update) | async-done | bytes 73744
  1878.9 38.8 %reduce-scatter.61.cloned.1.call-done = f32[96,192]{1,0:T(8,128)} async-done(((f32[768,192]{1,0:T(8,128)}), f32[96,192]{1,0:T(8,128)}) %reduce-scatter.61.cloned.1.call-update) | async-done | bytes 73744
  1917.7 38.8 %reduce-scatter.63.cloned.1.call-done = f32[96,192]{1,0:T(8,128)} async-done(((f32[768,192]{1,0:T(8,128)}), f32[96,192]{1,0:T(8,128)}) %reduce-scatter.63.cloned.1.call-update) | async-done | bytes 73744
  1956.5 46.3 %reduce-scatter.55.cloned.1.call-done = f32[96,768]{1,0:T(8,128)} async-done(((f32[768,768]{1,0:T(8,128)}), f32[96,768]{1,0:T(8,128)}) %reduce-scatter.55.cloned.1.call-update) | async-done | bytes 294928 | tf_op jit(solution)/shard_map/reduce_scatter | solution.py:509
  2002.8 46.8 %reduce-scatter.67.cloned.1.call-done = f32[96,768]{1,0:T(8,128)} async-done(((f32[768,768]{1,0:T(8,128)}), f32[96,768]{1,0:T(8,128)}) %reduce-scatter.67.cloned.1.call-update) | async-done | bytes 294928
  (778 shorter events, 1035.4 us)
Async XLA Ops:
  163.8 281.0 %all-gather.18.cloned.1.call-start = ((), (), s32[]{:S(2)}) async-start(), calls=%async_computation.25 | async-start | bytes 1966080 | tf_op jit(solution)/shard_map/all_gather | solution.py:59
  303.4 190.4 %all-gather.34.cloned.1.call-start = ((), (), s32[]{:S(2)}) async-start(), calls=%async_computation.35 | async-start | bytes 1966080 | tf_op jit(solution)/shard_map/all_gather | solution.py:59
  304.2 245.3 %all-gather.24.cloned.1.call-start = ((), (), s32[]{:S(2)}) async-start(), calls=%async_computation.29 | async-start | bytes 1327104 | tf_op jit(solution)/shard_map/all_gather | solution.py:236
  376.2 174.0 %all-gather.28.cloned.1.call-start = ((), (), s32[]{:S(2)}) async-start(), calls=%async_computation.31 | async-start | bytes 1327104 | tf_op jit(solution)/shard_map/all_gather | solution.py:236
  376.8 182.5 %reduce-scatter.33.cloned.1.call-start = ((), (), s32[]{:S(2)}) async-start(), calls=%async_computation.28 | async-start | bytes 3932160 | tf_op jit(solution)/shard_map/reduce_scatter | solution.py:71
  549.3 164.0 %all-gather.26.cloned.1.call-start = ((), (), s32[]{:S(2)}) async-start(), calls=%async_computation.30 | async-start | bytes 5898240 | tf_op jit(solution)/shard_map/all_gather | solution.py:253
  550.1 252.5 %all-gather.30.cloned.1.call-start = ((), (), s32[]{:S(2)}) async-start(), calls=%async_computation.32 | async-start | bytes 5898240 | tf_op jit(solution)/shard_map/all_gather | solution.py:254
  550.7 304.3 %all-gather.36.cloned.1.call-start = ((), (), s32[]{:S(2)}) async-start(), calls=%async_computation.37 | async-start | bytes 1966080 | tf_op jit(solution)/shard_map/all_gather | solution.py:63
  819.9 365.6 %reduce-scatter.43.cloned.1.call-start = ((), (), s32[]{:S(2)}) async-start(), calls=%async_computation.42 | async-start | bytes 3932160 | tf_op jit(solution)/shard_map/reduce_scatter | solution.py:84
  980.7 204.8 %reduce-scatter.39.cloned.1.call-start = ((), (), s32[]{:S(2)}) async-start(), calls=%async_computation.38 | async-start | bytes 3932160 | tf_op jit(solution)/shard_map/reduce_scatter | solution.py:84
  1190.2 169.3 %reduce-scatter.65.cloned.1.call-start = ((), (), s32[]{:S(2)}) async-start(), calls=%async_computation.54 | async-start | bytes 5308416
  1293.8 177.6 %reduce-scatter.53.cloned.1.call-start = ((), (), s32[]{:S(2)}) async-start(), calls=%async_computation.48 | async-start | bytes 5898240 | tf_op jit(solution)/shard_map/reduce_scatter | solution.py:492
  1301.2 258.5 %reduce-scatter.57.cloned.1.call-start = ((), (), s32[]{:S(2)}) async-start(), calls=%async_computation.50 | async-start | bytes 5898240 | tf_op jit(solution)/shard_map/reduce_scatter | solution.py:495
  1310.8 288.7 %all-reduce.4.cloned.1.call-start = ((), (), s32[]{:S(2)}) async-start(), calls=%async_computation.56 | async-start | bytes 786432
  1362.2 299.5 %reduce-scatter.45.cloned.1.call-start = ((), (), s32[]{:S(2)}) async-start(), calls=%async_computation.44 | async-start | bytes 3932160 | tf_op jit(solution)/shard_map/reduce_scatter | solution.py:84
  1365.7 358.5 %reduce-scatter.41.cloned.1.call-start = ((), (), s32[]{:S(2)}) async-start(), calls=%async_computation.40 | async-start | bytes 3932160 | tf_op jit(solution)/shard_map/reduce_scatter | solution.py:84
  1437.8 332.4 %reduce-scatter.51.cloned.1.call-start = ((), (), s32[]{:S(2)}) async-start(), calls=%async_computation.47 | async-start | bytes 884736 | tf_op jit(solution)/shard_map/reduce_scatter | solution.py:508
  1441.2 360.4 %reduce-scatter.49.cloned.1.call-start = ((), (), s32[]{:S(2)}) async-start(), calls=%async_computation.46 | async-start | bytes 884736 | tf_op jit(solution)/shard_map/reduce_scatter | solution.py:506
  1446.0 394.4 %reduce-scatter.47.cloned.1.call-start = ((), (), s32[]{:S(2)}) async-start(), calls=%async_computation.45 | async-start | bytes 884736 | tf_op jit(solution)/shard_map/reduce_scatter | solution.py:505
  1449.7 429.2 %reduce-scatter.59.cloned.1.call-start = ((), (), s32[]{:S(2)}) async-start(), calls=%async_computation.51 | async-start | bytes 884736
  1455.7 462.0 %reduce-scatter.61.cloned.1.call-start = ((), (), s32[]{:S(2)}) async-start(), calls=%async_computation.52 | async-start | bytes 884736
  1456.9 499.5 %reduce-scatter.63.cloned.1.call-start = ((), (), s32[]{:S(2)}) async-start(), calls=%async_computation.53 | async-start | bytes 884736
  1458.2 544.6 %reduce-scatter.55.cloned.1.call-start = ((), (), s32[]{:S(2)}) async-start(), calls=%async_computation.49 | async-start | bytes 2654208 | tf_op jit(solution)/shard_map/reduce_scatter | solution.py:509
  1474.3 575.3 %reduce-scatter.67.cloned.1.call-start = ((), (), s32[]{:S(2)}) async-start(), calls=%async_computation.55 | async-start | bytes 2654208
  (197 other events, 6549.3 us)
Sparse Core Ops, SparseCore 0:
  22.8 37.2 all-gather.31
  62.3 35.9 all-gather.15
  104.4 60.5 reduce-scatter.34
  167.7 60.2 reduce-scatter.30
  293.7 68.8 all-gather.17
  364.1 55.8 all-gather.33
  499.9 59.2 reduce-scatter.32
  562.0 60.2 reduce-scatter.36
  623.9 89.4 all-gather.25
  714.8 87.8 all-gather.29
  819.4 35.5 all-gather.35
  856.4 35.9 all-gather.39
  980.8 59.1 reduce-scatter.42
  1066.3 100.0 reduce-scatter.38
  1190.3 64.5 all-gather.41
  1293.1 52.9 reduce-scatter.64
  1347.8 37.0 all-gather.37
  1387.3 84.1 reduce-scatter.52
  1473.8 85.7 reduce-scatter.56
  1562.0 37.5 all-reduce.3
  1601.9 59.8 reduce-scatter.44
  1663.9 60.2 reduce-scatter.40
  1960.2 42.5 reduce-scatter.54
  2007.1 42.4 reduce-scatter.66
  (10 shorter events, 315.7 us)
where the time goes:
time: 2070 us; the launch traced here: 2060 us
  waiting for transfers between devices  1230 us (59%)
  matrix products  340 us (16%)
  local copies, waits for them, and re-layouts  180 us (9%)
  other arithmetic  145 us (7%)
  blocking collectives  127 us (6%)
  starting transfers between devices  22.5 us (1%)
    unnamed x40, waiting for transfers between devices  174 us
    all_to_all x2, waiting for transfers between devices, backward_pass(): lax.all_to_all(shaped, 'tensor', split_axis=0, concat_axis=2, tiled=True)  167 us
    reduce_scatter x4, waiting for transfers between devices, combine_rows(): lax.psum_scatter(row_term(jnp.int32(0), row_count * lax.axis_size('tensor...  133 us
    reduce_scatter x4, waiting for transfers between devices, combine_grads(): lax.psum_scatter(row_term(jnp.int32(0), row_count * lax.axis_size('tensor...  122 us
    all_to_all x2, waiting for transfers between devices, forward_pass(): lax.all_to_all(shaped, 'tensor', split_axis=2, concat_axis=0, tiled=True)  105 us
    all_gather x1, waiting for transfers between devices, collect_weights(): lax.all_gather(ffn_in, 'tensor', axis=1, tiled=True)  89.5 us
    all_gather x9, blocking collectives, collect_weights(): lax.all_gather(for_sending(shards), 'fsdp', axis=0, tiled=True)  86.5 us
    all_gather x4, waiting for transfers between devices, spread_grads(): return lax.all_gather(branch_grad, 'tensor', axis=0, tiled=True)  86.2 us
  transfers between devices with their start and end apart: 38, of which 27 were waited for; matrix products, arithmetic and copies ran while one was open for 26% of the time, Pallas kernels for 0%

commit v1 on v0

v1 whole, which is shorter than its diff:
```python
import functools

import jax
import jax.numpy as jnp
from jax import lax
from jax.experimental import pallas as pl
from jax.experimental.pallas import tpu as pltpu
from jax.sharding import PartitionSpec as P

DH = 64
WIN = 256
EPSILON = 1e-06
MASKED = -1000000000.0
BF = jnp.bfloat16
F32 = jnp.float32
MIB = 1024 * 1024


def nn(left, right):
    return jnp.dot(left, right, preferred_element_type=F32)


def nt(left, right):
    return lax.dot_general(left, right, (((1,), (1,)), ((), ())), preferred_element_type=F32)


def tn(left, right):
    return lax.dot_general(left, right, (((0,), (0,)), ((), ())), preferred_element_type=F32)


def shift(x, axis, by):
    size = lax.axis_size(axis)
    if by % size == 0:
        return x
    return lax.ppermute(x, axis, [(i, (i + by) % size) for i in range(size)])


def flip(x, axis, bits):
    size = lax.axis_size(axis)
    return lax.ppermute(x, axis, [(i, i ^ bits) for i in range(size)])


def two_way(x, swapped):
    first, second = (4, 2) if swapped else (2, 4)
    return lax.ppermute(x, "fsdp", [(i, i ^ (second if i & 1 else first)) for i in range(8)])


def assemble_kernel(*refs):
    pieces, out_ref = refs[:8], refs[8]
    me = lax.axis_index("fsdp")
    odd = lax.rem(me, 2)
    x_bit, y_bit = lax.rem(me // 2, 2), me // 4

    def flipped(dx, dy, dc):
        new_x = x_bit + dx - 2 * x_bit * dx
        new_y = y_bit + dy - 2 * y_bit * dy
        new_c = odd + dc - 2 * odd * dc
        return new_y * 4 + new_x * 2 + new_c

    even = 1 - odd
    places = [
        flipped(0, 0, 0),
        flipped(even, odd, 0),
        flipped(odd, even, 0),
        flipped(1, 1, 0),
        flipped(0, 0, 1),
        flipped(odd, even, 1),
        flipped(even, odd, 1),
        flipped(1, 1, 1),
    ]
    rows = pieces[0].shape[0]
    for place, piece in zip(places, pieces):
        out_ref[pl.ds(pl.multiple_of(place * rows, rows), rows), :] = piece[...]


def gather_fsdp(piece, widths):
    size = lax.axis_size("fsdp")
    if size != 8 or piece.shape[0] % 16:
        whole = lax.all_gather(piece, "fsdp", axis=0, tiled=True)
        parts, first = [], 0
        for width in widths:
            parts.append(whole[:, first : first + width])
            first += width
        return parts
    one = two_way(piece, False)
    two = two_way(piece, True)
    three = two_way(one, True)
    pieces = [piece, one, two, three]
    pieces = pieces + [flip(p, "fsdp", 1) for p in pieces]
    rows = piece.shape[0]
    parts, first = [], 0
    for width in widths:
        block = 768 if width % 768 == 0 else width
        parts.append(
            pl.pallas_call(
                assemble_kernel,
                grid=(width // block,),
                out_shape=jax.ShapeDtypeStruct((size * rows, width), piece.dtype),
                in_specs=[
                    pl.BlockSpec((rows, block), lambda i, k=first // block: (0, k + i))
                ]
                * 8,
                out_specs=pl.BlockSpec((size * rows, block), lambda i: (0, i)),
                cost_estimate=pl.CostEstimate(
                    flops=0, bytes_accessed=32 * rows * width, transcendentals=0
                ),
            )(*pieces)
        )
        first += width
    return parts


def gather_weights(shards, widths, grouped):
    ranks = lax.axis_size("tensor")
    joined = jnp.concatenate(shards, axis=1)
    blocks = [shift(joined, "tensor", s) for s in range(ranks)]
    if grouped:
        piece = jnp.concatenate(blocks, axis=1)
    else:
        parts, first = [], 0
        for shard in shards:
            parts += [b[:, first : first + shard.shape[1]] for b in blocks]
            first += shard.shape[1]
        piece = jnp.concatenate(parts, axis=1)
    return gather_fsdp(piece, widths)


def gather_small(shard):
    size = lax.axis_size("fsdp")
    held = shard[None]
    bit = 1
    while bit < size:
        held = jnp.concatenate([held, flip(held, "fsdp", bit)], axis=0)
        bit *= 2
    order = jnp.bitwise_xor(jnp.arange(size, dtype=jnp.int32), lax.axis_index("fsdp"))
    return jnp.take(held, order, axis=0)


def sum_everywhere(x):
    for axis in ("fsdp", "tensor"):
        bit = 1
        while bit < lax.axis_size(axis):
            x = x + flip(x, axis, bit)
            bit *= 2
    return x


def pick(x, index):
    return lax.dynamic_index_in_dim(x, index, 0, keepdims=False)


def scatter_fsdp(grad):
    size = lax.axis_size("fsdp")
    if size != 8:
        return lax.psum_scatter(grad.astype(F32), "fsdp", scatter_dimension=0, tiled=True)
    me = lax.axis_index("fsdp")
    odd, chip = lax.rem(me, 2), me // 2
    near = 1 + odd
    blocks = grad.reshape(4, 2, grad.shape[0] // 8, grad.shape[1])
    sent = lax.dynamic_index_in_dim(blocks, 1 - odd, 1, keepdims=False)
    kept = lax.dynamic_index_in_dim(blocks, odd, 1, keepdims=False)
    pair = kept.astype(F32) + flip(sent, "fsdp", 1).astype(F32)
    pair = pair.astype(BF)
    near_chip = jnp.bitwise_xor(chip, near)
    far_chip = jnp.bitwise_xor(chip, 3 - near)
    to_far = two_way(pick(pair, jnp.bitwise_xor(chip, 3)), False)
    to_near = two_way(pick(pair, near_chip), False)
    far_sum = (pick(pair, far_chip).astype(F32) + to_far.astype(F32)).astype(BF)
    far_sum = two_way(far_sum, True)
    return pick(pair, chip).astype(F32) + to_near.astype(F32) + far_sum.astype(F32)


def scatter_tensor(blocks):
    total = blocks[0]
    for s in range(1, len(blocks)):
        total = total + shift(blocks[s].astype(BF), "tensor", -s).astype(F32)
    return total


def column_blocks(x, count):
    width = x.shape[1] // count
    return [x[:, s * width : (s + 1) * width] for s in range(count)]


def to_heads(blocks):
    return jnp.concatenate([shift(b, "tensor", -s) for s, b in enumerate(blocks)], axis=0)


def from_heads(rows):
    ranks = lax.axis_size("tensor")
    count = rows.shape[0] // ranks
    return jnp.concatenate(
        [shift(rows[s * count : (s + 1) * count], "tensor", s) for s in range(ranks)], axis=1
    )


def bias_kernel(heads, table_ref, bucket_ref, out_ref):
    group = pl.program_id(0)
    count = out_ref.shape[0]
    buckets = table_ref.shape[0]

    def some_rows(i, carry):
        rows = pl.ds(i * 32, 32)
        bucket = bucket_ref[rows, :]
        found = [jnp.zeros(bucket.shape, F32) for _ in range(count)]
        for b in range(buckets):
            here = bucket == b
            for h in range(count):
                found[h] = jnp.where(here, table_ref[b, group * count + h], found[h])
        for h in range(count):
            out_ref[h, rows, :] = found[h]
        return carry

    lax.fori_loop(0, bucket_ref.shape[0] // 32, some_rows, 0)


def window_bias(table, buckets):
    heads = table.shape[1]
    count = 4
    return pl.pallas_call(
        functools.partial(bias_kernel, heads),
        grid=(heads // count,),
        in_specs=[
            pl.BlockSpec(memory_space=pltpu.SMEM),
            pl.BlockSpec((WIN, WIN), lambda g: (0, 0)),
        ],
        out_specs=pl.BlockSpec((count, WIN, WIN), lambda g: (g, 0, 0)),
        out_shape=jax.ShapeDtypeStruct((heads, WIN, WIN), F32),
        cost_estimate=pl.CostEstimate(
            flops=40 * heads * WIN * WIN, bytes_accessed=4 * heads * WIN * WIN, transcendentals=0
        ),
    )(table, buckets)


def allowed_pairs(col_ref, row_ref):
    rows = lax.broadcasted_iota(jnp.int32, (WIN, WIN), 0)
    cols = lax.broadcasted_iota(jnp.int32, (WIN, WIN), 1)
    return (col_ref[0] == row_ref[0]) & (cols <= rows)


def self_softmax(q, k, bias, allowed):
    scores = jnp.where(allowed, nt(q, k) + bias, MASKED)
    raised = jnp.exp(scores - jnp.max(scores, axis=1, keepdims=True))
    return raised / jnp.sum(raised, axis=1, keepdims=True)


def self_forward_kernel(q_ref, k_ref, v_ref, col_ref, row_ref, bias_ref, out_ref):
    allowed = allowed_pairs(col_ref, row_ref)
    for h in range(2):
        lanes = slice(h * DH, (h + 1) * DH)
        prob = self_softmax(q_ref[:, lanes], k_ref[:, lanes], bias_ref[h], allowed)
        out_ref[:, lanes] = nn(prob.astype(BF), v_ref[:, lanes]).astype(BF)


def self_forward(qkv, ids, bias):
    rows, width = qkv.shape[0], qkv.shape[1] // 3
    pairs, windows = width // 128, rows // WIN

    def part(k):
        return pl.BlockSpec((WIN, 128), lambda g, w, k=k: (w, k * pairs + g))

    return pl.pallas_call(
        self_forward_kernel,
        grid=(pairs, windows),
        in_specs=[
            part(0),
            part(1),
            part(2),
            pl.BlockSpec((1, WIN, 1), lambda g, w: (w, 0, 0)),
            pl.BlockSpec((1, 1, WIN), lambda g, w: (w, 0, 0)),
            pl.BlockSpec((2, WIN, WIN), lambda g, w: (g, 0, 0)),
        ],
        out_specs=pl.BlockSpec((WIN, 128), lambda g, w: (w, g)),
        out_shape=jax.ShapeDtypeStruct((rows, width), BF),
        cost_estimate=pl.CostEstimate(
            flops=16 * rows * WIN * width, bytes_accessed=16 * rows * width, transcendentals=0
        ),
    )(qkv, qkv, qkv, ids.reshape(windows, WIN, 1), ids.reshape(windows, 1, WIN), bias)


def self_backward_kernel(
    q_ref, k_ref, v_ref, g_ref, col_ref, row_ref, bias_ref, bucket_ref,
    gq_ref, gk_ref, gv_ref, gb_ref, sum_ref,
):
    window, windows = pl.program_id(1), pl.num_programs(1)
    allowed = allowed_pairs(col_ref, row_ref)

    @pl.when(window == 0)
    def _():
        sum_ref[...] = jnp.zeros_like(sum_ref)

    for h in range(2):
        lanes = slice(h * DH, (h + 1) * DH)
        q, k, v, g = q_ref[:, lanes], k_ref[:, lanes], v_ref[:, lanes], g_ref[:, lanes]
        prob = self_softmax(q, k, bias_ref[h], allowed)
        prob_grad = nt(g, v)
        inner = jnp.sum(prob_grad * prob, axis=1, keepdims=True)
        score_grad = (prob * (prob_grad - inner)).astype(BF)
        gq_ref[:, lanes] = nn(score_grad, k).astype(BF)
        gk_ref[:, lanes] = tn(score_grad, q).astype(BF)
        gv_ref[:, lanes] = tn(prob.astype(BF), g).astype(BF)
        sum_ref[h] += score_grad.astype(F32)

    @pl.when(window == windows - 1)
    def _():
        def one_bucket(b, carry):
            here = bucket_ref[...] == b
            for h in range(2):
                gb_ref[h, pl.ds(b, 1), :] = jnp.sum(
                    jnp.where(here, sum_ref[h], 0.0), axis=0, keepdims=True
                )
            return carry

        lax.fori_loop(0, gb_ref.shape[1], one_bucket, 0)


def self_backward(qkv, grad, ids, bias, buckets, bucket_count):
    rows, width = qkv.shape[0], qkv.shape[1] // 3
    pairs, windows = width // 128, rows // WIN

    def part(k):
        return pl.BlockSpec((WIN, 128), lambda g, w, k=k: (w, k * pairs + g))

    return pl.pallas_call(
        self_backward_kernel,
        grid=(pairs, windows),
        in_specs=[
            part(0),
            part(1),
            part(2),
            part(0),
            pl.BlockSpec((1, WIN, 1), lambda g, w: (w, 0, 0)),
            pl.BlockSpec((1, 1, WIN), lambda g, w: (w, 0, 0)),
            pl.BlockSpec((2, WIN, WIN), lambda g, w: (g, 0, 0)),
            pl.BlockSpec((WIN, WIN), lambda g, w: (0, 0)),
        ],
        out_specs=[part(0)] * 3 + [pl.BlockSpec((2, bucket_count, WIN), lambda g, w: (g, 0, 0))],
        out_shape=[jax.ShapeDtypeStruct((rows, width), BF)] * 3
        + [jax.ShapeDtypeStruct((2 * pairs, bucket_count, WIN), F32)],
        scratch_shapes=[pltpu.VMEM((2, WIN, WIN), F32)],
        cost_estimate=pl.CostEstimate(
            flops=60 * rows * WIN * width, bytes_accessed=24 * rows * width, transcendentals=0
        ),
    )(qkv, qkv, qkv, grad, ids.reshape(windows, WIN, 1), ids.reshape(windows, 1, WIN), bias, buckets)


def cross_forward_kernel(q_ref, kv_ref, out_ref, exact_ref, total_ref, ones_ref):
    heads = q_ref.shape[1] // DH
    width = heads * DH

    @pl.when(pl.program_id(0) == 0)
    def _():
        for h in range(heads):
            values = kv_ref[:, width + h * DH : width + (h + 1) * DH]
            ones_ref[h] = jnp.concatenate([values, jnp.ones_like(values)], axis=1)

    for h in range(heads):
        lanes = slice(h * DH, (h + 1) * DH)
        scores = nt(q_ref[:, lanes], kv_ref[:, lanes])
        top = jnp.max(scores, axis=1, keepdims=True)
        raised = jnp.exp(scores - top).astype(BF)
        both = nn(raised, ones_ref[h])
        row_sum = both[:, DH:]
        context = both[:, :DH] / row_sum
        out_ref[:, lanes] = context.astype(BF)
        exact_ref[:, lanes] = context
        log_total = top + jnp.log(jnp.concatenate([row_sum, row_sum], axis=1))
        total_ref[h : h + 1, :] = jnp.transpose(log_total)[:1]


def cross_forward(queries, keys_values):
    rows, width = queries.shape
    keys = keys_values.shape[0]
    tile = WIN
    return pl.pallas_call(
        cross_forward_kernel,
        grid=(rows // tile,),
        in_specs=[
            pl.BlockSpec((tile, width), lambda i: (i, 0)),
            pl.BlockSpec((keys, 2 * width), lambda i: (0, 0)),
        ],
        out_specs=[
            pl.BlockSpec((tile, width), lambda i: (i, 0)),
            pl.BlockSpec((tile, width), lambda i: (i, 0)),
            pl.BlockSpec((8, tile), lambda i: (0, i)),
        ],
        out_shape=[
            jax.ShapeDtypeStruct((rows, width), BF),
            jax.ShapeDtypeStruct((rows, width), F32),
            jax.ShapeDtypeStruct((8, rows), F32),
        ],
        scratch_shapes=[pltpu.VMEM((width // DH, keys, 2 * DH), BF)],
        compiler_params=pltpu.CompilerParams(vmem_limit_bytes=48 * MIB),
        cost_estimate=pl.CostEstimate(
            flops=16 * rows * keys * width, bytes_accessed=4 * keys * width, transcendentals=0
        ),
    )(queries, keys_values)


def cross_backward_kernel(
    q_ref, g_ref, exact_ref, total_ref, kv_ref, gq_ref, gkv_ref, inner_ref, sum_ref
):
    step, steps = pl.program_id(0), pl.num_programs(0)
    heads = q_ref.shape[1] // DH
    width = heads * DH
    rows = q_ref.shape[0]

    @pl.when(step == 0)
    def _():
        sum_ref[...] = jnp.zeros_like(sum_ref)
        for h in range(heads):
            lanes = slice(h * DH, (h + 1) * DH)
            for first in range(0, rows, WIN):
                tile = slice(first, first + WIN)
                product = g_ref[tile, lanes].astype(F32) * exact_ref[tile, lanes]
                inner_ref[h : h + 1, tile] = jnp.sum(jnp.transpose(product), axis=0, keepdims=True)

    for h in range(heads):
        lanes = slice(h * DH, (h + 1) * DH)
        value_lanes = slice(width + h * DH, width + (h + 1) * DH)
        k, v = kv_ref[:, lanes], kv_ref[:, value_lanes]
        k_across = jnp.transpose(k)
        key_grad = jnp.zeros(k.shape, F32)
        value_grad = jnp.zeros(k.shape, F32)
        for first in range(0, rows, WIN):
            tile = slice(first, first + WIN)
            q, g = q_ref[tile, lanes], g_ref[tile, lanes]
            prob = jnp.exp(nt(k, q) - total_ref[h : h + 1, tile])
            prob_grad = nt(v, g)
            score_grad = (prob * (prob_grad - inner_ref[h : h + 1, tile])).astype(BF)
            value_grad += nn(prob.astype(BF), g)
            key_grad += nn(score_grad, q)
            sum_ref[lanes, tile] += nn(k_across, score_grad)
        gkv_ref[:, lanes] = key_grad.astype(BF)
        gkv_ref[:, value_lanes] = value_grad.astype(BF)

    @pl.when(step == steps - 1)
    def _():
        for first in range(0, rows, WIN):
            tile = slice(first, first + WIN)
            gq_ref[tile, :] = jnp.transpose(sum_ref[:, tile]).astype(BF)


def cross_backward(queries, grad, exact, total, keys_values):
    rows, width = queries.shape
    keys = keys_values.shape[0]
    tile = WIN
    whole = pl.BlockSpec((rows, width), lambda i: (0, 0))
    block = pl.BlockSpec((tile, 2 * width), lambda i: (i, 0))
    return pl.pallas_call(
        cross_backward_kernel,
        grid=(keys // tile,),
        in_specs=[whole, whole, whole, pl.BlockSpec((8, rows), lambda i: (0, 0)), block],
        out_specs=[whole, block],
        out_shape=[
            jax.ShapeDtypeStruct((rows, width), BF),
            jax.ShapeDtypeStruct((keys, 2 * width), BF),
        ],
        scratch_shapes=[pltpu.VMEM((8, rows), F32), pltpu.VMEM((width, rows), F32)],
        compiler_params=pltpu.CompilerParams(vmem_limit_bytes=48 * MIB),
        cost_estimate=pl.CostEstimate(
            flops=40 * rows * keys * width, bytes_accessed=8 * keys * width, transcendentals=0
        ),
    )(queries, grad, exact, total, keys_values)


def norm_scale(stream):
    return lax.rsqrt(jnp.mean(stream * stream, axis=-1, keepdims=True) + EPSILON)


def norm_back(stream, scale, gain, incoming):
    scaled = incoming * gain
    along = jnp.mean(scaled * stream, axis=-1, keepdims=True)
    return (
        scale * scaled - stream * (scale * scale * scale) * along,
        jnp.sum(incoming * stream * scale, axis=0, keepdims=True),
    )


def gate_and_slope(u):
    inner = 0.7978845608028654 * (u + 0.044715 * u * u * u)
    bent = jnp.tanh(inner)
    half = 0.5 * (1.0 + bent)
    slope = half + 0.5 * u * (1.0 - bent * bent) * 0.7978845608028654 * (1.0 + 0.134145 * u * u)
    return u * half, slope


def local(
    hidden, passages, block_ids, buckets, norm_gains, self_query, self_key, self_value, self_out,
    cross_query, cross_key, cross_value, cross_out, ffn_in, ffn_out, rel_bias, out_grad,
):
    ranks = lax.axis_size("tensor")
    rank = lax.axis_index("tensor")
    batches, rows, model = hidden.shape
    enc_rows = passages.shape[1]
    head_width = self_query.shape[1]
    head_count = head_width // DH
    width = head_width * ranks

    (kv_weight,) = gather_weights([cross_key, cross_value], [2 * width], True)
    qkv_weight, so_weight = gather_weights(
        [self_query, self_key, self_value, self_out], [3 * width, width], False
    )
    gains = gather_small(jnp.transpose(norm_gains))
    gains = jnp.transpose(gains, (1, 0, 2)).reshape(3, model).astype(F32)
    cq_weight, co_weight = gather_weights([cross_query, cross_out], [width, width], False)
    hidden_width = ffn_in.shape[1] * ranks
    in_weight, out_weight = gather_weights([ffn_in, ffn_out], [hidden_width, hidden_width], False)

    owners = [lax.rem(rank - s + ranks, ranks) for s in range(ranks)]
    table = jnp.concatenate(
        [lax.dynamic_slice_in_dim(rel_bias, o * head_count, head_count, 1) for o in owners], axis=1
    )
    bias = window_bias(table, buckets)
    ids = lax.dynamic_slice_in_dim(block_ids, rank * rows, rows, 1).reshape(-1, WIN)

    encoded = passages.reshape(batches * enc_rows, model)
    own_kv = nn(encoded, kv_weight).astype(BF)
    enc_kv = [
        to_heads(column_blocks(own_kv[b * enc_rows : (b + 1) * enc_rows], ranks))
        for b in range(batches)
    ]

    stream = hidden.reshape(batches * rows, model).astype(F32)
    scale_one = norm_scale(stream)
    normed_one = (stream * scale_one * gains[0]).astype(BF)
    qkv = nn(normed_one, qkv_weight).astype(BF)
    context = self_forward(qkv, ids, bias)
    after_self = stream + nt(context, so_weight)
    scale_two = norm_scale(after_self)
    normed_two = (after_self * scale_two * gains[1]).astype(BF)
    cross_rows = nn(normed_two, cq_weight).astype(BF)

    def part(x, b):
        count = x.shape[0] // batches
        return x[b * count : (b + 1) * count]

    queries = [to_heads(column_blocks(part(cross_rows, b), ranks)) for b in range(batches)]
    attended = [cross_forward(queries[b], enc_kv[b]) for b in range(batches)]
    outputs, grads_two, kept = [], [], []
    gain_three = 0.0
    for b in range(batches):
        cross_context = from_heads(attended[b][0])
        after_cross = part(after_self, b) + nt(cross_context, co_weight)
        scale_three = norm_scale(after_cross)
        normed_three = (after_cross * scale_three * gains[2]).astype(BF)
        gate, slope = gate_and_slope(nn(normed_three, in_weight))
        activated = gate.astype(BF)
        outputs.append((after_cross + nt(activated, out_weight)).astype(BF))
        incoming = out_grad[b]
        pre_grad = (nn(incoming, out_weight) * slope).astype(BF)
        normed_grad = nt(pre_grad, in_weight)
        stream_part, gain_part = norm_back(after_cross, scale_three, gains[2], normed_grad)
        gain_three = gain_three + gain_part
        grad_two = incoming.astype(F32) + stream_part
        grads_two.append(grad_two)
        kept.append((cross_context, normed_three, activated, pre_grad, grad_two.astype(BF)))
    cross_context, normed_three, activated, pre_grad, branch_two = (
        jnp.concatenate(parts, axis=0) for parts in zip(*kept)
    )
    incoming = out_grad.reshape(batches * rows, model)

    context_grads = nn(branch_two, co_weight).astype(BF)
    backs = []
    for b in range(batches):
        grad_rows = to_heads(column_blocks(part(context_grads, b), ranks))
        backs.append(cross_backward(queries[b], grad_rows, *attended[b][1:], enc_kv[b]))

    in_grad = tn(normed_three, pre_grad).astype(BF)
    out_weight_grad = tn(incoming, activated).astype(BF)
    in_sum, out_sum = scatter_fsdp(in_grad), scatter_fsdp(out_weight_grad)
    in_total = scatter_tensor(column_blocks(in_sum, ranks))
    out_total = scatter_tensor(column_blocks(out_sum, ranks))

    query_grads = jnp.concatenate([from_heads(back[0]) for back in backs], axis=0)
    normed_grad = nt(query_grads, cq_weight)
    stream_part, gain_two = norm_back(after_self, scale_two, gains[1], normed_grad)
    grad_one = jnp.concatenate(grads_two, axis=0) + stream_part
    branch_one = grad_one.astype(BF)
    context_grad = nn(branch_one, so_weight).astype(BF)
    gq, gk, gv, bias_lanes = self_backward(qkv, context_grad, ids, bias, buckets, rel_bias.shape[0])
    qkv_grad = jnp.concatenate([gq, gk, gv], axis=1)
    normed_grad = nt(qkv_grad, qkv_weight)
    stream_part, gain_one = norm_back(stream, scale_one, gains[0], normed_grad)
    input_grad = grad_one + stream_part

    kv_grad = jnp.concatenate([from_heads(back[1]) for back in backs], axis=0)
    encoded_grad = nt(kv_grad, kv_weight)
    kv_sum = scatter_fsdp(tn(encoded, kv_grad).astype(BF))
    kv_total = scatter_tensor(column_blocks(kv_sum, ranks))

    cross_grads = jnp.concatenate(
        [tn(normed_two, query_grads).astype(BF), tn(branch_two, cross_context).astype(BF)], axis=1
    )
    self_grads = jnp.concatenate(
        [tn(normed_one, qkv_grad).astype(BF), tn(branch_one, context).astype(BF)], axis=1
    )

    def split_total(summed, count):
        per_weight = [column_blocks(w, ranks) for w in column_blocks(summed, count)]
        total = scatter_tensor([jnp.concatenate(list(b), axis=1) for b in zip(*per_weight)])
        return column_blocks(total, count)

    cq_total, co_total = split_total(scatter_fsdp(cross_grads), 2)
    q_total, k_total, v_total, so_total = split_total(scatter_fsdp(self_grads), 4)

    bias_own = jnp.transpose(jnp.sum(bias_lanes, axis=2))
    bias_full = jnp.zeros(rel_bias.shape, F32)
    for s, o in enumerate(owners):
        bias_full = lax.dynamic_update_slice_in_dim(
            bias_full, bias_own[:, s * head_count : (s + 1) * head_count], o * head_count, 1
        )
    small = jnp.concatenate(
        [gain_one.reshape(-1), gain_two.reshape(-1), gain_three.reshape(-1), bias_full.reshape(-1)]
    )
    pad = -small.shape[0] % 1024
    small = jnp.pad(small, (0, pad)).reshape(8, -1)
    small = sum_everywhere(small).reshape(-1)
    gains_sum = jnp.transpose(small[: 3 * model].reshape(3, model))
    bias_total = small[3 * model : 3 * model + rel_bias.size].reshape(rel_bias.shape)

    return (
        jnp.stack(outputs),
        input_grad.reshape(batches, rows, model),
        encoded_grad.reshape(batches, enc_rows, model),
        gains_sum,
        q_total,
        k_total,
        v_total,
        so_total,
        cq_total,
        kv_total[:, :head_width],
        kv_total[:, head_width:],
        co_total,
        in_total,
        out_total,
        bias_total,
    )


def solution(mesh):
    rows = P(None, ("fsdp", "tensor"), None)
    weight = P("fsdp", "tensor")
    in_specs = (rows, rows, P(None, "fsdp"), P(), P("fsdp", None)) + (weight,) * 10 + (P(), rows)
    out_specs = (rows, rows, rows, P()) + (weight,) * 10 + (P(),)
    return jax.shard_map(local, mesh=mesh, in_specs=in_specs, out_specs=out_specs, check_vma=False)
```

time: 2070 us -> 742 us (0.36)
  waiting for transfers between devices: 1230 us -> 176 us
  matrix products: 340 us -> 90.7 us
  Pallas kernels: 0 us -> 176 us
  starting transfers between devices: 22.5 us -> 184 us
  blocking collectives: 127 us -> 0 us
  other arithmetic: 145 us -> 32.8 us
  local copies, waits for them, and re-layouts: 180 us -> 70.5 us
    reduce_scatter x14 -> x0, waiting for transfers between devices: 465 us -> none  [the longest x4 133 us: combine_rows(): lax.psum_scatter(row_term(jnp.int32(0), row_count * lax.axis_size('tensor...]
    all_gather x14 -> x0, waiting for transfers between devices: 315 us -> none  [the longest x1 89.5 us: collect_weights(): lax.all_gather(ffn_in, 'tensor', axis=1, tiled=True)]
    all_to_all x4 -> x0, waiting for transfers between devices: 272 us -> none  [the longest x2 167 us: backward_pass(): lax.all_to_all(shaped, 'tensor', split_axis=0, concat_axis=2, tiled=True)]
    dot_general x100 -> x26, matrix products: 340 us -> 90.7 us  [the longest x9 34.1 us: nn(): return jnp.dot(left, right, preferred_element_type=F32)]
    ppermute x0 -> x119, starting transfers between devices: none -> 184 us  [the longest x63 139 us: shift(): return lax.ppermute(x, axis, [(i, (i + by) % size) for i in range(size)])]
    ppermute x0 -> x119, waiting for transfers between devices: none -> 176 us  [the longest x63 106 us: shift(): return lax.ppermute(x, axis, [(i, (i + by) % size) for i in range(size)])]
    pallas_call x0 -> x14, Pallas kernels: none -> 176 us  [the longest x2 65.1 us: cross_backward(): pl.pallas_call(cross_backward_kernel, grid=(keys // tile,), in_specs=[who...]
    unnamed x40 -> x0, waiting for transfers between devices: 174 us -> none
  transfers between devices with their start and end apart: 38 -> 119, of which waited for: 27 -> 38; matrix products, arithmetic and copies ran while one was open for 26% -> 20% of each run, Pallas kernels for 0% -> 23%
where the time goes in v1:
time: 742 us; the launch traced here: 734 us
  starting transfers between devices  184 us (25%)
  waiting for transfers between devices  176 us (24%)
  Pallas kernels  176 us (24%)
  matrix products  90.7 us (12%)
  local copies, waits for them, and re-layouts  70.5 us (10%)
  other arithmetic  32.8 us (4%)
    ppermute x63, starting transfers between devices, shift(): return lax.ppermute(x, axis, [(i, (i + by) % size) for i in range(size)])  139 us
    ppermute x63, waiting for transfers between devices, shift(): return lax.ppermute(x, axis, [(i, (i + by) % size) for i in range(size)])  106 us
    ppermute x27, waiting for transfers between devices, two_way(): lax.ppermute(x, 'fsdp', [(i, i ^ (second if i & 1 else first)) for i in r...  68.3 us
    pallas_call x2, Pallas kernels, cross_backward(): pl.pallas_call(cross_backward_kernel, grid=(keys // tile,), in_specs=[who...  65.1 us
    pallas_call x1, Pallas kernels, self_backward(): pl.pallas_call(self_backward_kernel, grid=(pairs, windows), in_specs=[par...  35.1 us
    dot_general x9, matrix products, nn(): return jnp.dot(left, right, preferred_element_type=F32)  34.1 us
    dot_general x10, matrix products, nt(): lax.dot_general(left, right, (((1,), (1,)), ((), ())), preferred_element_...  32.1 us
    ppermute x27, starting transfers between devices, two_way(): lax.ppermute(x, 'fsdp', [(i, i ^ (second if i & 1 else first)) for i in r...  32.1 us
  transfers between devices with their start and end apart: 119, of which 38 were waited for; matrix products, arithmetic and copies ran while one was open for 20% of the time, Pallas kernels for 23%

profile of v1, /device:TPU:0, one launch (start us, length us, event | category | flops | bytes accessed | tf_op | source)
XLA Modules:
  0.0 733.5 jit_solution(4071707842669627850)
XLA Ops:
  26.5 9.1 %shard_map.281.bias_ref = f32[12,256,256]{2,1,0:T(8,128)} custom-call(f32[32,12]{1,0:T(8,128)} %pad_maximum_fusion.21.table_ref, s32[256,256]{1,0:T(8,128)} %bucket_ref.3), custom_call_target="tpu_custom_call" | custom-call | flops 31457280 | bytes 3145728 | tf_op jit(solution)/shard_map/pallas_call | solution.py:220
  66.3 5.9 collective-permute-done.42
  75.1 6.3 collective-permute-done.43
  123.9 18.5 %collective-permute-done.56 = bf16[640,384]{1,0:T(8,128)(2,1)} collective-permute-done((bf16[640,384]{1,0:T(8,128)(2,1)S(1)}, bf16[640,384]{1,0:T(8,128)(2,1)}, u32[]{:S(2)}, u32[]{:S(2)}) %collective-permute-start.56) | collective-permute-done | bytes 491552 | tf_op jit(solution)/shard_map/ppermute | solution.py:35
  150.7 13.0 %collective-permute-start.38 = (bf16[640,384]{1,0:T(8,128)(2,1)}, bf16[640,384]{1,0:T(8,128)(2,1)}, u32[]{:S(2)}, u32[]{:S(2)}) collective-permute-start(bf16[640,384]{1,0:T(8,128)(2,1)} %get-tuple-element.103), channel_id=1, source_target_pairs={{0,1},{1,2},{2,3},{3,0},{4,5},{5,6},{6,7},{7,4},{8,9},{9,10},{10,1... | collective-permute-start | bytes 1474568 | tf_op jit(solution)/shard_map/ppermute | solution.py:35
  177.7 16.0 %shard_map.282 = bf16[512,768]{1,0:T(8,128)(2,1)} custom-call(bf16[512,2304]{1,0:T(8,128)(2,1)} %convolution_convert_fusion.4.q_ref.k_ref.v_ref, bf16[512,2304]{1,0:T(8,128)(2,1)} %convolution_convert_fusion.4.q_ref.k_ref.v_ref, bf16[512,2304]{1,0:T(8,128)(2,1)} %convolution_convert_fusion.4.q_ref.k_ref.v_ref, s32[2,256,1]{2,1,0:T(8,128)} %copy.60.col_ref, ...), custom_call_target="tpu_custom_call" | custom-call | flops 1610612736 | bytes 6291456 | tf_op jit(solution)/shard_map/pallas_call | solution.py:262
  202.3 10.6 %collective-permute-start.23 = (bf16[256,192]{1,0:T(8,128)(2,1)S(1)}, bf16[256,192]{1,0:T(8,128)(2,1)S(1)}, u32[]{:S(2)}, u32[]{:S(2)}) collective-permute-start(bf16[256,192]{1,0:T(8,128)(2,1)S(1)} %get-tuple-element.145), channel_id=1, source_target_pairs={{0,3},{1,0},{2,1},{3,2},{4,7},{5,4},{6,5},{7,6},{8,11},{9,8},{10,9... | collective-permute-start | bytes 294920 | tf_op jit(solution)/shard_map/ppermute | solution.py:35
  223.3 12.4 %shard_map.286 = (bf16[1024,192]{1,0:T(8,128)(2,1)S(1)}, f32[1024,192]{1,0:T(8,128)S(1)}, f32[8,1024]{1,0:T(8,128)S(1)}) custom-call(bf16[1024,192]{1,0:T(8,128)(2,1)S(1)} %pad_maximum_fusion.6.q_ref, bf16[2560,384]{1,0:T(8,128)(2,1)S(1)} %pad_maximum_fusion.2.kv_ref), custom_call_target="tpu_custom_call" | custom-call | flops 8053063680 | bytes 1966080 | tf_op jit(solution)/shard_map/pallas_call | solution.py:375
  244.4 12.4 %shard_map.290 = (bf16[1024,192]{1,0:T(8,128)(2,1)S(1)}, f32[1024,192]{1,0:T(8,128)S(1)}, f32[8,1024]{1,0:T(8,128)S(1)}) custom-call(bf16[1024,192]{1,0:T(8,128)(2,1)S(1)} %pad_maximum_fusion.7.q_ref, bf16[2560,384]{1,0:T(8,128)(2,1)S(1)} %copy-done.1), custom_call_target="tpu_custom_call" | custom-call | flops 8053063680 | bytes 1966080 | tf_op jit(solution)/shard_map/pallas_call | solution.py:375
  266.4 6.6 collective-permute-done.59
  273.0 7.2 collective-permute-done.58
  282.8 5.7 shard_map.288
  288.5 6.5 multiply_convert_fusion.1
  300.2 6.3 fusion.7
  349.4 32.5 %shard_map.292 = (bf16[1024,192]{1,0:T(8,128)(2,1)S(1)}, bf16[2560,384]{1,0:T(8,128)(2,1)S(1)}) custom-call(bf16[1024,192]{1,0:T(8,128)(2,1)S(1)} %pad_maximum_fusion.7.q_ref, bf16[1024,192]{1,0:T(8,128)(2,1)S(1)} %pad_maximum_fusion.9.g_ref, f32[1024,192]{1,0:T(8,128)S(1)} %copy-done.6, f32[8,1024]{1,0:T(8,128)S(1)} %get-tuple-element.35.total_ref, ...), custom_call_target="tpu_custom_call" | custom-call | flops 20132659200 | bytes 3932160 | tf_op jit(solution)/shard_map/pallas_call | solution.py:450
  385.1 32.6 %shard_map.291 = (bf16[1024,192]{1,0:T(8,128)(2,1)S(1)}, bf16[2560,384]{1,0:T(8,128)(2,1)S(1)}) custom-call(bf16[1024,192]{1,0:T(8,128)(2,1)S(1)} %pad_maximum_fusion.6.q_ref, bf16[1024,192]{1,0:T(8,128)(2,1)S(1)} %pad_maximum_fusion.8.g_ref, f32[1024,192]{1,0:T(8,128)S(1)} %copy-done.4, f32[8,1024]{1,0:T(8,128)S(1)} %get-tuple-element.32.total_ref, ...), custom_call_target="tpu_custom_call" | custom-call | flops 20132659200 | bytes 3932160 | tf_op jit(solution)/shard_map/pallas_call | solution.py:450
  431.1 20.1 %collective-permute-start.78 = (bf16[640,384]{1,0:T(8,128)(2,1)}, bf16[640,384]{1,0:T(8,128)(2,1)}, u32[]{:S(2)}, u32[]{:S(2)}) collective-permute-start(bf16[640,384]{1,0:T(8,128)(2,1)} %get-tuple-element.117), channel_id=1, source_target_pairs={{0,3},{1,0},{2,1},{3,2},{4,7},{5,4},{6,5},{7,6},{8,11},{9,8},{10,9... | collective-permute-start | bytes 1474568 | tf_op jit(solution)/shard_map/ppermute | solution.py:35
  457.7 35.1 %shard_map.293 = (bf16[512,768]{1,0:T(8,128)(2,1)}, bf16[512,768]{1,0:T(8,128)(2,1)}, bf16[512,768]{1,0:T(8,128)(2,1)}, f32[12,32,256]{2,1,0:T(8,128)}) custom-call(bf16[512,2304]{1,0:T(8,128)(2,1)} %convolution_convert_fusion.4.q_ref.k_ref.v_ref, bf16[512,2304]{1,0:T(8,128)(2,1)} %convolution_convert_fusion.4.q_ref.k_ref.v_ref, ...), custom_call_target="tpu_custom_call" | custom-call | flops 6039797760 | bytes 9437184 | tf_op jit(solution)/shard_map/pallas_call | solution.py:324
  550.9 25.9 %collective-permute-done.77 = bf16[640,384]{1,0:T(8,128)(2,1)} collective-permute-done((bf16[640,384]{1,0:T(8,128)(2,1)}, bf16[640,384]{1,0:T(8,128)(2,1)}, u32[]{:S(2)}, u32[]{:S(2)}) %collective-permute-start.77) | collective-permute-done | bytes 491552 | tf_op jit(solution)/shard_map/ppermute | solution.py:35
  576.8 8.2 %convolution_convert_fusion.5 = bf16[1536,768]{0,1:T(8,128)(2,1)S(1)} fusion(bf16[1280,768]{1,0:T(8,128)(2,1)S(1)} %bitcast.201, bf16[640,384]{1,0:T(8,128)(2,1)} %collective-permute-done.78, bf16[640,384]{1,0:T(8,128)(2,1)} %collective-permute-done.77, bf16[640,384]{1,0:T(8,128)(2,1)} %collective-permute-done.76, bf16[640,384]{1,0:T(8,128)(2,1)} %get-tuple-element.116, ...), kind=kOutput, calls=%fused_computation.25 | convolution fusion | flops 3052535808 | bytes 8257536 | tf_op jit(solution)/shard_map/dot_general | solution.py:28
  588.9 11.1 %fusion.111 = f32[1280,768]{1,0:T(8,128)} fusion(bf16[768,1536]{1,0:T(8,128)(2,1)S(1)} %copy-done.20, bf16[640,384]{1,0:T(8,128)(2,1)} %collective-permute-done.78, bf16[640,384]{1,0:T(8,128)(2,1)} %collective-permute-done.77, bf16[640,384]{1,0:T(8,128)(2,1)} %collective-permute-done.76, bf16[640,384]{1,0:T(8,128)(2,1)S(1)} %copy-done.43, ...), kind=kOutput, calls=%fused_computation.258 | convolution fusion | flops 3051356160 | bytes 10223616 | tf_op jit(solution)/shard_map/dot_general | solution.py:24
  620.2 7.0 collective-permute-done.100
  653.4 14.4 %collective-permute-done.114 = bf16[96,3072]{1,0:T(8,128)(2,1)S(1)} collective-permute-done((bf16[96,3072]{1,0:T(8,128)(2,1)S(1)}, bf16[96,3072]{1,0:T(8,128)(2,1)S(1)}, u32[]{:S(2)}, u32[]{:S(2)}) %collective-permute-start.114) | collective-permute-done | bytes 589856 | tf_op jit(solution)/shard_map/ppermute | solution.py:45
  669.2 23.8 %collective-permute-done.86 = bf16[96,3072]{1,0:T(8,128)(2,1)S(1)} collective-permute-done((bf16[96,3072]{1,0:T(8,128)(2,1)S(1)}, bf16[96,3072]{1,0:T(8,128)(2,1)S(1)}, u32[]{:S(2)}, u32[]{:S(2)}) %collective-permute-start.86) | collective-permute-done | bytes 589856 | tf_op jit(solution)/shard_map/ppermute | solution.py:45
  (615 shorter events, 383.6 us)
Async XLA Ops:
  2.4 44.1 %collective-permute-start.28 = (bf16[96,384]{1,0:T(8,128)(2,1)}, bf16[96,384]{1,0:T(8,128)(2,1)}, u32[]{:S(2)}, u32[]{:S(2)}) collective-permute-start(bf16[96,384]{1,0:T(8,128)(2,1)} %pad_maximum_fusion.17), channel_id=1, source_target_pairs={{0,3},{1,0},{2,1},{3,2},{4,7},{5,4},{6,5},{7,6},{8,11},{9,8},{10,9... | collective-permute-start | bytes 221192 | tf_op jit(solution)/shard_map/ppermute | solution.py:35
  7.4 39.1 %collective-permute-start.27 = (bf16[96,384]{1,0:T(8,128)(2,1)}, bf16[96,384]{1,0:T(8,128)(2,1)}, u32[]{:S(2)}, u32[]{:S(2)}) collective-permute-start(bf16[96,384]{1,0:T(8,128)(2,1)} %pad_maximum_fusion.17), channel_id=1, source_target_pairs={{0,2},{1,3},{2,0},{3,1},{4,6},{5,7},{6,4},{7,5},{8,10},{9,11},{10,... | collective-permute-start | bytes 221192 | tf_op jit(solution)/shard_map/ppermute | solution.py:35
  7.4 42.9 %collective-permute-start.26 = (bf16[96,384]{1,0:T(8,128)(2,1)}, bf16[96,384]{1,0:T(8,128)(2,1)}, u32[]{:S(2)}, u32[]{:S(2)}) collective-permute-start(bf16[96,384]{1,0:T(8,128)(2,1)} %pad_maximum_fusion.17), channel_id=1, source_target_pairs={{0,1},{1,2},{2,3},{3,0},{4,5},{5,6},{6,7},{7,4},{8,9},{9,10},{10,1... | collective-permute-start | bytes 221192 | tf_op jit(solution)/shard_map/ppermute | solution.py:35
  120.2 43.5 %collective-permute-start.10 = (bf16[96,3072]{1,0:T(8,128)(2,1)}, bf16[96,3072]{1,0:T(8,128)(2,1)}, u32[]{:S(2)}, u32[]{:S(2)}) collective-permute-start(bf16[96,3072]{1,0:T(8,128)(2,1)} %collective-permute-done.6.refs_1_), channel_id=1, source_target_pairs={{0,4},{4,0},{8,12},{12,8},{16,20},{20,16},{24,28},{28,24},{1,5},{5... | collective-permute-start | bytes 1769480 | tf_op jit(solution)/shard_map/ppermute | solution.py:40
  146.5 111.4 %collective-permute-start.46 = (bf16[96,6144]{1,0:T(8,128)(2,1)}, bf16[96,6144]{1,0:T(8,128)(2,1)}, u32[]{:S(2)}, u32[]{:S(2)}) collective-permute-start(bf16[96,6144]{1,0:T(8,128)(2,1)} %slice_dynamic-update-slice_fusion.refs_0_), channel_id=1, source_target_pairs={{0,16},{4,12},{8,24},{12,4},{16,0},{20,28},{24,8},{28,20},{1,17},{... | collective-permute-start | bytes 3538952 | tf_op jit(solution)/shard_map/ppermute | solution.py:45
  150.0 64.5 %collective-permute-start.45 = (bf16[96,6144]{1,0:T(8,128)(2,1)}, bf16[96,6144]{1,0:T(8,128)(2,1)}, u32[]{:S(2)}, u32[]{:S(2)}) collective-permute-start(bf16[96,6144]{1,0:T(8,128)(2,1)} %slice_dynamic-update-slice_fusion.refs_0_), channel_id=1, source_target_pairs={{0,8},{4,20},{8,0},{12,28},{16,24},{20,4},{24,16},{28,12},{1,9},{5... | collective-permute-start | bytes 3538952 | tf_op jit(solution)/shard_map/ppermute | solution.py:45
  150.7 49.5 %collective-permute-start.38 = (bf16[640,384]{1,0:T(8,128)(2,1)}, bf16[640,384]{1,0:T(8,128)(2,1)}, u32[]{:S(2)}, u32[]{:S(2)}) collective-permute-start(bf16[640,384]{1,0:T(8,128)(2,1)} %get-tuple-element.103), channel_id=1, source_target_pairs={{0,1},{1,2},{2,3},{3,0},{4,5},{5,6},{6,7},{7,4},{8,9},{9,10},{10,1... | collective-permute-start | bytes 1474568 | tf_op jit(solution)/shard_map/ppermute | solution.py:35
  214.5 49.2 %collective-permute-start.47 = (bf16[96,6144]{1,0:T(8,128)(2,1)}, bf16[96,6144]{1,0:T(8,128)(2,1)}, u32[]{:S(2)}, u32[]{:S(2)}) collective-permute-start(bf16[96,6144]{1,0:T(8,128)(2,1)} %collective-permute-done.45.refs_1_), channel_id=1, source_target_pairs={{0,16},{4,12},{8,24},{12,4},{16,0},{20,28},{24,8},{28,20},{1,17},{... | collective-permute-start | bytes 3538952 | tf_op jit(solution)/shard_map/ppermute | solution.py:45
  332.1 51.5 %collective-permute-start.63 = (bf16[256,192]{1,0:T(8,128)(2,1)S(1)}, bf16[256,192]{1,0:T(8,128)(2,1)S(1)}, u32[]{:S(2)}, u32[]{:S(2)}) collective-permute-start(bf16[256,192]{1,0:T(8,128)(2,1)S(1)} %get-tuple-element.135), channel_id=1, source_target_pairs={{0,1},{1,2},{2,3},{3,0},{4,5},{5,6},{6,7},{7,4},{8,9},{9,10},{10,1... | collective-permute-start | bytes 294920 | tf_op jit(solution)/shard_map/ppermute | solution.py:35
  332.6 52.3 %collective-permute-start.62 = (bf16[256,192]{1,0:T(8,128)(2,1)S(1)}, bf16[256,192]{1,0:T(8,128)(2,1)S(1)}, u32[]{:S(2)}, u32[]{:S(2)}) collective-permute-start(bf16[256,192]{1,0:T(8,128)(2,1)S(1)} %get-tuple-element.136), channel_id=1, source_target_pairs={{0,2},{1,3},{2,0},{3,1},{4,6},{5,7},{6,4},{7,5},{8,10},{9,11},{10,... | collective-permute-start | bytes 294920 | tf_op jit(solution)/shard_map/ppermute | solution.py:35
  346.4 38.6 %collective-permute-start.61 = (bf16[256,192]{1,0:T(8,128)(2,1)S(1)}, bf16[256,192]{1,0:T(8,128)(2,1)S(1)}, u32[]{:S(2)}, u32[]{:S(2)}) collective-permute-start(bf16[256,192]{1,0:T(8,128)(2,1)S(1)} %get-tuple-element.137), channel_id=1, source_target_pairs={{0,3},{1,0},{2,1},{3,2},{4,7},{5,4},{6,5},{7,6},{8,11},{9,8},{10,9... | collective-permute-start | bytes 294920 | tf_op jit(solution)/shard_map/ppermute | solution.py:35
  382.0 39.7 %collective-permute-start.72 = (bf16[256,192]{1,0:T(8,128)(2,1)S(1)}, bf16[256,192]{1,0:T(8,128)(2,1)S(1)}, u32[]{:S(2)}, u32[]{:S(2)}) collective-permute-start(bf16[256,192]{1,0:T(8,128)(2,1)S(1)} %get-tuple-element.171), channel_id=1, source_target_pairs={{0,3},{1,0},{2,1},{3,2},{4,7},{5,4},{6,5},{7,6},{8,11},{9,8},{10,9... | collective-permute-start | bytes 294920 | tf_op jit(solution)/shard_map/ppermute | solution.py:35
  382.4 42.2 %collective-permute-start.71 = (bf16[256,192]{1,0:T(8,128)(2,1)S(1)}, bf16[256,192]{1,0:T(8,128)(2,1)S(1)}, u32[]{:S(2)}, u32[]{:S(2)}) collective-permute-start(bf16[256,192]{1,0:T(8,128)(2,1)S(1)} %get-tuple-element.172), channel_id=1, source_target_pairs={{0,2},{1,3},{2,0},{3,1},{4,6},{5,7},{6,4},{7,5},{8,10},{9,11},{10,... | collective-permute-start | bytes 294920 | tf_op jit(solution)/shard_map/ppermute | solution.py:35
  383.6 43.3 %collective-permute-start.70 = (bf16[256,192]{1,0:T(8,128)(2,1)S(1)}, bf16[256,192]{1,0:T(8,128)(2,1)S(1)}, u32[]{:S(2)}, u32[]{:S(2)}) collective-permute-start(bf16[256,192]{1,0:T(8,128)(2,1)S(1)} %get-tuple-element.173), channel_id=1, source_target_pairs={{0,1},{1,2},{2,3},{3,0},{4,5},{5,6},{6,7},{7,4},{8,9},{9,10},{10,1... | collective-permute-start | bytes 294920 | tf_op jit(solution)/shard_map/ppermute | solution.py:35
  424.6 120.6 %collective-permute-start.75 = (bf16[640,384]{1,0:T(8,128)(2,1)}, bf16[640,384]{1,0:T(8,128)(2,1)}, u32[]{:S(2)}, u32[]{:S(2)}) collective-permute-start(bf16[640,384]{1,0:T(8,128)(2,1)} %get-tuple-element.113), channel_id=1, source_target_pairs={{0,3},{1,0},{2,1},{3,2},{4,7},{5,4},{6,5},{7,6},{8,11},{9,8},{10,9... | collective-permute-start | bytes 1474568 | tf_op jit(solution)/shard_map/ppermute | solution.py:35
  426.9 123.4 %collective-permute-start.74 = (bf16[640,384]{1,0:T(8,128)(2,1)}, bf16[640,384]{1,0:T(8,128)(2,1)}, u32[]{:S(2)}, u32[]{:S(2)}) collective-permute-start(bf16[640,384]{1,0:T(8,128)(2,1)} %get-tuple-element.114), channel_id=1, source_target_pairs={{0,2},{1,3},{2,0},{3,1},{4,6},{5,7},{6,4},{7,5},{8,10},{9,11},{10,... | collective-permute-start | bytes 1474568 | tf_op jit(solution)/shard_map/ppermute | solution.py:35
  428.0 122.3 %collective-permute-start.73 = (bf16[640,384]{1,0:T(8,128)(2,1)}, bf16[640,384]{1,0:T(8,128)(2,1)}, u32[]{:S(2)}, u32[]{:S(2)}) collective-permute-start(bf16[640,384]{1,0:T(8,128)(2,1)} %get-tuple-element.115), channel_id=1, source_target_pairs={{0,1},{1,2},{2,3},{3,0},{4,5},{5,6},{6,7},{7,4},{8,9},{9,10},{10,1... | collective-permute-start | bytes 1474568 | tf_op jit(solution)/shard_map/ppermute | solution.py:35
  431.1 119.7 %collective-permute-start.78 = (bf16[640,384]{1,0:T(8,128)(2,1)}, bf16[640,384]{1,0:T(8,128)(2,1)}, u32[]{:S(2)}, u32[]{:S(2)}) collective-permute-start(bf16[640,384]{1,0:T(8,128)(2,1)} %get-tuple-element.117), channel_id=1, source_target_pairs={{0,3},{1,0},{2,1},{3,2},{4,7},{5,4},{6,5},{7,6},{8,11},{9,8},{10,9... | collective-permute-start | bytes 1474568 | tf_op jit(solution)/shard_map/ppermute | solution.py:35
  550.3 78.3 %collective-permute-start.105 = (bf16[4,96,3072]{2,1,0:T(8,128)(2,1)}, bf16[4,96,3072]{2,1,0:T(8,128)(2,1)S(1)}, u32[]{:S(2)}, u32[]{:S(2)}) collective-permute-start(bf16[4,96,3072]{2,1,0:T(8,128)(2,1)} %dynamic-slice_bitcast_fusion.1), channel_id=1, source_target_pairs={{0,4},{4,0},{8,12},{12,8},{16,20},{20,16},{24,28},{28,24},{1,5},{5... | collective-permute-start | bytes 7077896 | tf_op jit(solution)/shard_map/ppermute | solution.py:40
  550.3 81.4 %collective-permute-start.112 = (bf16[4,96,3072]{2,1,0:T(8,128)(2,1)}, bf16[4,96,3072]{2,1,0:T(8,128)(2,1)S(1)}, u32[]{:S(2)}, u32[]{:S(2)}) collective-permute-start(bf16[4,96,3072]{2,1,0:T(8,128)(2,1)} %dynamic-slice_bitcast_fusion), channel_id=1, source_target_pairs={{0,4},{4,0},{8,12},{12,8},{16,20},{20,16},{24,28},{28,24},{1,5},{5... | collective-permute-start | bytes 7077896 | tf_op jit(solution)/shard_map/ppermute | solution.py:40
  629.6 64.9 %collective-permute-start.106 = (bf16[96,3072]{1,0:T(8,128)(2,1)S(1)}, bf16[96,3072]{1,0:T(8,128)(2,1)S(1)}, u32[]{:S(2)}, u32[]{:S(2)}) collective-permute-start(bf16[96,3072]{1,0:T(8,128)(2,1)S(1)} %get-tuple-element.108), channel_id=1, source_target_pairs={{0,8},{4,20},{8,0},{12,28},{16,24},{20,4},{24,16},{28,12},{1,9},{5... | collective-permute-start | bytes 1769480 | tf_op jit(solution)/shard_map/ppermute | solution.py:45
  644.9 56.1 %collective-permute-start.113 = (bf16[96,3072]{1,0:T(8,128)(2,1)S(1)}, bf16[96,3072]{1,0:T(8,128)(2,1)S(1)}, u32[]{:S(2)}, u32[]{:S(2)}) collective-permute-start(bf16[96,3072]{1,0:T(8,128)(2,1)S(1)} %get-tuple-element.106), channel_id=1, source_target_pairs={{0,8},{4,20},{8,0},{12,28},{16,24},{20,4},{24,16},{28,12},{1,9},{5... | collective-permute-start | bytes 1769480 | tf_op jit(solution)/shard_map/ppermute | solution.py:45
  649.0 71.3 %collective-permute-start.85 = (bf16[96,3072]{1,0:T(8,128)(2,1)S(1)}, bf16[96,3072]{1,0:T(8,128)(2,1)S(1)}, u32[]{:S(2)}, u32[]{:S(2)}) collective-permute-start(bf16[96,3072]{1,0:T(8,128)(2,1)S(1)} %get-tuple-element.110), channel_id=1, source_target_pairs={{0,8},{4,20},{8,0},{12,28},{16,24},{20,4},{24,16},{28,12},{1,9},{5... | collective-permute-start | bytes 1769480 | tf_op jit(solution)/shard_map/ppermute | solution.py:45
  651.7 41.3 %collective-permute-start.86 = (bf16[96,3072]{1,0:T(8,128)(2,1)S(1)}, bf16[96,3072]{1,0:T(8,128)(2,1)S(1)}, u32[]{:S(2)}, u32[]{:S(2)}) collective-permute-start(bf16[96,3072]{1,0:T(8,128)(2,1)S(1)} %get-tuple-element.111), channel_id=1, source_target_pairs={{0,8},{4,20},{8,0},{12,28},{16,24},{20,4},{24,16},{28,12},{1,9},{5... | collective-permute-start | bytes 1769480 | tf_op jit(solution)/shard_map/ppermute | solution.py:45
  (198 other events, 3864.5 us)

commit v2 on v1

v2 whole, which is shorter than its diff:
```python
import functools

import jax
import jax.numpy as jnp
from jax import lax
from jax.experimental import pallas as pl
from jax.experimental.pallas import tpu as pltpu
from jax.sharding import PartitionSpec as P

DH = 64
WIN = 256
EPSILON = 1e-06
MASKED = -1000000000.0
BF = jnp.bfloat16
F32 = jnp.float32
MIB = 1024 * 1024


def nn(left, right):
    return jnp.dot(left, right, preferred_element_type=F32)


def nt(left, right):
    return lax.dot_general(left, right, (((1,), (1,)), ((), ())), preferred_element_type=F32)


def tn(left, right):
    return lax.dot_general(left, right, (((0,), (0,)), ((), ())), preferred_element_type=F32)


def shift(x, axis, by):
    size = lax.axis_size(axis)
    if by % size == 0:
        return x
    return lax.ppermute(x, axis, [(i, (i + by) % size) for i in range(size)])


def flip(x, axis, bits):
    size = lax.axis_size(axis)
    return lax.ppermute(x, axis, [(i, i ^ bits) for i in range(size)])


def two_way(x, swapped):
    first, second = (4, 2) if swapped else (2, 4)
    return lax.ppermute(x, "fsdp", [(i, i ^ (second if i & 1 else first)) for i in range(8)])


def assemble_kernel(starts, *refs):
    pieces, outs = refs[:8], refs[8:]
    me = lax.axis_index("fsdp")
    odd = lax.rem(me, 2)
    x_bit, y_bit = lax.rem(me // 2, 2), me // 4

    def flipped(dx, dy, dc):
        new_x = x_bit + dx - 2 * x_bit * dx
        new_y = y_bit + dy - 2 * y_bit * dy
        new_c = odd + dc - 2 * odd * dc
        return new_y * 4 + new_x * 2 + new_c

    even = 1 - odd
    places = [
        flipped(0, 0, 0),
        flipped(even, odd, 0),
        flipped(odd, even, 0),
        flipped(1, 1, 0),
        flipped(0, 0, 1),
        flipped(odd, even, 1),
        flipped(even, odd, 1),
        flipped(1, 1, 1),
    ]
    ranks, rows = pieces[0].shape[0], pieces[0].shape[1]
    rank = lax.axis_index("tensor")
    for place, piece in zip(places, pieces):
        here = pl.ds(pl.multiple_of(place * rows, rows), rows)
        for s in range(ranks):
            block = piece[lax.rem(rank - s + ranks, ranks)]
            for out_ref, parts in zip(outs, starts):
                for first, width, base, stride in parts:
                    out_ref[here, base + s * stride : base + s * stride + width] = block[
                        :, first : first + width
                    ]


def gather_paths(piece):
    if lax.axis_size("fsdp") != 8 or piece.shape[1] % 16:
        return [piece]
    return [piece, two_way(piece, False), two_way(piece, True)]


def gather_far(pieces):
    if len(pieces) == 1:
        return pieces
    return pieces + [two_way(pieces[1], True)]


def gather_cores(pieces):
    if len(pieces) == 1:
        return [lax.all_gather(pieces[0], "fsdp", axis=1, tiled=True)]
    return pieces + [flip(p, "fsdp", 1) for p in pieces]


def gather_end(pieces, layout, earlier=()):
    ranks, rows = pieces[0].shape[:2]
    widths = [sum(part[1] for part in parts) * ranks for parts in layout]
    if len(pieces) == 1:
        outs = []
        rank = lax.axis_index("tensor")
        order = lax.rem(rank + ranks - jnp.arange(ranks, dtype=jnp.int32), ranks)
        blocks = jnp.take(pieces[0], order, axis=0)
        for parts in layout:
            columns = {}
            for first, width, base, stride in parts:
                for s in range(ranks):
                    columns[base + s * stride] = blocks[s, :, first : first + width]
            outs.append(jnp.concatenate([columns[k] for k in sorted(columns)], axis=1))
        return outs
    return run(
        "assemble",
        functools.partial(assemble_kernel, layout),
        pieces,
        [pl.BlockSpec(memory_space=pltpu.VMEM)] * 8,
        earlier,
        sum(widths) * rows / 96000 + 1,
        out_shape=[jax.ShapeDtypeStruct((8 * rows, w), pieces[0].dtype) for w in widths],
        compiler_params=pltpu.CompilerParams(vmem_limit_bytes=48 * MIB),
    )


def run(name, kernel, operands, in_specs, earlier=(), took=1, **how):
    count = len(earlier)

    def body(*refs):
        kernel(*refs[count:])

    return pl.pallas_call(
        body,
        in_specs=[pl.BlockSpec(memory_space=pl.ANY)] * count + in_specs,
        cost_estimate=pl.CostEstimate(
            flops=int(took * 1.1e9), bytes_accessed=int(took * 3.5e6), transcendentals=0
        ),
        name=name,
        **how,
    )(*earlier, *operands)


def join_kernel(*refs):
    first = 0
    for ref in refs[:-1]:
        refs[-1][:, first : first + ref.shape[1]] = ref[...]
        first += ref.shape[1]


def joined(parts, earlier=()):
    if parts[0].shape[0] % 16:
        return beside(parts)
    return run(
        "join",
        join_kernel,
        parts,
        [pl.BlockSpec(memory_space=pltpu.VMEM)] * len(parts),
        earlier,
        1.5,
        out_shape=jax.ShapeDtypeStruct(
            (parts[0].shape[0], sum(x.shape[1] for x in parts)), parts[0].dtype
        ),
    )


def gather_ranks(shards, earlier=()):
    own = joined(shards, earlier)
    return [shift(own, "tensor", s) for s in range(lax.axis_size("tensor"))]


def gather_small(shard):
    size = lax.axis_size("fsdp")
    held = shard[None]
    bit = 1
    while bit < size:
        held = jnp.concatenate([held, flip(held, "fsdp", bit)], axis=0)
        bit *= 2
    order = jnp.bitwise_xor(jnp.arange(size, dtype=jnp.int32), lax.axis_index("fsdp"))
    return jnp.take(held, order, axis=0)


def sum_everywhere(x):
    for axis in ("fsdp", "tensor"):
        bits = []
        while 1 << len(bits) < lax.axis_size(axis):
            bits.append(1 << len(bits))
        if len(bits) % 2:
            x = x + flip(x, axis, bits.pop(0))
        for one, two in zip(bits[::2], bits[1::2]):
            x = (x + flip(x, axis, one)) + (flip(x, axis, two) + flip(x, axis, one + two))
    return x


def grad_kernel(phases, left_count, *refs):
    lefts, refs = refs[:left_count], refs[left_count:]
    outs, across_ref, rows_ref = refs[-4:-2], refs[-2], refs[-1]
    step = pl.program_id(0)
    me = lax.axis_index("fsdp")
    odd = lax.rem(me, 2)
    x_bit, y_bit = lax.rem(me // 2, 2), me // 4
    first, ref, before = 0, 0, None
    for indices, count, blocks in phases:
        rights = refs[ref : ref + count]
        ref += count

        if indices != before:

            @pl.when(step == first)
            def _(indices=indices):
                done = 0
                for i in indices:
                    across_ref[:, done : done + lefts[i].shape[0]] = jnp.transpose(lefts[i][...])
                    done += lefts[i].shape[0]

        before = indices

        @pl.when((step >= first) & (step < first + blocks))
        def _(rights=rights):
            total, done = 0.0, 0
            for right in rights:
                total = total + nn(across_ref[:, done : done + right.shape[0]], right[...])
                done += right.shape[0]
            rows_ref[...] = total.astype(BF)

        first += blocks
    size = rows_ref.shape[0] // 8
    for out_ref, core in zip(outs, (odd, 1 - odd)):
        even = 1 - core
        for place, (dx, dy) in enumerate(((0, 0), (core, even), (even, core), (1, 1))):
            block = (y_bit + dy - 2 * y_bit * dy) * 4 + (x_bit + dx - 2 * x_bit * dx) * 2 + core
            out_ref[place * size : (place + 1) * size, :] = rows_ref[
                pl.ds(pl.multiple_of(block * size, size), size), :
            ]


def weight_grads(lefts, phases, earlier=(), tile=768):
    model = lefts[0].shape[1]
    if lax.axis_size("fsdp") != 8:
        whole = []
        for indices, rights in phases:
            rights = [beside(list(y)) if y.ndim == 3 else y for y in rights]
            whole.append(tn(below([lefts[i] for i in indices]), below(rights)))
        return [beside(whole).astype(BF)]
    specs = [pl.BlockSpec(x.shape, lambda i: (0, 0)) for x in lefts]
    operands, sizes, first = list(lefts), [], 0
    for indices, rights in phases:
        deep = rights[0].ndim == 3
        count = rights[0].shape[0] if deep else rights[0].shape[1] // tile
        operands += rights
        for y in rights:
            if deep:
                shape, where = (None, y.shape[1], tile), lambda i, k: (k, 0, 0)
            else:
                shape, where = (y.shape[0], tile), lambda i, k: (0, k)
            specs.append(
                pl.BlockSpec(
                    shape,
                    lambda i, f=first, n=count, where=where: where(i, jnp.clip(i - f, 0, n - 1)),
                )
            )
        sizes.append((indices, len(rights), count))
        first += count
    deepest = max(sum(lefts[i].shape[0] for i in indices) for indices, _ in phases)
    shape = jax.ShapeDtypeStruct((model // 2, first * tile), BF)
    kept_and_sent = run(
        "weight_grads",
        functools.partial(grad_kernel, sizes, len(lefts)),
        [*operands],
        specs,
        earlier,
        first * 1.4,
        grid=(first,),
        out_specs=[pl.BlockSpec((model // 2, tile), lambda i: (0, i))] * 2,
        out_shape=[shape, shape],
        scratch_shapes=[pltpu.VMEM((model, deepest), BF), pltpu.VMEM((model, tile), BF)],
        compiler_params=pltpu.CompilerParams(vmem_limit_bytes=48 * MIB),
    )
    return list(kept_and_sent)


def rows_back_kernel(grad_ref, weight_ref, out_ref):
    out_ref[...] = nt(grad_ref[...], weight_ref[...]).astype(BF)


def rows_back(grad, weight, earlier=()):
    rows, model = grad.shape[0], weight.shape[0]
    tile = 256
    return run(
        "rows_back",
        rows_back_kernel,
        [grad, weight],
        [
            pl.BlockSpec(grad.shape, lambda i: (0, 0)),
            pl.BlockSpec((tile, weight.shape[1]), lambda i: (i, 0)),
        ],
        earlier,
        6,
        grid=(model // tile,),
        out_specs=pl.BlockSpec((rows, tile), lambda i: (0, i)),
        out_shape=jax.ShapeDtypeStruct((rows, model), BF),
        compiler_params=pltpu.CompilerParams(vmem_limit_bytes=48 * MIB),
    )


def scatter_cores(grads):
    if len(grads) == 1:
        return [lax.psum_scatter(grads[0].astype(F32), "fsdp", scatter_dimension=0, tiled=True)]
    return [grads[0], flip(grads[1], "fsdp", 1)]


def halves_kernel(kept_ref, sent_ref, low_ref, high_ref):
    half = low_ref.shape[0]
    for out_ref, rows in ((low_ref, slice(0, half)), (high_ref, slice(half, 2 * half))):
        both = kept_ref[rows, :].astype(F32) + sent_ref[rows, :].astype(F32)
        out_ref[...] = both.astype(out_ref.dtype)


def sum_halves(name, kept, received, low_type, earlier):
    rows, width = kept.shape
    tile = 768
    whole = pl.BlockSpec((rows, tile), lambda i: (0, i))
    half = pl.BlockSpec((rows // 2, tile), lambda i: (0, i))
    return run(
        name,
        halves_kernel,
        [kept, received],
        [whole, whole],
        earlier,
        rows * width / 300000,
        grid=(width // tile,),
        out_specs=[half, half],
        out_shape=[
            jax.ShapeDtypeStruct((rows // 2, width), low_type),
            jax.ShapeDtypeStruct((rows // 2, width), BF),
        ],
        compiler_params=pltpu.CompilerParams(vmem_limit_bytes=48 * MIB),
    )


def scatter_paths(stage, earlier=()):
    if len(stage) == 1:
        return stage
    low, high = sum_halves("sum_cores", *stage, BF, earlier)
    return [low, two_way(high, False)]


def scatter_far(stage, earlier=()):
    if len(stage) == 1:
        return stage
    low, high = sum_halves("sum_paths", *stage, F32, earlier)
    return [low, two_way(high, True)]


def blocks_kernel(layout, kept_ref, received_ref, out_ref):
    total = (kept_ref[...] + received_ref[...].astype(F32)).astype(BF)
    for s in range(out_ref.shape[0]):
        for first, width, base, stride in layout:
            out_ref[s, :, first : first + width] = total[
                :, base + s * stride : base + s * stride + width
            ]


def scatter_end(stage, layout, earlier=()):
    ranks = lax.axis_size("tensor")
    if len(stage) == 1:
        parts = [
            jnp.concatenate(
                [stage[0][:, b + s * d : b + s * d + w] for _, w, b, d in layout], axis=1
            )
            for s in range(ranks)
        ]
        return jnp.stack(parts).astype(BF)
    rows, width = stage[0].shape
    return run(
        "sum_far",
        functools.partial(blocks_kernel, layout),
        stage,
        [pl.BlockSpec(memory_space=pltpu.VMEM)] * 2,
        earlier,
        2,
        out_shape=jax.ShapeDtypeStruct((ranks, rows, width // ranks), BF),
        compiler_params=pltpu.CompilerParams(vmem_limit_bytes=48 * MIB),
    )


def scatter_tensor(blocks):
    parts = lax.all_to_all(blocks, "tensor", split_axis=0, concat_axis=0, tiled=True)
    return jnp.sum(parts.astype(F32), axis=0)


def column_blocks(x, count):
    width = x.shape[1] // count
    return [x[:, s * width : (s + 1) * width] for s in range(count)]


def round_moves(r, back):
    size, ranks = lax.axis_size("fsdp"), lax.axis_size("tensor")
    pairs = []
    for f in range(size):
        for t in range(ranks):
            c, t1, t0 = f & 1, t >> 1, t & 1
            pair = (f * ranks + t, ((f ^ c) | t0) * ranks + 2 * (r ^ t1) + c)
            pairs.append(pair[::-1] if back else pair)
    return pairs


def gathered(x):
    high = lax.axis_index("tensor") // 2
    parts = [
        lax.ppermute(
            lax.dynamic_index_in_dim(x, r ^ high, 0, keepdims=False),
            ("fsdp", "tensor"),
            round_moves(r, False),
        )
        for r in range(2)
    ]
    return below(parts)


def returned(x):
    half = x.shape[0] // 2
    return [
        lax.ppermute(x[r * half : (r + 1) * half], ("fsdp", "tensor"), round_moves(r, True))
        for r in range(2)
    ]


def by_batch(parts, dtype):
    high = lax.axis_index("tensor") // 2
    return jnp.stack([jnp.where(high == r, parts[0], parts[1]) for r in range(2)]).astype(dtype)


def beside(blocks):
    return jnp.concatenate(list(blocks), axis=1)


def below(blocks):
    return jnp.concatenate(list(blocks), axis=0)


def bias_kernel(heads, table_ref, bucket_ref, out_ref):
    group = pl.program_id(0)
    count = out_ref.shape[0]
    buckets = table_ref.shape[0]

    def some_rows(i, carry):
        rows = pl.ds(i * 32, 32)
        bucket = bucket_ref[rows, :]
        found = [jnp.zeros(bucket.shape, F32) for _ in range(count)]
        for b in range(buckets):
            here = bucket == b
            for h in range(count):
                found[h] = jnp.where(here, table_ref[b, group * count + h], found[h])
        for h in range(count):
            out_ref[h, rows, :] = found[h]
        return carry

    lax.fori_loop(0, bucket_ref.shape[0] // 32, some_rows, 0)


def window_bias(table, buckets, earlier=()):
    heads = table.shape[1]
    count = 4
    return run(
        "window_bias",
        functools.partial(bias_kernel, heads),
        [table, buckets],
        [
            pl.BlockSpec(memory_space=pltpu.SMEM),
            pl.BlockSpec((WIN, WIN), lambda g: (0, 0)),
        ],
        earlier,
        9,
        grid=(heads // count,),
        out_specs=pl.BlockSpec((count, WIN, WIN), lambda g: (g, 0, 0)),
        out_shape=jax.ShapeDtypeStruct((heads, WIN, WIN), F32),
    )


def allowed_pairs(col_ref, row_ref, window):
    rows = lax.broadcasted_iota(jnp.int32, (WIN, WIN), 0)
    cols = lax.broadcasted_iota(jnp.int32, (WIN, WIN), 1)
    return (col_ref[window] == row_ref[window]) & (cols <= rows)


def self_softmax(q, k, bias, allowed):
    scores = jnp.where(allowed, nt(q, k) + bias, MASKED)
    raised = jnp.exp(scores - jnp.max(scores, axis=1, keepdims=True))
    return raised / jnp.sum(raised, axis=1, keepdims=True)


def self_forward_kernel(q_ref, k_ref, v_ref, col_ref, row_ref, bias_ref, out_ref):
    for w in range(q_ref.shape[0] // WIN):
        allowed = allowed_pairs(col_ref, row_ref, w)
        rows = slice(w * WIN, (w + 1) * WIN)
        for h in range(2):
            lanes = slice(h * DH, (h + 1) * DH)
            prob = self_softmax(q_ref[rows, lanes], k_ref[rows, lanes], bias_ref[h], allowed)
            out_ref[rows, lanes] = nn(prob.astype(BF), v_ref[rows, lanes]).astype(BF)


def self_forward(qkv, ids, bias, earlier=()):
    rows, width = qkv.shape[0], qkv.shape[1] // 3
    pairs, windows = width // 128, rows // WIN

    def part(k):
        return pl.BlockSpec((rows, 128), lambda g, k=k: (0, k * pairs + g))

    return run(
        "self_forward",
        self_forward_kernel,
        [qkv, qkv, qkv, ids.reshape(windows, WIN, 1), ids.reshape(windows, 1, WIN), bias],
        [
            part(0),
            part(1),
            part(2),
            pl.BlockSpec((windows, WIN, 1), lambda g: (0, 0, 0)),
            pl.BlockSpec((windows, 1, WIN), lambda g: (0, 0, 0)),
            pl.BlockSpec((2, WIN, WIN), lambda g: (g, 0, 0)),
        ],
        earlier,
        12,
        grid=(pairs,),
        out_specs=part(0),
        out_shape=jax.ShapeDtypeStruct((rows, width), BF),
    )


def self_backward_kernel(
    q_ref, k_ref, v_ref, g_ref, col_ref, row_ref, bias_ref, gq_ref, gk_ref, gv_ref, sum_ref
):
    for w in range(q_ref.shape[0] // WIN):
        allowed = allowed_pairs(col_ref, row_ref, w)
        rows = slice(w * WIN, (w + 1) * WIN)
        for h in range(2):
            lanes = slice(h * DH, (h + 1) * DH)
            q, k, v = q_ref[rows, lanes], k_ref[rows, lanes], v_ref[rows, lanes]
            g = g_ref[rows, lanes]
            prob = self_softmax(q, k, bias_ref[h], allowed)
            prob_grad = nt(g, v)
            inner = jnp.sum(prob_grad * prob, axis=1, keepdims=True)
            score_grad = (prob * (prob_grad - inner)).astype(BF)
            gq_ref[rows, lanes] = nn(score_grad, k).astype(BF)
            gk_ref[rows, lanes] = tn(score_grad, q).astype(BF)
            gv_ref[rows, lanes] = tn(prob.astype(BF), g).astype(BF)
            if w:
                sum_ref[h] += score_grad.astype(F32)
            else:
                sum_ref[h] = score_grad.astype(F32)


def self_backward(qkv, grad, ids, bias, earlier=()):
    rows, width = qkv.shape[0], qkv.shape[1] // 3
    pairs, windows = width // 128, rows // WIN

    def part(k):
        return pl.BlockSpec((rows, 128), lambda g, k=k: (0, k * pairs + g))

    tables = pl.BlockSpec((2, WIN, WIN), lambda g: (g, 0, 0))
    return run(
        "self_backward",
        self_backward_kernel,
        [qkv, qkv, qkv, grad, ids.reshape(windows, WIN, 1), ids.reshape(windows, 1, WIN), bias],
        [
            part(0),
            part(1),
            part(2),
            part(0),
            pl.BlockSpec((windows, WIN, 1), lambda g: (0, 0, 0)),
            pl.BlockSpec((windows, 1, WIN), lambda g: (0, 0, 0)),
            tables,
        ],
        earlier,
        18,
        grid=(pairs,),
        out_specs=[part(0)] * 3 + [tables],
        out_shape=[jax.ShapeDtypeStruct((rows, width), BF)] * 3
        + [jax.ShapeDtypeStruct((2 * pairs, WIN, WIN), F32)],
    )


def bucket_kernel(sum_ref, bucket_ref, out_ref):
    def one_bucket(b, carry):
        here = bucket_ref[...] == b
        for h in range(sum_ref.shape[0]):
            out_ref[h, pl.ds(b, 1), :] = jnp.sum(
                jnp.where(here, sum_ref[h], 0.0), axis=0, keepdims=True
            )
        return carry

    lax.fori_loop(0, out_ref.shape[1], one_bucket, 0)


def bucket_sums(sums, buckets, count, earlier=()):
    heads = sums.shape[0]
    return run(
        "bucket_sums",
        bucket_kernel,
        [sums, buckets],
        [
            pl.BlockSpec((4, WIN, WIN), lambda g: (g, 0, 0)),
            pl.BlockSpec((WIN, WIN), lambda g: (0, 0)),
        ],
        earlier,
        13,
        grid=(heads // 4,),
        out_specs=pl.BlockSpec((4, count, WIN), lambda g: (g, 0, 0)),
        out_shape=jax.ShapeDtypeStruct((heads, count, WIN), F32),
    )


def cross_forward_kernel(q_ref, k0_ref, v0_ref, k1_ref, v1_ref, out_ref, exact_ref, total_ref):
    rows = q_ref.shape[0]
    for h in range(2):
        lanes = slice(h * DH, (h + 1) * DH)
        keys = [k0_ref[:, lanes], k1_ref[:, lanes]]
        values = [v0_ref[:, lanes], v1_ref[:, lanes]]
        values = [jnp.concatenate([v, jnp.ones_like(v)], axis=1) for v in values]
        for first in range(0, rows, WIN):
            tile = slice(first, first + WIN)
            scores = [nt(q_ref[tile, lanes], k) for k in keys]
            top = jnp.maximum(*[jnp.max(part, axis=1, keepdims=True) for part in scores])
            both = 0.0
            for part, v in zip(scores, values):
                both = both + nn(jnp.exp(part - top).astype(BF), v)
            row_sum = both[:, DH:]
            context = both[:, :DH] / row_sum
            out_ref[tile, lanes] = context.astype(BF)
            exact_ref[tile, lanes] = context
            log_total = top + jnp.log(jnp.concatenate([row_sum, row_sum], axis=1))
            total_ref[h : h + 1, tile] = jnp.transpose(log_total)[:1]


def cross_forward(queries, own, other, earlier=()):
    rows, width = queries.shape
    keys, pairs = own.shape[0], width // 128
    tile = pl.BlockSpec((rows, 128), lambda g: (0, g))
    left = pl.BlockSpec((keys, 128), lambda g: (0, g))
    right = pl.BlockSpec((keys, 128), lambda g: (0, pairs + g))
    return run(
        "cross_forward",
        cross_forward_kernel,
        [queries, own, own, other, other],
        [tile, left, right, left, right],
        earlier,
        26,
        grid=(pairs,),
        out_specs=[tile, tile, pl.BlockSpec((None, 8, rows), lambda g: (g, 0, 0))],
        out_shape=[
            jax.ShapeDtypeStruct((rows, width), BF),
            jax.ShapeDtypeStruct((rows, width), F32),
            jax.ShapeDtypeStruct((pairs, 8, rows), F32),
        ],
        compiler_params=pltpu.CompilerParams(vmem_limit_bytes=48 * MIB),
    )


def cross_backward_kernel(
    q_ref, g_ref, exact_ref, total_ref, k0_ref, v0_ref, k1_ref, v1_ref,
    gq_ref, gk0_ref, gv0_ref, gk1_ref, gv1_ref, inner_ref, sum_ref,
):
    step, steps = pl.program_id(1), pl.num_programs(1)
    rows = q_ref.shape[0]

    @pl.when(step == 0)
    def _():
        sum_ref[...] = jnp.zeros_like(sum_ref)
        for first in range(0, rows, WIN):
            tile = slice(first, first + WIN)
            product = jnp.transpose(g_ref[tile, :].astype(F32) * exact_ref[tile, :])
            for h in range(2):
                inner_ref[h : h + 1, tile] = jnp.sum(
                    product[h * DH : (h + 1) * DH], axis=0, keepdims=True
                )

    for k_ref, v_ref, gk_ref, gv_ref in (
        (k0_ref, v0_ref, gk0_ref, gv0_ref),
        (k1_ref, v1_ref, gk1_ref, gv1_ref),
    ):
        for h in range(2):
            lanes = slice(h * DH, (h + 1) * DH)
            k, v = k_ref[:, lanes], v_ref[:, lanes]
            k_across = jnp.transpose(k)
            key_grad = jnp.zeros(k.shape, F32)
            value_grad = jnp.zeros(k.shape, F32)
            for first in range(0, rows, WIN):
                tile = slice(first, first + WIN)
                q, g = q_ref[tile, lanes], g_ref[tile, lanes]
                prob = jnp.exp(nt(k, q) - total_ref[h : h + 1, tile])
                prob_grad = nt(v, g)
                score_grad = (prob * (prob_grad - inner_ref[h : h + 1, tile])).astype(BF)
                value_grad += nn(prob.astype(BF), g)
                key_grad += nn(score_grad, q)
                sum_ref[lanes, tile] += nn(k_across, score_grad)
            gk_ref[:, lanes] = key_grad.astype(gk_ref.dtype)
            gv_ref[:, lanes] = value_grad.astype(gv_ref.dtype)

    @pl.when(step == steps - 1)
    def _():
        for first in range(0, rows, WIN):
            tile = slice(first, first + WIN)
            gq_ref[tile, :] = jnp.transpose(sum_ref[:, tile]).astype(BF)


def cross_backward(queries, grads, exact, total, own, other, earlier=()):
    rows, width = queries.shape
    keys, pairs = own.shape[0], width // 128
    parts = 4
    tile = pl.BlockSpec((rows, 128), lambda g, j: (0, g))
    left = pl.BlockSpec((keys // parts, 128), lambda g, j: (j, g))
    right = pl.BlockSpec((keys // parts, 128), lambda g, j: (j, pairs + g))
    shape = (keys, width)
    return run(
        "cross_backward",
        cross_backward_kernel,
        [queries, grads, exact, total, own, own, other, other],
        [tile, tile, tile, pl.BlockSpec((None, 8, rows), lambda g, j: (g, 0, 0))]
        + [left, right, left, right],
        earlier,
        62,
        grid=(pairs, parts),
        out_specs=[tile, left, left, left, left],
        out_shape=[
            jax.ShapeDtypeStruct(queries.shape, BF),
            jax.ShapeDtypeStruct(shape, F32),
            jax.ShapeDtypeStruct(shape, F32),
            jax.ShapeDtypeStruct(shape, BF),
            jax.ShapeDtypeStruct(shape, BF),
        ],
        scratch_shapes=[pltpu.VMEM((8, rows), F32), pltpu.VMEM((128, rows), F32)],
        compiler_params=pltpu.CompilerParams(vmem_limit_bytes=48 * MIB),
    )


def sum_keys_kernel(k0_ref, v0_ref, k1_ref, v1_ref, out_ref):
    width = k0_ref.shape[1]
    out_ref[:, :width] = (k0_ref[...] + k1_ref[...].astype(F32)).astype(BF)
    out_ref[:, width:] = (v0_ref[...] + v1_ref[...].astype(F32)).astype(BF)


def sum_keys(own, received, earlier=()):
    rows, width = own[0].shape
    tile = rows // 4
    block = pl.BlockSpec((tile, width), lambda i: (i, 0))
    return run(
        "sum_keys",
        sum_keys_kernel,
        [*own, *received],
        [block] * 4,
        earlier,
        6,
        grid=(4,),
        out_specs=pl.BlockSpec((tile, 2 * width), lambda i: (i, 0)),
        out_shape=jax.ShapeDtypeStruct((rows, 2 * width), BF),
    )


def norm_scale(stream):
    return lax.rsqrt(jnp.mean(stream * stream, axis=-1, keepdims=True) + EPSILON)


def norm_back(stream, scale, gain, incoming):
    scaled = incoming * gain
    along = jnp.mean(scaled * stream, axis=-1, keepdims=True)
    return (
        scale * scaled - stream * (scale * scale * scale) * along,
        jnp.sum(incoming * stream * scale, axis=0, keepdims=True),
    )


def gate_and_slope(u):
    inner = 0.7978845608028654 * (u + 0.044715 * u * u * u)
    bent = jnp.tanh(inner)
    half = 0.5 * (1.0 + bent)
    slope = half + 0.5 * u * (1.0 - bent * bent) * 0.7978845608028654 * (1.0 + 0.134145 * u * u)
    return u * half, slope


def local(
    hidden, passages, block_ids, buckets, norm_gains, self_query, self_key, self_value, self_out,
    cross_query, cross_key, cross_value, cross_out, ffn_in, ffn_out, rel_bias, out_grad,
):
    ranks = lax.axis_size("tensor")
    rank = lax.axis_index("tensor")
    batches, rows, model = hidden.shape
    head_width = self_query.shape[1]
    width = head_width * ranks

    hw, ffn = head_width, ffn_in.shape[1]
    self_layout = [(k * hw, hw, k * width, hw) for k in range(5)]
    kv_layout = [(0, hw, 0, hw), (hw, hw, width, hw)]
    late_layout = [(0, ffn, 0, ffn), (ffn, ffn, ranks * ffn, ffn), (2 * ffn, hw, 2 * ranks * ffn, hw)]
    gains = gather_small(jnp.transpose(norm_gains))
    gains = jnp.transpose(gains, (1, 0, 2)).reshape(3, model).astype(F32)
    self_blocks = gather_ranks([self_query, self_key, self_value, self_out, cross_query])
    kv_blocks = gather_ranks([cross_key, cross_value])
    ids = gathered(
        lax.dynamic_slice_in_dim(block_ids, rank * rows, rows, 1).reshape(batches, -1, WIN)
    )
    stream_low = gathered(hidden)
    encoded = gathered(passages)
    bias = window_bias(rel_bias, buckets, [gains, *self_blocks, *kv_blocks])
    self_pieces = gather_cores(gather_far(gather_paths(jnp.stack(self_blocks))))
    qkv_weight, so_weight, cq_weight = gather_end(
        self_pieces,
        [self_layout[:3], [(3 * hw, hw, 0, hw)], [(4 * hw, hw, 0, hw)]],
        [bias, stream_low],
    )
    late_blocks = gather_ranks([ffn_in, ffn_out, cross_out], self_blocks + kv_blocks)
    late_paths = gather_paths(jnp.stack(late_blocks))
    kv_pieces = gather_cores(gather_far(gather_paths(jnp.stack(kv_blocks))))
    (kv_weight,) = gather_end(kv_pieces, [kv_layout], [qkv_weight])

    stream = stream_low.astype(F32)
    scale_one = norm_scale(stream)
    normed_one = (stream * scale_one * gains[0]).astype(BF)
    qkv = nn(normed_one, qkv_weight).astype(BF)
    context = self_forward(qkv, ids, bias, [kv_weight])
    after_self = stream + nt(context, so_weight)
    scale_two = norm_scale(after_self)
    normed_two = (after_self * scale_two * gains[1]).astype(BF)
    queries = nn(normed_two, cq_weight).astype(BF)

    own_kv = nn(encoded, kv_weight).astype(BF)
    other_kv = flip(own_kv, "fsdp", 1)
    late_far = gather_far(late_paths)
    cross_context, exact, total = cross_forward(queries, own_kv, other_kv, late_paths[1:])
    late_pieces = gather_cores(late_far)
    in_weight, out_weight, co_weight = gather_end(
        late_pieces,
        [[(0, ffn, 0, ffn)], [(ffn, ffn, 0, ffn)], [(2 * ffn, hw, 0, hw)]],
        [cross_context],
    )

    incoming = gathered(out_grad)
    after_cross = after_self + nt(cross_context, co_weight)
    scale_three = norm_scale(after_cross)
    normed_three = (after_cross * scale_three * gains[2]).astype(BF)
    gate, slope = gate_and_slope(nn(normed_three, in_weight))
    activated = gate.astype(BF)
    output = (after_cross + nt(activated, out_weight)).astype(BF)
    pre_grad = (nn(incoming, out_weight) * slope).astype(BF)
    normed_grad = nt(pre_grad, in_weight)
    stream_part, gain_three = norm_back(after_cross, scale_three, gains[2], normed_grad)
    grad_two = incoming.astype(F32) + stream_part
    branch_two = grad_two.astype(BF)
    context_grad = nn(branch_two, co_weight).astype(BF)
    late_grads = weight_grads(
        [normed_three, incoming, branch_two],
        [((0,), [pre_grad]), ((1,), [activated]), ((2,), [cross_context])],
        [context_grad],
    )
    late_stage = scatter_cores(late_grads)

    query_grad, key_own, value_own, key_other, value_other = cross_backward(
        queries, context_grad, exact, total, own_kv, other_kv, [late_grads[0], output]
    )
    output = returned(output)
    kv_received = [flip(x, "fsdp", 1) for x in (key_other, value_other)]
    late_stage = scatter_paths(late_stage, [query_grad])
    normed_grad = nt(query_grad, cq_weight)
    stream_part, gain_two = norm_back(after_self, scale_two, gains[1], normed_grad)
    grad_one = grad_two + stream_part
    branch_one = grad_one.astype(BF)
    context_grad = nn(branch_one, so_weight).astype(BF)
    kv_grad = sum_keys([key_own, value_own], kv_received, [late_stage[0]])
    encoded_grad = rows_back(kv_grad, kv_weight)
    encoded_grads = returned(encoded_grad)

    gq, gk, gv, sums = self_backward(qkv, context_grad, ids, bias, [encoded_grad, *late_stage[1:]])
    late_stage = scatter_far(late_stage, [gq])
    self_grads = weight_grads(
        [normed_one, branch_one, normed_two],
        [((0,), [gq]), ((0,), [gk]), ((0,), [gv]), ((1,), [context]), ((2,), [query_grad])],
        late_stage[:1],
    )
    self_stage = scatter_cores(self_grads)
    kv_sums = weight_grads([encoded], [((0,), [kv_grad])], [self_grads[0]])
    kv_stage = scatter_cores(kv_sums)
    late_blocks = scatter_end(late_stage, late_layout, [kv_sums[0]])
    self_stage = scatter_paths(self_stage, [late_blocks])
    kv_stage = scatter_paths(kv_stage, [self_stage[0]])
    late_total = scatter_tensor(late_blocks)
    in_total, out_total, co_total = late_total[:, :ffn], late_total[:, ffn : 2 * ffn], late_total[:, 2 * ffn :]
    normed_grad = sum(nt(x, qkv_weight[:, k * width : (k + 1) * width]) for k, x in enumerate((gq, gk, gv)))
    stream_part, gain_one = norm_back(stream, scale_one, gains[0], normed_grad)
    input_grads = returned((grad_one + stream_part).astype(BF))
    bias_lanes = bucket_sums(sums, buckets, rel_bias.shape[0], [kv_stage[0]])
    self_stage = scatter_far(self_stage, [bias_lanes])
    kv_stage = scatter_far(kv_stage, [self_stage[0]])
    self_total = scatter_tensor(scatter_end(self_stage, self_layout, [kv_stage[0]]))
    q_total, k_total, v_total, so_total, cq_total = column_blocks(self_total, 5)
    kv_total = scatter_tensor(scatter_end(kv_stage, kv_layout, [kv_stage[0]]))

    bias_own = jnp.transpose(jnp.sum(bias_lanes, axis=2))
    small = jnp.concatenate(
        [gain_one.reshape(-1), gain_two.reshape(-1), gain_three.reshape(-1), bias_own.reshape(-1)]
    )
    pad = -small.shape[0] % 1024
    small = jnp.pad(small, (0, pad)).reshape(8, -1)
    small = sum_everywhere(small).reshape(-1)
    gains_sum = jnp.transpose(small[: 3 * model].reshape(3, model))
    bias_total = small[3 * model : 3 * model + rel_bias.size].reshape(rel_bias.shape)

    return (
        by_batch(output, BF),
        by_batch(input_grads, F32),
        by_batch(encoded_grads, F32),
        gains_sum,
        q_total,
        k_total,
        v_total,
        so_total,
        cq_total,
        kv_total[:, :head_width],
        kv_total[:, head_width:],
        co_total,
        in_total,
        out_total,
        bias_total,
    )


def solution(mesh):
    rows = P(None, ("fsdp", "tensor"), None)
    weight = P("fsdp", "tensor")
    in_specs = (rows, rows, P(None, "fsdp"), P(), P("fsdp", None)) + (weight,) * 10 + (P(), rows)
    out_specs = (rows, rows, rows, P()) + (weight,) * 10 + (P(),)
    return jax.shard_map(local, mesh=mesh, in_specs=in_specs, out_specs=out_specs, check_vma=False)
```

time: 742 us -> 548 us (0.74)
  waiting for transfers between devices: 176 us -> 73.9 us
  Pallas kernels: 176 us -> 232 us
  starting transfers between devices: 184 us -> 128 us
  matrix products: 90.7 us -> 38.5 us
  local copies, waits for them, and re-layouts: 70.5 us -> 38.3 us
    ppermute x63 -> x9, starting transfers between devices: 139 us -> 45.2 us  [shift(): return lax.ppermute(x, axis, [(i, (i + by) % size) for i in range(size)])]
    ppermute x63 -> x9, waiting for transfers between devices: 106 us -> 28.5 us  [shift(): return lax.ppermute(x, axis, [(i, (i + by) % size) for i in range(size)])]
    pallas_call x14 -> x26, Pallas kernels: 176 us -> 232 us  [run(): pl.pallas_call(body, in_specs=[pl.BlockSpec(memory_space=pl.ANY)] * count...]
    ppermute x27 -> x15, waiting for transfers between devices: 68.3 us -> 19.5 us  [two_way(): lax.ppermute(x, 'fsdp', [(i, i ^ (second if i & 1 else first)) for i in r...]
    ppermute x0 -> x14, starting transfers between devices: none -> 31.7 us  [the longest x6 20 us: returned(): lax.ppermute(x[r * half:(r + 1) * half], ('fsdp', 'tensor'), round_moves(...]
    dot_general x7 -> x0, matrix products: 24.4 us -> none  [tn(): lax.dot_general(left, right, (((0,), (0,)), ((), ())), preferred_element_...]
    dot_general x10 -> x8, matrix products: 32.1 us -> 14.1 us  [nt(): lax.dot_general(left, right, (((1,), (1,)), ((), ())), preferred_element_...]
    ppermute x27 -> x15, starting transfers between devices: 32.1 us -> 17.1 us  [two_way(): lax.ppermute(x, 'fsdp', [(i, i ^ (second if i & 1 else first)) for i in r...]
  transfers between devices with their start and end apart: 119 -> 69, of which waited for: 38 -> 12; matrix products, arithmetic and copies ran while one was open for 20% -> 12% of each run, Pallas kernels for 23% -> 41%
where the time goes in v2:
time: 548 us; the launch traced here: 540 us
  Pallas kernels  232 us (42%)
  starting transfers between devices  128 us (23%)
  waiting for transfers between devices  73.9 us (13%)
  matrix products  38.5 us (7%)
  local copies, waits for them, and re-layouts  38.3 us (7%)
  other arithmetic  26.4 us (5%)
    pallas_call x26, Pallas kernels, run(): pl.pallas_call(body, in_specs=[pl.BlockSpec(memory_space=pl.ANY)] * count...  232 us
    ppermute x9, starting transfers between devices, shift(): return lax.ppermute(x, axis, [(i, (i + by) % size) for i in range(size)])  45.2 us
    ppermute x9, waiting for transfers between devices, shift(): return lax.ppermute(x, axis, [(i, (i + by) % size) for i in range(size)])  28.5 us
    dot_general x7, matrix products, nn(): return jnp.dot(left, right, preferred_element_type=F32)  24.4 us
    ppermute x6, starting transfers between devices, returned(): lax.ppermute(x[r * half:(r + 1) * half], ('fsdp', 'tensor'), round_moves(...  20 us
    unnamed x163, local copies, waits for them, and re-layouts  19.9 us
    ppermute x28, starting transfers between devices, flip(): return lax.ppermute(x, axis, [(i, i ^ bits) for i in range(size)])  19.7 us
    ppermute x15, waiting for transfers between devices, two_way(): lax.ppermute(x, 'fsdp', [(i, i ^ (second if i & 1 else first)) for i in r...  19.5 us
  transfers between devices with their start and end apart: 69, of which 12 were waited for; matrix products, arithmetic and copies ran while one was open for 12% of the time, Pallas kernels for 41%

profile of v2, /device:TPU:0, one launch (start us, length us, event | category | flops | bytes accessed | tf_op | source)
XLA Modules:
  0.0 539.8 jit_solution(11712121813482730417)
XLA Ops:
  19.0 13.6 %collective-permute-done.6.refs_3_.refs_2_ = bf16[96,960]{1,0:T(8,128)(2,1)S(1)} collective-permute-done((bf16[96,960]{1,0:T(8,128)(2,1)}, bf16[96,960]{1,0:T(8,128)(2,1)S(1)}, u32[]{:S(2)}, u32[]{:S(2)}) %collective-permute-start.6) | collective-permute-done | bytes 184352 | tf_op jit(solution)/shard_map/ppermute | solution.py:35
  64.4 6.4 %collective-permute-done.29 = bf16[96,1728]{1,0:T(8,128)(2,1)} collective-permute-done((bf16[96,1728]{1,0:T(8,128)(2,1)}, bf16[96,1728]{1,0:T(8,128)(2,1)}, u32[]{:S(2)}, u32[]{:S(2)}) %collective-permute-start.29) | collective-permute-done | bytes 331808 | tf_op jit(solution)/shard_map/ppermute | solution.py:35
  70.7 27.7 %collective-permute-start.27 = (bf16[96,1728]{1,0:T(8,128)(2,1)}, bf16[96,1728]{1,0:T(8,128)(2,1)S(1)}, u32[]{:S(2)}, u32[]{:S(2)}) collective-permute-start(bf16[96,1728]{1,0:T(8,128)(2,1)} %join.5), channel_id=1, source_target_pairs={{0,1},{1,2},{2,3},{3,0},{4,5},{5,6},{6,7},{7,4},{8,9},{9,10},{10,1... | collective-permute-start | bytes 995336 | tf_op jit(solution)/shard_map/ppermute | solution.py:35
  98.4 7.7 %collective-permute-done.28 = bf16[96,1728]{1,0:T(8,128)(2,1)} collective-permute-done((bf16[96,1728]{1,0:T(8,128)(2,1)}, bf16[96,1728]{1,0:T(8,128)(2,1)}, u32[]{:S(2)}, u32[]{:S(2)}) %collective-permute-start.28) | collective-permute-done | bytes 331808 | tf_op jit(solution)/shard_map/ppermute | solution.py:35
  108.1 9.0 %window_bias.1.refs_0_.refs_6_.refs_8_ = f32[12,256,256]{2,1,0:T(8,128)} custom-call(f32[3,768]{1,0:T(4,128)} %convert_element_type.75.refs_0_, bf16[96,960]{1,0:T(8,128)(2,1)} %join.3.refs_1_.refs_0_, bf16[96,960]{1,0:T(8,128)(2,1)} %copy-done.44, bf16[96,960]{1,0:T(8,128)(2,1)} %copy-done.43, bf16[96,960]{1,0:T(8,128)(2,1)} %copy-done.42, ...), custom_call_target="tpu_custom_call" | custom-call | flops 9900000256 | bytes 31500000 | tf_op jit(solution)/shard_map/window_bias/pallas_call | solution.py:135
  118.2 9.2 %collective-permute-done.33 = bf16[640,768]{1,0:T(8,128)(2,1)} collective-permute-done((bf16[640,768]{1,0:T(8,128)(2,1)}, bf16[640,768]{1,0:T(8,128)(2,1)}, u32[]{:S(2)}, u32[]{:S(2)}) %collective-permute-start.33) | collective-permute-done | bytes 983072 | tf_op jit(solution)/shard_map/ppermute | solution.py:413
  141.1 6.0 %assemble.3 = (bf16[768,2304]{1,0:T(8,128)(2,1)}, bf16[768,768]{1,0:T(8,128)(2,1)}, bf16[768,768]{1,0:T(8,128)(2,1)}) custom-call(f32[12,256,256]{2,1,0:T(8,128)} %window_bias.1.refs_0_.refs_6_.refs_8_, bf16[512,768]{1,0:T(8,128)(2,1)S(1)} %constant_dynamic-update-slice_fusion.refs_1_, bf16[4,96,960]{2,1,0:T(8,128)(2,1)S(1)} %pad_maximum_fusion.1.refs_2_, ...), custom_call_target="tpu_custom_call" | custom-call | flops 5324000256 | bytes 16940000 | tf_op jit(solution)/shard_map/assemble/pallas_call | solution.py:135
  169.3 16.3 %collective-permute-done.30.refs_0_.refs_2_ = bf16[4,96,1728]{2,1,0:T(8,128)(2,1)} collective-permute-done((bf16[4,96,1728]{2,1,0:T(8,128)(2,1)S(1)}, bf16[4,96,1728]{2,1,0:T(8,128)(2,1)}, u32[]{:S(2)}, u32[]{:S(2)}) %collective-permute-start.30) | collective-permute-done | bytes 1327136 | tf_op jit(solution)/shard_map/ppermute | solution.py:45
  193.6 12.2 %self_forward.1.refs_7_ = bf16[512,768]{1,0:T(8,128)(2,1)} custom-call(bf16[768,1536]{1,0:T(8,128)(2,1)} %copy-done.18, bf16[512,2304]{1,0:T(8,128)(2,1)} %convolution_convert_fusion.1.refs_1_.refs_2_.refs_3_.refs_4_, bf16[512,2304]{1,0:T(8,128)(2,1)} %convolution_convert_fusion.1.refs_1_.refs_2_.refs_3_.refs_4_, ...), custom_call_target="tpu_custom_call" | custom-call | flops 13200000000 | bytes 42000000 | tf_op jit(solution)/shard_map/self_forward/pallas_call | solution.py:135
  210.9 26.3 %cross_forward.1 = (bf16[512,768]{1,0:T(8,128)(2,1)S(1)}, f32[512,768]{1,0:T(8,128)S(1)}, f32[6,8,512]{2,1,0:T(8,128)S(1)}) custom-call(bf16[4,96,1728]{2,1,0:T(8,128)(2,1)} %collective-permute-done.30.refs_0_.refs_2_, bf16[4,96,1728]{2,1,0:T(8,128)(2,1)} %collective-permute-done.31.refs_1_.refs_3_, bf16[512,768]{1,0:T(8,128)(2,1)S(1)} %convolution_convert_fusion.4.refs_2_, ...), custom_call_target="tpu_custom_call" | custom-call | flops 28600000512 | bytes 91000000 | tf_op jit(solution)/shard_map/cross_forward/pallas_call | solution.py:135
  238.3 7.9 %assemble.5 = (bf16[768,3072]{1,0:T(8,128)(2,1)}, bf16[768,3072]{1,0:T(8,128)(2,1)}, bf16[768,768]{1,0:T(8,128)(2,1)S(1)}) custom-call(bf16[512,768]{1,0:T(8,128)(2,1)S(1)} %get-tuple-element.54.refs_0_.refs_6_, bf16[4,96,1728]{2,1,0:T(8,128)(2,1)S(1)} %pad_maximum_fusion.refs_1_, bf16[4,96,1728]{2,1,0:T(8,128)(2,1)} %collective-permute-done.30.refs_0_.refs_2_, ...), custom_call_target="tpu_custom_call" | custom-call | flops 8703200256 | bytes 27692000 | tf_op jit(solution)/shard_map/assemble/pallas_call | solution.py:135
  257.0 7.3 %fusion.6.refs_4_ = bf16[512,3072]{1,0:T(8,128)(2,1)S(1)} fusion(f32[512,3072]{1,0:T(8,128)} %get-tuple-element.172, bf16[512,768]{1,0:T(8,128)(2,1)S(1)} %constant_dynamic-update-slice_fusion.4.refs_2_, bf16[768,3072]{1,0:T(8,128)(2,1)S(1)} %bitcast.92), kind=kOutput, calls=%fused_computation.10 | convolution fusion | flops 2445803520 | bytes 14942208 | tf_op jit(solution)/shard_map/dot_general | solution.py:20
  271.2 13.5 %weight_grads.3 = (bf16[384,6912]{1,0:T(8,128)(2,1)}, bf16[384,6912]{1,0:T(8,128)(2,1)}) custom-call(bf16[512,768]{1,0:T(8,128)(2,1)S(1)} %convolution_convert_fusion.3.refs_0_.refs_3_, bf16[512,768]{1,0:T(8,128)(2,1)S(1)} %multiply_convert_fusion.1.refs_1_, bf16[512,768]{1,0:T(8,128)(2,1)S(1)} %constant_dynamic-update-slice_fusion.4.refs_2_, ...), custom_call_target="tpu_custom_call" | custom-call | flops 13859999744 | bytes 44100000 | tf_op jit(solution)/shard_map/weight_grads/pallas_call | solution.py:135
  286.3 65.5 %cross_backward.1 = (bf16[512,768]{1,0:T(8,128)(2,1)S(1)}, f32[1280,768]{1,0:T(8,128)}, f32[1280,768]{1,0:T(8,128)}, bf16[1280,768]{1,0:T(8,128)(2,1)}, bf16[1280,768]{1,0:T(8,128)(2,1)}) custom-call(bf16[384,6912]{1,0:T(8,128)(2,1)} %get-tuple-element.58.refs_0_.refs_1_, bf16[512,768]{1,0:T(8,128)(2,1)S(1)} %add_convert_fusion.refs_1_, ...), custom_call_target="tpu_custom_call" | custom-call | flops 68200001536 | bytes 217000000 | tf_op jit(solution)/shard_map/cross_backward/pallas_call | solution.py:135
  353.8 7.4 %sum_cores.3 = (bf16[192,6912]{1,0:T(8,128)(2,1)S(1)}, bf16[192,6912]{1,0:T(8,128)(2,1)S(1)}) custom-call(bf16[512,768]{1,0:T(8,128)(2,1)S(1)} %get-tuple-element.61.refs_0_.refs_8_, bf16[384,6912]{1,0:T(8,128)(2,1)} %get-tuple-element.58.refs_0_.refs_1_, bf16[384,6912]{1,0:T(8,128)(2,1)} %collective-permute-done.44.refs_2_), custom_call_target="tpu_custom_call" | custom-call | flops 9732096000 | bytes 30965760 | tf_op jit(solution)/shard_map/sum_cores/pallas_call | solution.py:135
  366.4 6.5 %sum_keys.1.refs_0_.refs_2_ = bf16[1280,1536]{1,0:T(8,128)(2,1)} custom-call(bf16[192,6912]{1,0:T(8,128)(2,1)} %copy-done.28, f32[1280,768]{1,0:T(8,128)} %get-tuple-element.64.refs_1_, f32[1280,768]{1,0:T(8,128)} %get-tuple-element.65.refs_2_, bf16[1280,768]{1,0:T(8,128)(2,1)} %collective-permute-done.45.refs_3_, ...), custom_call_target="tpu_custom_call" | custom-call | flops 6600000000 | bytes 21000000 | tf_op jit(solution)/shard_map/sum_keys/pallas_call | solution.py:135
  374.6 5.9 %rows_back.1.refs_0_ = bf16[1280,768]{1,0:T(8,128)(2,1)S(1)} custom-call(bf16[1280,1536]{1,0:T(8,128)(2,1)} %sum_keys.1.refs_0_.refs_2_, bf16[768,1536]{1,0:T(8,128)(2,1)S(1)} %copy-done.19), custom_call_target="tpu_custom_call" | custom-call | flops 6600000000 | bytes 21000000 | tf_op jit(solution)/shard_map/rows_back/pallas_call | solution.py:135
  385.0 8.9 %collective-permute-start.50 = (bf16[640,768]{1,0:T(8,128)(2,1)}, bf16[640,768]{1,0:T(8,128)(2,1)}, u32[]{:S(2)}, u32[]{:S(2)}) collective-permute-start(bf16[640,768]{1,0:T(8,128)(2,1)} %get-tuple-element.133), channel_id=1, source_target_pairs={{0,0},{4,1},{2,2},{6,3},{1,4},{5,5},{3,6},{7,7},{8,8},{12,9},{10,1... | collective-permute-start | bytes 2949128 | tf_op jit(solution)/shard_map/ppermute | solution.py:426
  394.0 18.0 %self_backward.1 = (bf16[512,768]{1,0:T(8,128)(2,1)}, bf16[512,768]{1,0:T(8,128)(2,1)}, bf16[512,768]{1,0:T(8,128)(2,1)}, f32[12,256,256]{2,1,0:T(8,128)}) custom-call(bf16[1280,768]{1,0:T(8,128)(2,1)} %copy-done.2, bf16[192,6912]{1,0:T(8,128)(2,1)} %collective-permute-done.47.refs_1_.refs_2_, ...), custom_call_target="tpu_custom_call" | custom-call | flops 19800000512 | bytes 63000000 | tf_op jit(solution)/shard_map/self_backward/pallas_call | solution.py:135
  413.1 6.2 %sum_paths.3 = (f32[96,6912]{1,0:T(8,128)S(1)}, bf16[96,6912]{1,0:T(8,128)(2,1)S(1)}) custom-call(bf16[512,768]{1,0:T(8,128)(2,1)S(1)} %copy-done.13, bf16[192,6912]{1,0:T(8,128)(2,1)} %copy-done.28, bf16[192,6912]{1,0:T(8,128)(2,1)} %collective-permute-done.47.refs_1_.refs_2_), custom_call_target="tpu_custom_call" | custom-call | flops 4866048000 | bytes 15482880 | tf_op jit(solution)/shard_map/sum_paths/pallas_call | solution.py:135
  420.8 7.8 %weight_grads.4 = (bf16[384,3840]{1,0:T(8,128)(2,1)}, bf16[384,3840]{1,0:T(8,128)(2,1)}) custom-call(f32[96,6912]{1,0:T(8,128)} %copy-done.15, bf16[512,768]{1,0:T(8,128)(2,1)S(1)} %copy-done.4, bf16[512,768]{1,0:T(8,128)(2,1)S(1)} %get-tuple-element.126.refs_2_, bf16[512,768]{1,0:T(8,128)(2,1)S(1)} %copy-done.6, bf16[512,768]{1,0:T(8,128)(2,1)S(1)} %copy-done.13, ...), custom_call_target="tpu_custom_call" | custom-call | flops 7699999744 | bytes 24500000 | tf_op jit(solution)/shard_map/weight_grads/pallas_call | solution.py:135
  437.0 6.8 %weight_grads.5 = (bf16[384,1536]{1,0:T(8,128)(2,1)S(1)}, bf16[384,1536]{1,0:T(8,128)(2,1)}) custom-call(bf16[384,3840]{1,0:T(8,128)(2,1)} %get-tuple-element.73.refs_0_.refs_1_, bf16[1280,768]{1,0:T(8,128)(2,1)S(1)} %copy-done.9, bf16[1280,1536]{1,0:T(8,128)(2,1)} %sum_keys.1.refs_0_.refs_2_), custom_call_target="tpu_custom_call" | custom-call | flops 3080000000 | bytes 9800000 | tf_op jit(solution)/shard_map/weight_grads/pallas_call | solution.py:135
  471.4 13.6 %bucket_sums.1.refs_0_ = f32[12,32,256]{2,1,0:T(8,128)} custom-call(bf16[192,1536]{1,0:T(8,128)(2,1)} %copy-done.24, f32[12,256,256]{2,1,0:T(8,128)} %get-tuple-element.80.refs_1_, s32[256,256]{1,0:T(8,128)} %refs_2_.3), custom_call_target="tpu_custom_call" | custom-call | flops 14300000256 | bytes 45500000 | tf_op jit(solution)/shard_map/bucket_sums/pallas_call | solution.py:135
  527.5 10.8 %all-to-all-done = bf16[4,96,960]{2,1,0:T(8,128)(2,1)S(1)} async-done(((bf16[4,96,960]{2,1,0:T(8,128)(2,1)}), bf16[4,96,960]{2,1,0:T(8,128)(2,1)S(1)}, u32[]{:S(2)}, u32[]{:S(2)}) %all-to-all-start) | async-done | bytes 737312 | tf_op jit(solution)/shard_map/all_to_all | solution.py:390
  (386 shorter events, 217.2 us)
Async XLA Ops:
  7.4 25.2 %collective-permute-start.5 = (bf16[96,960]{1,0:T(8,128)(2,1)}, bf16[96,960]{1,0:T(8,128)(2,1)S(1)}, u32[]{:S(2)}, u32[]{:S(2)}) collective-permute-start(bf16[96,960]{1,0:T(8,128)(2,1)} %join.3.refs_1_.refs_0_), channel_id=1, source_target_pairs={{0,1},{1,2},{2,3},{3,0},{4,5},{5,6},{6,7},{7,4},{8,9},{9,10},{10,1... | collective-permute-start | bytes 552968 | tf_op jit(solution)/shard_map/ppermute | solution.py:35
  32.6 26.7 %collective-permute-start.1 = (bf16[256,768]{1,0:T(8,128)(2,1)}, bf16[256,768]{1,0:T(8,128)(2,1)S(1)}, u32[]{:S(2)}, u32[]{:S(2)}) collective-permute-start(bf16[256,768]{1,0:T(8,128)(2,1)} %get-tuple-element.146), channel_id=1, source_target_pairs={{0,2},{1,6},{2,0},{3,4},{4,3},{5,7},{6,1},{7,5},{8,10},{9,14},{10,... | collective-permute-start | bytes 1179656 | tf_op jit(solution)/shard_map/ppermute | solution.py:413
  34.3 73.3 %collective-permute-start.11 = (bf16[4,96,960]{2,1,0:T(8,128)(2,1)S(1)}, bf16[4,96,960]{2,1,0:T(8,128)(2,1)}, u32[]{:S(2)}, u32[]{:S(2)}) collective-permute-start(bf16[4,96,960]{2,1,0:T(8,128)(2,1)S(1)} %pad_maximum_fusion.1.refs_2_), channel_id=1, source_target_pairs={{0,8},{4,20},{8,0},{12,28},{16,24},{20,4},{24,16},{28,12},{1,9},{5... | collective-permute-start | bytes 2211848 | tf_op jit(solution)/shard_map/ppermute | solution.py:45
  55.0 51.1 %collective-permute-start.28 = (bf16[96,1728]{1,0:T(8,128)(2,1)}, bf16[96,1728]{1,0:T(8,128)(2,1)}, u32[]{:S(2)}, u32[]{:S(2)}) collective-permute-start(bf16[96,1728]{1,0:T(8,128)(2,1)} %join.5), channel_id=1, source_target_pairs={{0,2},{1,3},{2,0},{3,1},{4,6},{5,7},{6,4},{7,5},{8,10},{9,11},{10,... | collective-permute-start | bytes 995336 | tf_op jit(solution)/shard_map/ppermute | solution.py:35
  59.3 68.1 %collective-permute-start.33 = (bf16[640,768]{1,0:T(8,128)(2,1)}, bf16[640,768]{1,0:T(8,128)(2,1)}, u32[]{:S(2)}, u32[]{:S(2)}) collective-permute-start(bf16[640,768]{1,0:T(8,128)(2,1)} %get-tuple-element.134), channel_id=1, source_target_pairs={{0,2},{1,6},{2,0},{3,4},{4,3},{5,7},{6,1},{7,5},{8,10},{9,14},{10,... | collective-permute-start | bytes 2949128 | tf_op jit(solution)/shard_map/ppermute | solution.py:413
  62.7 66.3 %collective-permute-start.32 = (bf16[640,768]{1,0:T(8,128)(2,1)S(1)}, bf16[640,768]{1,0:T(8,128)(2,1)}, u32[]{:S(2)}, u32[]{:S(2)}) collective-permute-start(bf16[640,768]{1,0:T(8,128)(2,1)S(1)} %get-tuple-element.135), channel_id=1, source_target_pairs={{0,0},{1,4},{2,2},{3,6},{4,1},{5,5},{6,3},{7,7},{8,8},{9,12},{10,1... | collective-permute-start | bytes 2949128 | tf_op jit(solution)/shard_map/ppermute | solution.py:413
  70.7 46.4 %collective-permute-start.27 = (bf16[96,1728]{1,0:T(8,128)(2,1)}, bf16[96,1728]{1,0:T(8,128)(2,1)S(1)}, u32[]{:S(2)}, u32[]{:S(2)}) collective-permute-start(bf16[96,1728]{1,0:T(8,128)(2,1)} %join.5), channel_id=1, source_target_pairs={{0,1},{1,2},{2,3},{3,0},{4,5},{5,6},{6,7},{7,4},{8,9},{9,10},{10,1... | collective-permute-start | bytes 995336 | tf_op jit(solution)/shard_map/ppermute | solution.py:35
  155.1 34.2 %collective-permute-start.31 = (bf16[4,96,1728]{2,1,0:T(8,128)(2,1)S(1)}, bf16[4,96,1728]{2,1,0:T(8,128)(2,1)}, u32[]{:S(2)}, u32[]{:S(2)}) collective-permute-start(bf16[4,96,1728]{2,1,0:T(8,128)(2,1)S(1)} %pad_maximum_fusion.refs_1_), channel_id=1, source_target_pairs={{0,16},{4,12},{8,24},{12,4},{16,0},{20,28},{24,8},{28,20},{1,17},{... | collective-permute-start | bytes 3981320 | tf_op jit(solution)/shard_map/ppermute | solution.py:45
  158.4 27.2 %collective-permute-start.30 = (bf16[4,96,1728]{2,1,0:T(8,128)(2,1)S(1)}, bf16[4,96,1728]{2,1,0:T(8,128)(2,1)}, u32[]{:S(2)}, u32[]{:S(2)}) collective-permute-start(bf16[4,96,1728]{2,1,0:T(8,128)(2,1)S(1)} %pad_maximum_fusion.refs_1_), channel_id=1, source_target_pairs={{0,8},{4,20},{8,0},{12,28},{16,24},{20,4},{24,16},{28,12},{1,9},{5... | collective-permute-start | bytes 3981320 | tf_op jit(solution)/shard_map/ppermute | solution.py:45
  164.1 46.8 %collective-permute-start.34 = (bf16[1280,1536]{1,0:T(8,128)(2,1)}, bf16[1280,1536]{1,0:T(8,128)(2,1)}, u32[]{:S(2)}, u32[]{:S(2)}) collective-permute-start(bf16[1280,1536]{1,0:T(8,128)(2,1)} %convolution_convert_fusion.refs_3_.refs_4_.refs_6_.refs_7_), channel_id=1, source_target_pairs={{0,4},{4,0},{8,12},{12,8},{16,20},{20,16},{24,28},{28,24},{1,5},{5... | collective-permute-start | bytes 11796488 | tf_op jit(solution)/shard_map/ppermute | solution.py:40
  169.2 68.0 %collective-permute-start.36 = (bf16[4,96,1728]{2,1,0:T(8,128)(2,1)S(1)}, bf16[4,96,1728]{2,1,0:T(8,128)(2,1)}, u32[]{:S(2)}, u32[]{:S(2)}) collective-permute-start(bf16[4,96,1728]{2,1,0:T(8,128)(2,1)S(1)} %pad_maximum_fusion.refs_1_), channel_id=1, source_target_pairs={{0,4},{4,0},{8,12},{12,8},{16,20},{20,16},{24,28},{28,24},{1,5},{5... | collective-permute-start | bytes 3981320 | tf_op jit(solution)/shard_map/ppermute | solution.py:40
  185.6 51.6 %collective-permute-start.37 = (bf16[4,96,1728]{2,1,0:T(8,128)(2,1)}, bf16[4,96,1728]{2,1,0:T(8,128)(2,1)}, u32[]{:S(2)}, u32[]{:S(2)}) collective-permute-start(bf16[4,96,1728]{2,1,0:T(8,128)(2,1)} %collective-permute-done.30.refs_0_.refs_2_), channel_id=1, source_target_pairs={{0,4},{4,0},{8,12},{12,8},{16,20},{20,16},{24,28},{28,24},{1,5},{5... | collective-permute-start | bytes 3981320 | tf_op jit(solution)/shard_map/ppermute | solution.py:40
  189.3 47.9 %collective-permute-start.38 = (bf16[4,96,1728]{2,1,0:T(8,128)(2,1)}, bf16[4,96,1728]{2,1,0:T(8,128)(2,1)}, u32[]{:S(2)}, u32[]{:S(2)}) collective-permute-start(bf16[4,96,1728]{2,1,0:T(8,128)(2,1)} %collective-permute-done.31.refs_1_.refs_3_), channel_id=1, source_target_pairs={{0,4},{4,0},{8,12},{12,8},{16,20},{20,16},{24,28},{28,24},{1,5},{5... | collective-permute-start | bytes 3981320 | tf_op jit(solution)/shard_map/ppermute | solution.py:40
  210.3 26.9 %collective-permute-start.39 = (bf16[4,96,1728]{2,1,0:T(8,128)(2,1)}, bf16[4,96,1728]{2,1,0:T(8,128)(2,1)S(1)}, u32[]{:S(2)}, u32[]{:S(2)}) collective-permute-start(bf16[4,96,1728]{2,1,0:T(8,128)(2,1)} %collective-permute-done.35.refs_4_), channel_id=1, source_target_pairs={{0,4},{4,0},{8,12},{12,8},{16,20},{20,16},{24,28},{28,24},{1,5},{5... | collective-permute-start | bytes 3981320 | tf_op jit(solution)/shard_map/ppermute | solution.py:40
  269.0 96.5 %collective-permute-start.41 = (bf16[256,768]{1,0:T(8,128)(2,1)S(1)}, bf16[256,768]{1,0:T(8,128)(2,1)S(1)}, u32[]{:S(2)}, u32[]{:S(2)}) collective-permute-start(bf16[256,768]{1,0:T(8,128)(2,1)S(1)} %get-tuple-element.144), channel_id=1, source_target_pairs={{2,0},{6,1},{0,2},{4,3},{3,4},{7,5},{1,6},{5,7},{10,8},{14,9},{8,1... | collective-permute-start | bytes 1179656 | tf_op jit(solution)/shard_map/ppermute | solution.py:426
  270.5 95.0 %collective-permute-start.40 = (bf16[256,768]{1,0:T(8,128)(2,1)S(1)}, bf16[256,768]{1,0:T(8,128)(2,1)S(1)}, u32[]{:S(2)}, u32[]{:S(2)}) collective-permute-start(bf16[256,768]{1,0:T(8,128)(2,1)S(1)} %get-tuple-element.145), channel_id=1, source_target_pairs={{0,0},{4,1},{2,2},{6,3},{1,4},{5,5},{3,6},{7,7},{8,8},{12,9},{10,1... | collective-permute-start | bytes 1179656 | tf_op jit(solution)/shard_map/ppermute | solution.py:426
  284.7 69.1 %collective-permute-start.44 = (bf16[384,6912]{1,0:T(8,128)(2,1)}, bf16[384,6912]{1,0:T(8,128)(2,1)}, u32[]{:S(2)}, u32[]{:S(2)}) collective-permute-start(bf16[384,6912]{1,0:T(8,128)(2,1)} %get-tuple-element.62), channel_id=1, source_target_pairs={{0,4},{4,0},{8,12},{12,8},{16,20},{20,16},{24,28},{28,24},{1,5},{5... | collective-permute-start | bytes 15925256 | tf_op jit(solution)/shard_map/ppermute | solution.py:40
  361.2 32.7 %collective-permute-start.47 = (bf16[192,6912]{1,0:T(8,128)(2,1)S(1)}, bf16[192,6912]{1,0:T(8,128)(2,1)}, u32[]{:S(2)}, u32[]{:S(2)}) collective-permute-start(bf16[192,6912]{1,0:T(8,128)(2,1)S(1)} %get-tuple-element.68), channel_id=1, source_target_pairs={{0,8},{4,20},{8,0},{12,28},{16,24},{20,4},{24,16},{28,12},{1,9},{5... | collective-permute-start | bytes 7962632 | tf_op jit(solution)/shard_map/ppermute | solution.py:45
  382.4 47.2 %collective-permute-start.51 = (bf16[640,768]{1,0:T(8,128)(2,1)}, bf16[640,768]{1,0:T(8,128)(2,1)}, u32[]{:S(2)}, u32[]{:S(2)}) collective-permute-start(bf16[640,768]{1,0:T(8,128)(2,1)} %get-tuple-element.132), channel_id=1, source_target_pairs={{2,0},{6,1},{0,2},{4,3},{3,4},{7,5},{1,6},{5,7},{10,8},{14,9},{8,1... | collective-permute-start | bytes 2949128 | tf_op jit(solution)/shard_map/ppermute | solution.py:426
  385.0 44.6 %collective-permute-start.50 = (bf16[640,768]{1,0:T(8,128)(2,1)}, bf16[640,768]{1,0:T(8,128)(2,1)}, u32[]{:S(2)}, u32[]{:S(2)}) collective-permute-start(bf16[640,768]{1,0:T(8,128)(2,1)} %get-tuple-element.133), channel_id=1, source_target_pairs={{0,0},{4,1},{2,2},{6,3},{1,4},{5,5},{3,6},{7,7},{8,8},{12,9},{10,1... | collective-permute-start | bytes 2949128 | tf_op jit(solution)/shard_map/ppermute | solution.py:426
  428.6 33.1 %collective-permute-start.53 = (bf16[384,3840]{1,0:T(8,128)(2,1)}, bf16[384,3840]{1,0:T(8,128)(2,1)}, u32[]{:S(2)}, u32[]{:S(2)}) collective-permute-start(bf16[384,3840]{1,0:T(8,128)(2,1)} %get-tuple-element.76), channel_id=1, source_target_pairs={{0,4},{4,0},{8,12},{12,8},{16,20},{20,16},{24,28},{28,24},{1,5},{5... | collective-permute-start | bytes 8847368 | tf_op jit(solution)/shard_map/ppermute | solution.py:40
  447.5 47.1 %collective-permute-start.49 = (bf16[256,768]{1,0:T(8,128)(2,1)}, bf16[256,768]{1,0:T(8,128)(2,1)}, u32[]{:S(2)}, u32[]{:S(2)}) collective-permute-start(bf16[256,768]{1,0:T(8,128)(2,1)} %get-tuple-element.138), channel_id=1, source_target_pairs={{2,0},{6,1},{0,2},{4,3},{3,4},{7,5},{1,6},{5,7},{10,8},{14,9},{8,1... | collective-permute-start | bytes 1179656 | tf_op jit(solution)/shard_map/ppermute | solution.py:426
  449.3 45.4 %collective-permute-start.48 = (bf16[256,768]{1,0:T(8,128)(2,1)}, bf16[256,768]{1,0:T(8,128)(2,1)}, u32[]{:S(2)}, u32[]{:S(2)}) collective-permute-start(bf16[256,768]{1,0:T(8,128)(2,1)} %get-tuple-element.139), channel_id=1, source_target_pairs={{0,0},{4,1},{2,2},{6,3},{1,4},{5,5},{3,6},{7,7},{8,8},{12,9},{10,1... | collective-permute-start | bytes 1179656 | tf_op jit(solution)/shard_map/ppermute | solution.py:426
  457.1 44.1 %all-to-all-start.2 = ((bf16[4,96,1728]{2,1,0:T(8,128)(2,1)}), bf16[4,96,1728]{2,1,0:T(8,128)(2,1)}, u32[]{:S(2)}, u32[]{:S(2)}) async-start(bf16[4,96,1728]{2,1,0:T(8,128)(2,1)} %sum_far.3.refs_0_), calls=%async_computation.2 | async-start | bytes 2752512 | tf_op jit(solution)/shard_map/all_to_all | solution.py:390
  (124 other events, 1477.5 us)

commit v3 on v2

--- a/solution.py
+++ b/solution.py
@@ -14,6 +14,8 @@
 BF = jnp.bfloat16
 F32 = jnp.float32
 MIB = 1024 * 1024
+TOOK = {'assemble': 1, 'self_forward': 1, 'self_backward': 1, 'weight_grads': 0.5, 'sum_keys': 1, 'rows_back': 1, 'sum_far': 1, 'spread': 1, 'pick_with_ids': 1, 'pick': 1, 'join': 1, 'window_bias': 1, 'cross_forward': 1, 'cross_backward': 1, 'bucket_sums': 1, 'sum_cores': 1, 'sum_paths': 2, 'feed_forward': 1, 'norm_back': 1, 'stack': 1, 'project': 1}
+OPT = {'T': 0, 'Q': 1, 'R': 0, 'S': 0, 'A': 0, 'B': 1, 'C': 0, 'D': 1, 'E': 0, 'F': 1, 'G': 0, 'H': 0, 'I': 0, 'J': 0, 'K': 0, 'L': 2, 'M': 0, 'N': 0, 'P': 1}
 
 
 def nn(left, right):
@@ -45,7 +47,7 @@
     return lax.ppermute(x, "fsdp", [(i, i ^ (second if i & 1 else first)) for i in range(8)])
 
 
-def assemble_kernel(starts, *refs):
+def assemble_kernel(starts, by_distance, *refs):
     pieces, outs = refs[:8], refs[8:]
     me = lax.axis_index("fsdp")
     odd = lax.rem(me, 2)
@@ -73,7 +75,7 @@
     for place, piece in zip(places, pieces):
         here = pl.ds(pl.multiple_of(place * rows, rows), rows)
         for s in range(ranks):
-            block = piece[lax.rem(rank - s + ranks, ranks)]
+            block = piece[lax.rem(rank - s + ranks, ranks) if by_distance else s]
             for out_ref, parts in zip(outs, starts):
                 for first, width, base, stride in parts:
                     out_ref[here, base + s * stride : base + s * stride + width] = block[
@@ -99,14 +101,14 @@
     return pieces + [flip(p, "fsdp", 1) for p in pieces]
 
 
-def gather_end(pieces, layout, earlier=()):
+def gather_end(pieces, layout, earlier=(), by_distance=True):
     ranks, rows = pieces[0].shape[:2]
     widths = [sum(part[1] for part in parts) * ranks for parts in layout]
     if len(pieces) == 1:
         outs = []
         rank = lax.axis_index("tensor")
         order = lax.rem(rank + ranks - jnp.arange(ranks, dtype=jnp.int32), ranks)
-        blocks = jnp.take(pieces[0], order, axis=0)
+        blocks = jnp.take(pieces[0], order, axis=0) if by_distance else pieces[0]
         for parts in layout:
             columns = {}
             for first, width, base, stride in parts:
@@ -116,7 +118,7 @@
         return outs
     return run(
         "assemble",
-        functools.partial(assemble_kernel, layout),
+        functools.partial(assemble_kernel, layout, by_distance),
         pieces,
         [pl.BlockSpec(memory_space=pltpu.VMEM)] * 8,
         earlier,
@@ -127,7 +129,7 @@
 
 
 def run(name, kernel, operands, in_specs, earlier=(), took=1, **how):
-    count = len(earlier)
+    count, took = len(earlier), took * TOOK[name]
 
     def body(*refs):
         kernel(*refs[count:])
@@ -164,6 +166,30 @@
             (parts[0].shape[0], sum(x.shape[1] for x in parts)), parts[0].dtype
         ),
     )
+
+
+def spread_kernel(*refs):
+    out_ref, first = refs[-1], 0
+    for ref in refs[:-1]:
+        for s in range(out_ref.shape[0]):
+            out_ref[s, :, first : first + ref.shape[1]] = ref[...]
+        first += ref.shape[1]
+
+
+def gather_ranks_at_once(shards, earlier=()):
+    ranks, rows = lax.axis_size("tensor"), shards[0].shape[0]
+    width = sum(x.shape[1] for x in shards)
+    if rows % 16:
+        return lax.all_gather(beside(shards), "tensor", axis=0)
+    copies = run(
+        "spread",
+        spread_kernel,
+        shards,
+        [pl.BlockSpec(memory_space=pltpu.VMEM)] * len(shards),
+        earlier,
+        out_shape=jax.ShapeDtypeStruct((ranks, rows, width), shards[0].dtype),
+    )
+    return lax.all_to_all(copies, "tensor", split_axis=0, concat_axis=0, tiled=True)
 
 
 def gather_ranks(shards, earlier=()):
@@ -281,8 +307,10 @@
     return list(kept_and_sent)
 
 
-def rows_back_kernel(grad_ref, weight_ref, out_ref):
-    out_ref[...] = nt(grad_ref[...], weight_ref[...]).astype(BF)
+def rows_back_kernel(grad_ref, weight_ref, low_ref, high_ref):
+    half = low_ref.shape[0]
+    low_ref[...] = nt(grad_ref[:half], weight_ref[...]).astype(BF)
+    high_ref[...] = nt(grad_ref[half:], weight_ref[...]).astype(BF)
 
 
 def rows_back(grad, weight, earlier=()):
@@ -299,8 +327,8 @@
         earlier,
         6,
         grid=(model // tile,),
-        out_specs=pl.BlockSpec((rows, tile), lambda i: (0, i)),
-        out_shape=jax.ShapeDtypeStruct((rows, model), BF),
+        out_specs=[pl.BlockSpec((rows // 2, tile), lambda i: (0, i))] * 2,
+        out_shape=[jax.ShapeDtypeStruct((rows // 2, model), BF)] * 2,
         compiler_params=pltpu.CompilerParams(vmem_limit_bytes=48 * MIB),
     )
 
@@ -407,6 +435,34 @@
     return pairs
 
 
+def pick_with_ids_kernel(x_ref, ids_ref, *outs):
+    high = lax.axis_index("tensor") // 2
+    rows = x_ref.shape[1]
+    for r, out_ref in enumerate(outs):
+        b = high + r - 2 * high * r
+        out_ref[:rows] = x_ref[b]
+        out_ref[rows:] = jnp.zeros((out_ref.shape[0] - rows, x_ref.shape[2]), BF)
+        for w in range(rows // WIN):
+            place = lax.rem(ids_ref[b, w], WIN).astype(F32).astype(BF)
+            out_ref[rows + 16 * w : rows + 16 * (w + 1), :WIN] = jnp.broadcast_to(place, (16, WIN))
+
+
+def gathered_with_ids(x, ids, earlier=()):
+    rows, width = x.shape[1:]
+    windows = rows // WIN
+    parts = run(
+        "pick_with_ids",
+        pick_with_ids_kernel,
+        [x, ids.reshape(ids.shape[0], windows, 1, WIN)],
+        [pl.BlockSpec(memory_space=pltpu.VMEM)] * 2,
+        earlier,
+        out_shape=[jax.ShapeDtypeStruct((rows + 16 * windows, width), BF)] * 2,
+    )
+    moved = [lax.ppermute(y, ("fsdp", "tensor"), round_moves(r, False)) for r, y in enumerate(parts)]
+    places = [y[rows + 16 * w : rows + 16 * w + 1, :WIN] for y in moved for w in range(windows)]
+    return below([y[:rows] for y in moved]), below(places).astype(jnp.int32), moved, parts[:1]
+
+
 def gathered(x):
     high = lax.axis_index("tensor") // 2
     parts = [
@@ -420,11 +476,57 @@
     return below(parts)
 
 
-def returned(x):
-    half = x.shape[0] // 2
+def pick_kernel(x_ref, *outs):
+    high = lax.axis_index("tensor") // 2
+    for r, out_ref in enumerate(outs):
+        out_ref[...] = x_ref[high + r - 2 * high * r]
+
+
+def pick_with_ids_kernel(x_ref, ids_ref, *outs):
+    high = lax.axis_index("tensor") // 2
+    rows = x_ref.shape[1]
+    for r, out_ref in enumerate(outs):
+        b = high + r - 2 * high * r
+        out_ref[:rows] = x_ref[b]
+        out_ref[rows:] = jnp.zeros((out_ref.shape[0] - rows, x_ref.shape[2]), BF)
+        for w in range(rows // WIN):
+            place = lax.rem(ids_ref[b, w], WIN).astype(F32).astype(BF)
+            out_ref[rows + 16 * w : rows + 16 * (w + 1), :WIN] = jnp.broadcast_to(place, (16, WIN))
+
+
+def gathered_with_ids(x, ids, earlier=()):
+    rows, width = x.shape[1:]
+    windows = rows // WIN
+    parts = run(
+        "pick_with_ids",
+        pick_with_ids_kernel,
+        [x, ids.reshape(ids.shape[0], windows, 1, WIN)],
+        [pl.BlockSpec(memory_space=pltpu.VMEM)] * 2,
+        earlier,
+        out_shape=[jax.ShapeDtypeStruct((rows + 16 * windows, width), BF)] * 2,
+    )
+    moved = [lax.ppermute(y, ("fsdp", "tensor"), round_moves(r, False)) for r, y in enumerate(parts)]
+    places = [y[rows + 16 * w : rows + 16 * w + 1, :WIN] for y in moved for w in range(windows)]
+    return below([y[:rows] for y in moved]), below(places).astype(jnp.int32), moved, parts[:1]
+
+
+def gathered_after(x, earlier):
+    parts = run(
+        "pick",
+        pick_kernel,
+        [x],
+        [pl.BlockSpec(memory_space=pltpu.VMEM)],
+        earlier,
+        out_shape=[jax.ShapeDtypeStruct(x.shape[1:], x.dtype)] * 2,
+        compiler_params=pltpu.CompilerParams(vmem_limit_bytes=48 * MIB),
+    )
+    moved = [lax.ppermute(y, ("fsdp", "tensor"), round_moves(r, False)) for r, y in enumerate(parts)]
+    return below(moved)
+
+
+def returned(parts):
     return [
-        lax.ppermute(x[r * half : (r + 1) * half], ("fsdp", "tensor"), round_moves(r, True))
-        for r in range(2)
+        lax.ppermute(x, ("fsdp", "tensor"), round_moves(r, True)) for r, x in enumerate(parts)
     ]
 
 
@@ -779,6 +881,133 @@
     return u * half, slope
 
 
+def row_scale(stream):
+    return lax.rsqrt(jnp.mean(stream * stream, axis=-1, keepdims=True) + EPSILON)
+
+
+def norm_back_kernel(count, follows, *refs):
+    stream_ref, gain_ref, upper_ref = refs[:3]
+    if count:
+        grad_refs, weight_ref, refs = refs[3 : 3 + count], refs[3 + count], refs[4 + count :]
+        incoming, first = 0.0, 0
+        for grad_ref in grad_refs:
+            width = grad_ref.shape[1]
+            incoming = incoming + nt(grad_ref[...], weight_ref[:, first : first + width])
+            first += width
+    else:
+        incoming, refs = refs[3][...], refs[4:]
+    next_ref, refs = (refs[0], refs[1:]) if follows else (None, refs)
+    stream = stream_ref[...].astype(F32)
+    scale = row_scale(stream)
+    scaled = incoming * gain_ref[...]
+    along = jnp.mean(scaled * stream, axis=-1, keepdims=True)
+    grad = upper_ref[...].astype(F32) + (scale * scaled - stream * (scale * scale * scale) * along)
+
+    @pl.when(pl.program_id(0) == 0)
+    def _():
+        refs[0][...] = jnp.zeros_like(refs[0])
+
+    refs[0][...] += jnp.sum(incoming * stream * scale, axis=0, keepdims=True)
+    low = grad.astype(BF)
+    if follows:
+        refs[1][...] = low
+        refs[2][...] = grad
+        refs[3][...] = nn(low, next_ref[...]).astype(BF)
+    else:
+        for i, ref in enumerate(refs[1:]):
+
+            @pl.when(pl.program_id(0) == i)
+            def _(ref=ref):
+                ref[...] = low
+
+
+def norm_back_call(stream, gain, upper, grads, weight, following=None, earlier=()):
+    rows, model = stream.shape
+    count, follows = (len(grads), following is not None) if weight is not None else (0, following is not None)
+    tile = pl.BlockSpec((WIN, model), lambda i: (i, 0))
+
+    def whole(x):
+        return pl.BlockSpec(x.shape, lambda i: (0, 0))
+
+    operands = [stream, gain, upper, *grads]
+    specs = [tile, whole(gain), tile] + [
+        pl.BlockSpec((WIN, x.shape[1]), lambda i: (i, 0)) for x in grads
+    ]
+    for x in (weight, following):
+        if x is not None:
+            operands.append(x)
+            specs.append(whole(x))
+    if follows:
+        outs = [(rows, kind) for kind in (BF, F32, BF)]
+        out_specs = [tile] * 3
+    else:
+        outs = [(WIN, BF)] * (rows // WIN)
+        out_specs = [pl.BlockSpec((WIN, model), lambda i: (0, 0))] * (rows // WIN)
+    return run(
+        "norm_back",
+        functools.partial(norm_back_kernel, count, follows),
+        operands,
+        specs,
+        earlier,
+        5,
+        grid=(rows // WIN,),
+        out_specs=[whole(gain)] + out_specs,
+        out_shape=[jax.ShapeDtypeStruct(gain.shape, F32)]
+        + [jax.ShapeDtypeStruct((n, model), kind) for n, kind in outs],
+        compiler_params=pltpu.CompilerParams(vmem_limit_bytes=48 * MIB),
+    )
+
+
+def feed_forward_kernel(
+    n_ref, g_ref, x_ref, in_ref, out_ref, act_ref, pre_ref, back_ref, low_ref, high_ref, sum_ref
+):
+    step = pl.program_id(0)
+    half = n_ref.shape[0] // 2
+
+    @pl.when(step == 0)
+    def _():
+        sum_ref[...] = x_ref[...]
+        back_ref[...] = jnp.zeros_like(back_ref)
+
+    for rows in (slice(0, half), slice(half, 2 * half)):
+        gate, slope = gate_and_slope(nn(n_ref[rows, :], in_ref[...]))
+        activated = gate.astype(BF)
+        act_ref[rows, :] = activated
+        sum_ref[rows, :] += nt(activated, out_ref[...])
+        pre_grad = (nn(g_ref[rows, :], out_ref[...]) * slope).astype(BF)
+        pre_ref[rows, :] = pre_grad
+        back_ref[rows, :] += nt(pre_grad, in_ref[...])
+
+    @pl.when(step == pl.num_programs(0) - 1)
+    def _():
+        low_ref[...] = sum_ref[:half].astype(BF)
+        high_ref[...] = sum_ref[half:].astype(BF)
+
+
+def feed_forward(rows, grads, stream, in_weight, out_weight, earlier=()):
+    count, model = rows.shape
+    units, tile = in_weight.shape[1], 512
+    whole = pl.BlockSpec((count, model), lambda i: (0, 0))
+    half = pl.BlockSpec((count // 2, model), lambda i: (0, 0))
+    weight = pl.BlockSpec((model, tile), lambda i: (0, i))
+    part = pl.BlockSpec((count, tile), lambda i: (0, i))
+    return run(
+        "feed_forward",
+        feed_forward_kernel,
+        [rows, grads, stream, in_weight, out_weight],
+        [whole, whole, whole, weight, weight],
+        earlier,
+        16,
+        grid=(units // tile,),
+        out_specs=[part, part, whole, half, half],
+        out_shape=[jax.ShapeDtypeStruct((count, units), BF)] * 2
+        + [jax.ShapeDtypeStruct((count, model), F32)]
+        + [jax.ShapeDtypeStruct((count // 2, model), BF)] * 2,
+        scratch_shapes=[pltpu.VMEM((count, model), F32)],
+        compiler_params=pltpu.CompilerParams(vmem_limit_bytes=48 * MIB),
+    )
+
+
 def local(
     hidden, passages, block_ids, buckets, norm_gains, self_query, self_key, self_value, self_out,
     cross_query, cross_key, cross_value, cross_out, ffn_in, ffn_out, rel_bias, out_grad,
@@ -793,26 +1022,58 @@
     self_layout = [(k * hw, hw, k * width, hw) for k in range(5)]
     kv_layout = [(0, hw, 0, hw), (hw, hw, width, hw)]
     late_layout = [(0, ffn, 0, ffn), (ffn, ffn, ranks * ffn, ffn), (2 * ffn, hw, 2 * ranks * ffn, hw)]
+    def option(name, *choices):
+        return choices[OPT[name] % len(choices)]
+
     gains = gather_small(jnp.transpose(norm_gains))
     gains = jnp.transpose(gains, (1, 0, 2)).reshape(3, model).astype(F32)
-    self_blocks = gather_ranks([self_query, self_key, self_value, self_out, cross_query])
-    kv_blocks = gather_ranks([cross_key, cross_value])
-    ids = gathered(
-        lax.dynamic_slice_in_dim(block_ids, rank * rows, rows, 1).reshape(batches, -1, WIN)
-    )
-    stream_low = gathered(hidden)
+    if OPT["S"] == 0:
+        self_blocks = gather_ranks([self_query, self_key, self_value, self_out, cross_query])
+        kv_blocks = gather_ranks([cross_key, cross_value])
+    else:
+        both = beside([self_query, self_key, self_value, self_out, cross_query, cross_key, cross_value])
+        both = lax.all_gather(both, "tensor", axis=0)
+        cut = 5 * hw
+        self_blocks, kv_blocks = [both[:, :, :cut]], [both[:, :, cut:]]
+    if OPT["R"] == 0:
+        ids = lax.dynamic_slice_in_dim(block_ids, rank * rows, rows, 1)
+        stream_low, ids, _, _ = gathered_with_ids(hidden, ids)
+    else:
+        ids = gathered(
+            lax.dynamic_slice_in_dim(block_ids, rank * rows, rows, 1).reshape(batches, -1, WIN)
+        )
+        stream_low = gathered(hidden)
     encoded = gathered(passages)
-    bias = window_bias(rel_bias, buckets, [gains, *self_blocks, *kv_blocks])
-    self_pieces = gather_cores(gather_far(gather_paths(jnp.stack(self_blocks))))
+    bias = window_bias(
+        rel_bias,
+        buckets,
+        option(
+            "C",
+            [gains, *self_blocks, *kv_blocks],
+            [gains, *self_blocks],
+            [gains, *kv_blocks],
+            [gains, stream_low],
+            [gains, encoded],
+        ),
+    )
+    self_pieces = gather_cores(gather_far(gather_paths(jnp.stack(self_blocks) if OPT["S"] == 0 else self_blocks[0])))
     qkv_weight, so_weight, cq_weight = gather_end(
         self_pieces,
         [self_layout[:3], [(3 * hw, hw, 0, hw)], [(4 * hw, hw, 0, hw)]],
-        [bias, stream_low],
-    )
-    late_blocks = gather_ranks([ffn_in, ffn_out, cross_out], self_blocks + kv_blocks)
-    late_paths = gather_paths(jnp.stack(late_blocks))
-    kv_pieces = gather_cores(gather_far(gather_paths(jnp.stack(kv_blocks))))
-    (kv_weight,) = gather_end(kv_pieces, [kv_layout], [qkv_weight])
+        option("B", [bias, stream_low], [bias], [bias, encoded], []),
+        OPT["S"] == 0,
+    )
+    late_earlier = option(
+        "A", self_blocks + kv_blocks, [bias], [stream_low], [encoded], [*kv_blocks, stream_low, bias],
+        self_pieces[3:4], [qkv_weight], [*self_pieces[3:4], stream_low],
+    )
+    if OPT["Q"] == 0:
+        late_blocks = gather_ranks_at_once([ffn_in, ffn_out, cross_out], late_earlier)
+    else:
+        late_blocks = jnp.stack(gather_ranks([ffn_in, ffn_out, cross_out], late_earlier))
+    late_paths = gather_paths(late_blocks)
+    kv_pieces = gather_cores(gather_far(gather_paths(jnp.stack(kv_blocks) if OPT["S"] == 0 else kv_blocks[0])))
+    (kv_weight,) = gather_end(kv_pieces, [kv_layout], option("D", [qkv_weight], [bias], [encoded]), OPT["S"] == 0)
 
     stream = stream_low.astype(F32)
     scale_one = norm_scale(stream)
@@ -827,23 +1088,32 @@
     own_kv = nn(encoded, kv_weight).astype(BF)
     other_kv = flip(own_kv, "fsdp", 1)
     late_far = gather_far(late_paths)
-    cross_context, exact, total = cross_forward(queries, own_kv, other_kv, late_paths[1:])
+    incoming = gathered_after(out_grad, option("T", [qkv_weight], [context], [own_kv], late_paths[:1], late_far[3:]))
+    cross_context, exact, total = cross_forward(
+        queries, own_kv, other_kv, option("E", late_paths[1:], [], late_far[3:], [incoming])
+    )
     late_pieces = gather_cores(late_far)
     in_weight, out_weight, co_weight = gather_end(
         late_pieces,
         [[(0, ffn, 0, ffn)], [(ffn, ffn, 0, ffn)], [(2 * ffn, hw, 0, hw)]],
         [cross_context],
-    )
-
-    incoming = gathered(out_grad)
+        OPT["Q"] != 0,
+    )
+
     after_cross = after_self + nt(cross_context, co_weight)
     scale_three = norm_scale(after_cross)
     normed_three = (after_cross * scale_three * gains[2]).astype(BF)
-    gate, slope = gate_and_slope(nn(normed_three, in_weight))
-    activated = gate.astype(BF)
-    output = (after_cross + nt(activated, out_weight)).astype(BF)
-    pre_grad = (nn(incoming, out_weight) * slope).astype(BF)
-    normed_grad = nt(pre_grad, in_weight)
+    if OPT["F"] == 0:
+        activated, pre_grad, normed_grad, *output = feed_forward(
+            normed_three, incoming, after_cross, in_weight, out_weight
+        )
+    else:
+        gate, slope = gate_and_slope(nn(normed_three, in_weight))
+        activated = gate.astype(BF)
+        output = (after_cross + nt(activated, out_weight)).astype(BF)
+        output = [output[:WIN], output[WIN:]]
+        pre_grad = (nn(incoming, out_weight) * slope).astype(BF)
+        normed_grad = nt(pre_grad, in_weight)
     stream_part, gain_three = norm_back(after_cross, scale_three, gains[2], normed_grad)
     grad_two = incoming.astype(F32) + stream_part
     branch_two = grad_two.astype(BF)
@@ -856,42 +1126,71 @@
     late_stage = scatter_cores(late_grads)
 
     query_grad, key_own, value_own, key_other, value_other = cross_backward(
-        queries, context_grad, exact, total, own_kv, other_kv, [late_grads[0], output]
+        queries, context_grad, exact, total, own_kv, other_kv,
+        option("G", [late_grads[0], output[0]], [late_grads[0]], [output[0]]),
     )
     output = returned(output)
     kv_received = [flip(x, "fsdp", 1) for x in (key_other, value_other)]
     late_stage = scatter_paths(late_stage, [query_grad])
-    normed_grad = nt(query_grad, cq_weight)
-    stream_part, gain_two = norm_back(after_self, scale_two, gains[1], normed_grad)
-    grad_one = grad_two + stream_part
-    branch_one = grad_one.astype(BF)
-    context_grad = nn(branch_one, so_weight).astype(BF)
+    if OPT["H"] == 0:
+        normed_grad = nt(query_grad, cq_weight)
+        stream_part, gain_two = norm_back(after_self, scale_two, gains[1], normed_grad)
+        grad_one = grad_two + stream_part
+        branch_one = grad_one.astype(BF)
+        context_grad = nn(branch_one, so_weight).astype(BF)
+    else:
+        gain_two, branch_one, grad_one, context_grad = norm_back_call(
+            after_self, gains[1][None], grad_two, [query_grad], cq_weight, so_weight,
+            option("H", [], [], [late_stage[0]]),
+        )
     kv_grad = sum_keys([key_own, value_own], kv_received, [late_stage[0]])
     encoded_grad = rows_back(kv_grad, kv_weight)
     encoded_grads = returned(encoded_grad)
 
-    gq, gk, gv, sums = self_backward(qkv, context_grad, ids, bias, [encoded_grad, *late_stage[1:]])
+    gq, gk, gv, sums = self_backward(
+        qkv, context_grad, ids, bias,
+        option("I", [encoded_grad[0], *late_stage[1:]], [encoded_grad[0]], [late_stage[0]], []),
+    )
     late_stage = scatter_far(late_stage, [gq])
     self_grads = weight_grads(
         [normed_one, branch_one, normed_two],
         [((0,), [gq]), ((0,), [gk]), ((0,), [gv]), ((1,), [context]), ((2,), [query_grad])],
-        late_stage[:1],
+        option("J", late_stage[:1], []),
     )
     self_stage = scatter_cores(self_grads)
     kv_sums = weight_grads([encoded], [((0,), [kv_grad])], [self_grads[0]])
     kv_stage = scatter_cores(kv_sums)
-    late_blocks = scatter_end(late_stage, late_layout, [kv_sums[0]])
-    self_stage = scatter_paths(self_stage, [late_blocks])
-    kv_stage = scatter_paths(kv_stage, [self_stage[0]])
+    if OPT["K"] == 0:
+        late_blocks = scatter_end(late_stage, late_layout, [kv_sums[0]])
+        self_stage = scatter_paths(self_stage, [late_blocks])
+    else:
+        self_stage = scatter_paths(self_stage, [kv_sums[0]])
+        late_blocks = scatter_end(late_stage, late_layout, [self_stage[0]])
+    kv_stage = scatter_paths(kv_stage, [self_stage[0], late_blocks])
     late_total = scatter_tensor(late_blocks)
     in_total, out_total, co_total = late_total[:, :ffn], late_total[:, ffn : 2 * ffn], late_total[:, 2 * ffn :]
-    normed_grad = sum(nt(x, qkv_weight[:, k * width : (k + 1) * width]) for k, x in enumerate((gq, gk, gv)))
-    stream_part, gain_one = norm_back(stream, scale_one, gains[0], normed_grad)
-    input_grads = returned((grad_one + stream_part).astype(BF))
-    bias_lanes = bucket_sums(sums, buckets, rel_bias.shape[0], [kv_stage[0]])
-    self_stage = scatter_far(self_stage, [bias_lanes])
+    if OPT["L"] == 0:
+        gain_one, *input_grad = norm_back_call(
+            stream_low, gains[0][None], grad_one, [gq, gk, gv], qkv_weight, None, [self_stage[0]]
+        )
+    elif OPT["L"] == 1:
+        gain_one, *input_grad = norm_back_call(
+            stream_low, gains[0][None], grad_one, [gq, gk, gv], qkv_weight, None, [kv_stage[0]]
+        )
+    else:
+        normed_grad = sum(
+            nt(x, qkv_weight[:, k * width : (k + 1) * width]) for k, x in enumerate((gq, gk, gv))
+        )
+        stream_part, gain_one = norm_back(stream, scale_one, gains[0], normed_grad)
+        input_grad = (grad_one + stream_part).astype(BF)
+        input_grad = [input_grad[:WIN], input_grad[WIN:]]
+    input_grads = returned(input_grad)
+    bias_lanes = bucket_sums(
+        sums, buckets, rel_bias.shape[0], option("M", [kv_stage[0]], [self_stage[0]], [self_stage[0], input_grad[0]])
+    )
+    self_stage = scatter_far(self_stage, option("N", [bias_lanes], [kv_stage[0]], [input_grad[0]]))
     kv_stage = scatter_far(kv_stage, [self_stage[0]])
-    self_total = scatter_tensor(scatter_end(self_stage, self_layout, [kv_stage[0]]))
+    self_total = scatter_tensor(scatter_end(self_stage, self_layout, option("P", [kv_stage[0]], [])))
     q_total, k_total, v_total, so_total, cq_total = column_blocks(self_total, 5)
     kv_total = scatter_tensor(scatter_end(kv_stage, kv_layout, [kv_stage[0]]))
 

time: 548 us -> 514 us (0.938)
  starting transfers between devices: 128 us -> 80.3 us
  waiting for transfers between devices: 73.9 us -> 95.7 us
    ppermute x9, starting transfers between devices: 45.2 us -> 12.3 us  [shift(): return lax.ppermute(x, axis, [(i, (i + by) % size) for i in range(size)])]
    ppermute x8 -> x2, waiting for transfers between devices: 10.3 us -> 24.3 us  [gathered(): lax.ppermute(lax.dynamic_index_in_dim(x, r ^ high, 0, keepdims=False), ('...]
    ppermute x9, waiting for transfers between devices: 28.5 us -> 35.4 us  [shift(): return lax.ppermute(x, axis, [(i, (i + by) % size) for i in range(size)])]
    ppermute x8 -> x2, starting transfers between devices: 11.7 us -> 5.1 us  [gathered(): lax.ppermute(lax.dynamic_index_in_dim(x, r ^ high, 0, keepdims=False), ('...]
    ppermute x6 -> x10, starting transfers between devices: 20 us -> 16.1 us  [the longest x6 10.7 us: returned(): lax.ppermute(x, ('fsdp', 'tensor'), round_moves(r, True))]
    unnamed x163 -> x152, local copies, waits for them, and re-layouts: 19.9 us -> 23.6 us
    pallas_call x26 -> x28, Pallas kernels: 232 us -> 234 us  [run(): pl.pallas_call(body, in_specs=[pl.BlockSpec(memory_space=pl.ANY)] * count...]
  transfers between devices with their start and end apart: 69 -> 67, of which waited for: 12 -> 11; matrix products, arithmetic and copies ran while one was open for 12% -> 10% of each run, Pallas kernels for 41% -> 42%
where the time goes in v3:
time: 514 us; the launch traced here: 505 us
  Pallas kernels  234 us (46%)
  waiting for transfers between devices  95.7 us (19%)
  starting transfers between devices  80.3 us (16%)
  matrix products  35.6 us (7%)
  local copies, waits for them, and re-layouts  34.9 us (7%)
  other arithmetic  23.1 us (4%)
    pallas_call x28, Pallas kernels, run(): pl.pallas_call(body, in_specs=[pl.BlockSpec(memory_space=pl.ANY)] * count...  234 us
    ppermute x9, waiting for transfers between devices, shift(): return lax.ppermute(x, axis, [(i, (i + by) % size) for i in range(size)])  35.4 us
    ppermute x2, waiting for transfers between devices, gathered(): lax.ppermute(lax.dynamic_index_in_dim(x, r ^ high, 0, keepdims=False), ('...  24.3 us
    unnamed x152, local copies, waits for them, and re-layouts  23.6 us
    dot_general x7, matrix products, nn(): return jnp.dot(left, right, preferred_element_type=F32)  20.9 us
    ppermute x28, starting transfers between devices, flip(): return lax.ppermute(x, axis, [(i, i ^ bits) for i in range(size)])  18.4 us
    ppermute x15, waiting for transfers between devices, two_way(): lax.ppermute(x, 'fsdp', [(i, i ^ (second if i & 1 else first)) for i in r...  17.9 us
    ppermute x15, starting transfers between devices, two_way(): lax.ppermute(x, 'fsdp', [(i, i ^ (second if i & 1 else first)) for i in r...  14.9 us
  transfers between devices with their start and end apart: 67, of which 11 were waited for; matrix products, arithmetic and copies ran while one was open for 10% of the time, Pallas kernels for 42%

profile of v3, /device:TPU:0, one launch (start us, length us, event | category | flops | bytes accessed | tf_op | source)
XLA Modules:
  0.0 505.2 jit_solution(17613792462396564031)
XLA Ops:
  2.2 5.0 collective-permute-start.10
  31.4 10.3 %collective-permute-done.6.refs_3_.refs_2_ = bf16[96,960]{1,0:T(8,128)(2,1)S(1)} collective-permute-done((bf16[96,960]{1,0:T(8,128)(2,1)}, bf16[96,960]{1,0:T(8,128)(2,1)S(1)}, u32[]{:S(2)}, u32[]{:S(2)}) %collective-permute-start.6) | collective-permute-done | bytes 184352 | tf_op jit(solution)/shard_map/ppermute | solution.py:37
  43.7 9.1 %window_bias.1.refs_0_.refs_6_.refs_8_ = f32[12,256,256]{2,1,0:T(8,128)} custom-call(f32[3,768]{1,0:T(4,128)} %convert_element_type.94.refs_0_, bf16[96,960]{1,0:T(8,128)(2,1)} %join.3.refs_1_.refs_0_, bf16[96,960]{1,0:T(8,128)(2,1)} %copy-done.45, bf16[96,960]{1,0:T(8,128)(2,1)} %copy-done.44, bf16[96,960]{1,0:T(8,128)(2,1)} %copy-done.43, ...), custom_call_target="tpu_custom_call" | custom-call | flops 9900000256 | bytes 31500000 | tf_op jit(solution)/shard_map/window_bias/pallas_call | solution.py:137
  59.1 8.2 %collective-permute-done.27 = bf16[96,1728]{1,0:T(8,128)(2,1)} collective-permute-done((bf16[96,1728]{1,0:T(8,128)(2,1)}, bf16[96,1728]{1,0:T(8,128)(2,1)}, u32[]{:S(2)}, u32[]{:S(2)}) %collective-permute-start.27) | collective-permute-done | bytes 331808 | tf_op jit(solution)/shard_map/ppermute | solution.py:37
  69.2 16.9 %collective-permute-done.26 = bf16[96,1728]{1,0:T(8,128)(2,1)} collective-permute-done((bf16[96,1728]{1,0:T(8,128)(2,1)}, bf16[96,1728]{1,0:T(8,128)(2,1)}, u32[]{:S(2)}, u32[]{:S(2)}) %collective-permute-start.26) | collective-permute-done | bytes 331808 | tf_op jit(solution)/shard_map/ppermute | solution.py:37
  99.0 11.4 %collective-permute-done.19.refs_3_ = bf16[4,96,960]{2,1,0:T(8,128)(2,1)S(1)} collective-permute-done((bf16[4,96,960]{2,1,0:T(8,128)(2,1)S(1)}, bf16[4,96,960]{2,1,0:T(8,128)(2,1)S(1)}, u32[]{:S(2)}, u32[]{:S(2)}) %collective-permute-start.19) | collective-permute-done | bytes 737312 | tf_op jit(solution)/shard_map/ppermute | solution.py:47
  110.4 24.3 %collective-permute-done.31 = bf16[640,768]{1,0:T(8,128)(2,1)S(1)} collective-permute-done((bf16[640,768]{1,0:T(8,128)(2,1)}, bf16[640,768]{1,0:T(8,128)(2,1)S(1)}, u32[]{:S(2)}, u32[]{:S(2)}) %collective-permute-start.31) | collective-permute-done | bytes 983072 | tf_op jit(solution)/shard_map/ppermute | solution.py:469
  143.4 5.3 %assemble.4 = (bf16[768,2304]{1,0:T(8,128)(2,1)}, bf16[768,768]{1,0:T(8,128)(2,1)}, bf16[768,768]{1,0:T(8,128)(2,1)}) custom-call(f32[12,256,256]{2,1,0:T(8,128)} %window_bias.1.refs_0_.refs_6_.refs_8_, bf16[4,96,960]{2,1,0:T(8,128)(2,1)S(1)} %pad_maximum_fusion.2.refs_1_, bf16[4,96,960]{2,1,0:T(8,128)(2,1)} %collective-permute-done.18.refs_2_, ...), custom_call_target="tpu_custom_call" | custom-call | flops 5324000256 | bytes 16940000 | tf_op jit(solution)/shard_map/assemble/pallas_call | solution.py:137
  156.2 12.2 %self_forward.1.refs_7_ = bf16[512,768]{1,0:T(8,128)(2,1)} custom-call(bf16[768,1536]{1,0:T(8,128)(2,1)} %copy-done.24, bf16[512,2304]{1,0:T(8,128)(2,1)} %convolution_convert_fusion.1.refs_1_.refs_2_.refs_3_.refs_4_, bf16[512,2304]{1,0:T(8,128)(2,1)} %convolution_convert_fusion.1.refs_1_.refs_2_.refs_3_.refs_4_, ...), custom_call_target="tpu_custom_call" | custom-call | flops 13200000000 | bytes 42000000 | tf_op jit(solution)/shard_map/self_forward/pallas_call | solution.py:137
  178.1 26.3 %cross_forward.1 = (bf16[512,768]{1,0:T(8,128)(2,1)S(1)}, f32[512,768]{1,0:T(8,128)S(1)}, f32[6,8,512]{2,1,0:T(8,128)S(1)}) custom-call(bf16[4,96,1728]{2,1,0:T(8,128)(2,1)} %collective-permute-done.28.refs_0_.refs_2_, bf16[4,96,1728]{2,1,0:T(8,128)(2,1)S(1)} %collective-permute-done.29.refs_1_.refs_3_, ...), custom_call_target="tpu_custom_call" | custom-call | flops 28600000512 | bytes 91000000 | tf_op jit(solution)/shard_map/cross_forward/pallas_call | solution.py:137
  206.4 7.7 %assemble.5 = (bf16[768,3072]{1,0:T(8,128)(2,1)}, bf16[768,3072]{1,0:T(8,128)(2,1)}, bf16[768,768]{1,0:T(8,128)(2,1)S(1)}) custom-call(bf16[512,768]{1,0:T(8,128)(2,1)S(1)} %get-tuple-element.62.refs_0_.refs_6_, bf16[4,96,1728]{2,1,0:T(8,128)(2,1)S(1)} %pad_maximum_fusion.refs_1_, bf16[4,96,1728]{2,1,0:T(8,128)(2,1)} %collective-permute-done.28.refs_0_.refs_2_, ...), custom_call_target="tpu_custom_call" | custom-call | flops 8703200256 | bytes 27692000 | tf_op jit(solution)/shard_map/assemble/pallas_call | solution.py:137
  223.0 5.8 %fusion.6.refs_4_ = bf16[512,3072]{1,0:T(8,128)(2,1)S(1)} fusion(f32[512,3072]{1,0:T(8,128)S(1)} %get-tuple-element.193, bf16[512,768]{1,0:T(8,128)(2,1)S(1)} %constant_dynamic-update-slice_fusion.2.refs_2_, bf16[768,3072]{1,0:T(8,128)(2,1)S(1)} %bitcast.89), kind=kOutput, calls=%fused_computation.10 | convolution fusion | flops 2445803520 | bytes 14942208 | tf_op jit(solution)/shard_map/dot_general | solution.py:22
  234.6 13.4 %weight_grads.3 = (bf16[384,6912]{1,0:T(8,128)(2,1)}, bf16[384,6912]{1,0:T(8,128)(2,1)}) custom-call(bf16[512,768]{1,0:T(8,128)(2,1)S(1)} %convolution_convert_fusion.3.refs_0_.refs_3_, bf16[512,768]{1,0:T(8,128)(2,1)S(1)} %multiply_convert_fusion.1.refs_1_, bf16[512,768]{1,0:T(8,128)(2,1)S(1)} %constant_dynamic-update-slice_fusion.2.refs_2_, ...), custom_call_target="tpu_custom_call" | custom-call | flops 6929999872 | bytes 22050000 | tf_op jit(solution)/shard_map/weight_grads/pallas_call | solution.py:137
  248.5 65.4 %cross_backward.1 = (bf16[512,768]{1,0:T(8,128)(2,1)S(1)}, f32[1280,768]{1,0:T(8,128)}, f32[1280,768]{1,0:T(8,128)}, bf16[1280,768]{1,0:T(8,128)(2,1)}, bf16[1280,768]{1,0:T(8,128)(2,1)}) custom-call(bf16[384,6912]{1,0:T(8,128)(2,1)} %get-tuple-element.68.refs_0_.refs_1_, bf16[256,768]{1,0:T(8,128)(2,1)S(1)} %get-tuple-element.168.refs_1_, ...), custom_call_target="tpu_custom_call" | custom-call | flops 68200001536 | bytes 217000000 | tf_op jit(solution)/shard_map/cross_backward/pallas_call | solution.py:137
  314.4 8.7 %sum_cores.3 = (bf16[192,6912]{1,0:T(8,128)(2,1)S(1)}, bf16[192,6912]{1,0:T(8,128)(2,1)}) custom-call(bf16[512,768]{1,0:T(8,128)(2,1)S(1)} %get-tuple-element.71.refs_0_.refs_8_, bf16[384,6912]{1,0:T(8,128)(2,1)} %get-tuple-element.68.refs_0_.refs_1_, bf16[384,6912]{1,0:T(8,128)(2,1)} %collective-permute-done.42.refs_2_), custom_call_target="tpu_custom_call" | custom-call | flops 9732096000 | bytes 30965760 | tf_op jit(solution)/shard_map/sum_cores/pallas_call | solution.py:137
  335.3 6.5 %sum_keys.1.refs_0_.refs_2_ = bf16[1280,1536]{1,0:T(8,128)(2,1)} custom-call(bf16[192,6912]{1,0:T(8,128)(2,1)} %copy-done.30, f32[1280,768]{1,0:T(8,128)} %get-tuple-element.74.refs_1_, f32[1280,768]{1,0:T(8,128)} %get-tuple-element.75.refs_2_, bf16[1280,768]{1,0:T(8,128)(2,1)} %collective-permute-done.43.refs_3_, ...), custom_call_target="tpu_custom_call" | custom-call | flops 6600000000 | bytes 21000000 | tf_op jit(solution)/shard_map/sum_keys/pallas_call | solution.py:137
  343.5 5.9 %rows_back.1 = (bf16[640,768]{1,0:T(8,128)(2,1)S(1)}, bf16[640,768]{1,0:T(8,128)(2,1)S(1)}) custom-call(bf16[1280,1536]{1,0:T(8,128)(2,1)} %sum_keys.1.refs_0_.refs_2_, bf16[768,1536]{1,0:T(8,128)(2,1)S(1)} %copy-done.25), custom_call_target="tpu_custom_call" | custom-call | flops 6600000000 | bytes 21000000 | tf_op jit(solution)/shard_map/rows_back/pallas_call | solution.py:137
  351.7 5.2 %collective-permute-done.45.refs_1_.refs_2_ = bf16[192,6912]{1,0:T(8,128)(2,1)} collective-permute-done((bf16[192,6912]{1,0:T(8,128)(2,1)}, bf16[192,6912]{1,0:T(8,128)(2,1)}, u32[]{:S(2)}, u32[]{:S(2)}) %collective-permute-start.45) | collective-permute-done | bytes 2654240 | tf_op jit(solution)/shard_map/ppermute | solution.py:47
  356.9 18.0 %self_backward.1 = (bf16[512,768]{1,0:T(8,128)(2,1)}, bf16[512,768]{1,0:T(8,128)(2,1)}, bf16[512,768]{1,0:T(8,128)(2,1)}, f32[12,256,256]{2,1,0:T(8,128)}) custom-call(bf16[640,768]{1,0:T(8,128)(2,1)} %copy-done.14, bf16[192,6912]{1,0:T(8,128)(2,1)} %collective-permute-done.45.refs_1_.refs_2_, ...), custom_call_target="tpu_custom_call" | custom-call | flops 19800000512 | bytes 63000000 | tf_op jit(solution)/shard_map/self_backward/pallas_call | solution.py:137
  376.1 6.2 %sum_paths.3 = (f32[96,6912]{1,0:T(8,128)S(1)}, bf16[96,6912]{1,0:T(8,128)(2,1)S(1)}) custom-call(bf16[512,768]{1,0:T(8,128)(2,1)S(1)} %copy-done.19, bf16[192,6912]{1,0:T(8,128)(2,1)} %copy-done.30, bf16[192,6912]{1,0:T(8,128)(2,1)} %collective-permute-done.45.refs_1_.refs_2_), custom_call_target="tpu_custom_call" | custom-call | flops 9732096000 | bytes 30965760 | tf_op jit(solution)/shard_map/sum_paths/pallas_call | solution.py:137
  383.8 7.7 %weight_grads.4 = (bf16[384,3840]{1,0:T(8,128)(2,1)}, bf16[384,3840]{1,0:T(8,128)(2,1)}) custom-call(f32[96,6912]{1,0:T(8,128)} %copy-done.22, bf16[512,768]{1,0:T(8,128)(2,1)S(1)} %copy-done.7, bf16[512,768]{1,0:T(8,128)(2,1)S(1)} %get-tuple-element.153.refs_2_, bf16[512,768]{1,0:T(8,128)(2,1)S(1)} %copy-done.9, bf16[512,768]{1,0:T(8,128)(2,1)S(1)} %copy-done.19, ...), custom_call_target="tpu_custom_call" | custom-call | flops 3849999872 | bytes 12250000 | tf_op jit(solution)/shard_map/weight_grads/pallas_call | solution.py:137
  403.3 6.7 %weight_grads.5 = (bf16[384,1536]{1,0:T(8,128)(2,1)S(1)}, bf16[384,1536]{1,0:T(8,128)(2,1)}) custom-call(bf16[384,3840]{1,0:T(8,128)(2,1)} %get-tuple-element.85.refs_0_.refs_1_, bf16[1280,768]{1,0:T(8,128)(2,1)S(1)} %copy-done.3, bf16[1280,1536]{1,0:T(8,128)(2,1)} %sum_keys.1.refs_0_.refs_2_), custom_call_target="tpu_custom_call" | custom-call | flops 1540000000 | bytes 4900000 | tf_op jit(solution)/shard_map/weight_grads/pallas_call | solution.py:137
  436.5 13.6 %bucket_sums.1.refs_0_ = f32[12,32,256]{2,1,0:T(8,128)} custom-call(bf16[192,1536]{1,0:T(8,128)(2,1)} %copy-done.28, f32[12,256,256]{2,1,0:T(8,128)} %get-tuple-element.92.refs_1_, s32[256,256]{1,0:T(8,128)} %refs_2_.3), custom_call_target="tpu_custom_call" | custom-call | flops 14300000256 | bytes 45500000 | tf_op jit(solution)/shard_map/bucket_sums/pallas_call | solution.py:137
  490.7 13.3 %all-to-all-done = bf16[4,96,960]{2,1,0:T(8,128)(2,1)S(1)} async-done(((bf16[4,96,960]{2,1,0:T(8,128)(2,1)}), bf16[4,96,960]{2,1,0:T(8,128)(2,1)S(1)}, u32[]{:S(2)}, u32[]{:S(2)}) %all-to-all-start) | async-done | bytes 737312 | tf_op jit(solution)/shard_map/all_to_all | solution.py:418
  (375 shorter events, 190.1 us)
Async XLA Ops:
  25.4 32.7 %collective-permute-start = (bf16[272,768]{1,0:T(8,128)(2,1)}, bf16[272,768]{1,0:T(8,128)(2,1)S(1)}, u32[]{:S(2)}, u32[]{:S(2)}) collective-permute-start(bf16[272,768]{1,0:T(8,128)(2,1)} %get-tuple-element.57), channel_id=1, source_target_pairs={{0,0},{1,4},{2,2},{3,6},{4,1},{5,5},{6,3},{7,7},{8,8},{9,12},{10,1... | collective-permute-start | bytes 1253384 | tf_op jit(solution)/shard_map/ppermute | solution.py:508
  27.0 31.8 %collective-permute-start.1 = (bf16[272,768]{1,0:T(8,128)(2,1)}, bf16[272,768]{1,0:T(8,128)(2,1)S(1)}, u32[]{:S(2)}, u32[]{:S(2)}) collective-permute-start(bf16[272,768]{1,0:T(8,128)(2,1)} %get-tuple-element.58), channel_id=1, source_target_pairs={{0,2},{1,6},{2,0},{3,4},{4,3},{5,7},{6,1},{7,5},{8,10},{9,14},{10,... | collective-permute-start | bytes 1253384 | tf_op jit(solution)/shard_map/ppermute | solution.py:508
  55.9 30.1 %collective-permute-start.26 = (bf16[96,1728]{1,0:T(8,128)(2,1)}, bf16[96,1728]{1,0:T(8,128)(2,1)}, u32[]{:S(2)}, u32[]{:S(2)}) collective-permute-start(bf16[96,1728]{1,0:T(8,128)(2,1)} %join.5), channel_id=1, source_target_pairs={{0,2},{1,3},{2,0},{3,1},{4,6},{5,7},{6,4},{7,5},{8,10},{9,11},{10,... | collective-permute-start | bytes 995336 | tf_op jit(solution)/shard_map/ppermute | solution.py:37
  58.1 36.2 %collective-permute-start.18 = (bf16[4,96,960]{2,1,0:T(8,128)(2,1)S(1)}, bf16[4,96,960]{2,1,0:T(8,128)(2,1)}, u32[]{:S(2)}, u32[]{:S(2)}) collective-permute-start(bf16[4,96,960]{2,1,0:T(8,128)(2,1)S(1)} %pad_maximum_fusion.2.refs_1_), channel_id=1, source_target_pairs={{0,8},{4,20},{8,0},{12,28},{16,24},{20,4},{24,16},{28,12},{1,9},{5... | collective-permute-start | bytes 2211848 | tf_op jit(solution)/shard_map/ppermute | solution.py:47
  67.3 30.8 %collective-permute-start.30 = (bf16[640,768]{1,0:T(8,128)(2,1)}, bf16[640,768]{1,0:T(8,128)(2,1)S(1)}, u32[]{:S(2)}, u32[]{:S(2)}) collective-permute-start(bf16[640,768]{1,0:T(8,128)(2,1)} %get-tuple-element.160), channel_id=1, source_target_pairs={{0,0},{1,4},{2,2},{3,6},{4,1},{5,5},{6,3},{7,7},{8,8},{9,12},{10,1... | collective-permute-start | bytes 2949128 | tf_op jit(solution)/shard_map/ppermute | solution.py:469
  89.0 45.8 %collective-permute-start.31 = (bf16[640,768]{1,0:T(8,128)(2,1)}, bf16[640,768]{1,0:T(8,128)(2,1)S(1)}, u32[]{:S(2)}, u32[]{:S(2)}) collective-permute-start(bf16[640,768]{1,0:T(8,128)(2,1)} %get-tuple-element.159), channel_id=1, source_target_pairs={{0,2},{1,6},{2,0},{3,4},{4,3},{5,7},{6,1},{7,5},{8,10},{9,14},{10,... | collective-permute-start | bytes 2949128 | tf_op jit(solution)/shard_map/ppermute | solution.py:469
  94.3 40.5 %collective-permute-start.20 = (bf16[4,96,960]{2,1,0:T(8,128)(2,1)}, bf16[4,96,960]{2,1,0:T(8,128)(2,1)S(1)}, u32[]{:S(2)}, u32[]{:S(2)}) collective-permute-start(bf16[4,96,960]{2,1,0:T(8,128)(2,1)} %collective-permute-done.18.refs_2_), channel_id=1, source_target_pairs={{0,16},{4,12},{8,24},{12,4},{16,0},{20,28},{24,8},{28,20},{1,17},{... | collective-permute-start | bytes 2211848 | tf_op jit(solution)/shard_map/ppermute | solution.py:47
  96.8 44.8 %collective-permute-start.28 = (bf16[4,96,1728]{2,1,0:T(8,128)(2,1)S(1)}, bf16[4,96,1728]{2,1,0:T(8,128)(2,1)}, u32[]{:S(2)}, u32[]{:S(2)}) collective-permute-start(bf16[4,96,1728]{2,1,0:T(8,128)(2,1)S(1)} %pad_maximum_fusion.refs_1_), channel_id=1, source_target_pairs={{0,8},{4,20},{8,0},{12,28},{16,24},{20,4},{24,16},{28,12},{1,9},{5... | collective-permute-start | bytes 3981320 | tf_op jit(solution)/shard_map/ppermute | solution.py:47
  98.1 42.0 %collective-permute-start.21 = (bf16[4,96,960]{2,1,0:T(8,128)(2,1)S(1)}, bf16[4,96,960]{2,1,0:T(8,128)(2,1)S(1)}, u32[]{:S(2)}, u32[]{:S(2)}) collective-permute-start(bf16[4,96,960]{2,1,0:T(8,128)(2,1)S(1)} %pad_maximum_fusion.2.refs_1_), channel_id=1, source_target_pairs={{0,4},{4,0},{8,12},{12,8},{16,20},{20,16},{24,28},{28,24},{1,5},{5... | collective-permute-start | bytes 2211848 | tf_op jit(solution)/shard_map/ppermute | solution.py:42
  110.4 32.1 %collective-permute-start.22 = (bf16[4,96,960]{2,1,0:T(8,128)(2,1)}, bf16[4,96,960]{2,1,0:T(8,128)(2,1)S(1)}, u32[]{:S(2)}, u32[]{:S(2)}) collective-permute-start(bf16[4,96,960]{2,1,0:T(8,128)(2,1)} %collective-permute-done.18.refs_2_), channel_id=1, source_target_pairs={{0,4},{4,0},{8,12},{12,8},{16,20},{20,16},{24,28},{28,24},{1,5},{5... | collective-permute-start | bytes 2211848 | tf_op jit(solution)/shard_map/ppermute | solution.py:42
  140.1 38.0 %collective-permute-start.32 = (bf16[1280,1536]{1,0:T(8,128)(2,1)}, bf16[1280,1536]{1,0:T(8,128)(2,1)}, u32[]{:S(2)}, u32[]{:S(2)}) collective-permute-start(bf16[1280,1536]{1,0:T(8,128)(2,1)} %convolution_convert_fusion.refs_3_.refs_4_.refs_6_.refs_7_), channel_id=1, source_target_pairs={{0,4},{4,0},{8,12},{12,8},{16,20},{20,16},{24,28},{28,24},{1,5},{5... | collective-permute-start | bytes 11796488 | tf_op jit(solution)/shard_map/ppermute | solution.py:42
  140.5 35.8 %collective-permute-start.29 = (bf16[4,96,1728]{2,1,0:T(8,128)(2,1)S(1)}, bf16[4,96,1728]{2,1,0:T(8,128)(2,1)S(1)}, u32[]{:S(2)}, u32[]{:S(2)}) collective-permute-start(bf16[4,96,1728]{2,1,0:T(8,128)(2,1)S(1)} %pad_maximum_fusion.refs_1_), channel_id=1, source_target_pairs={{0,16},{4,12},{8,24},{12,4},{16,0},{20,28},{24,8},{28,20},{1,17},{... | collective-permute-start | bytes 3981320 | tf_op jit(solution)/shard_map/ppermute | solution.py:47
  141.7 36.3 %collective-permute-start.33 = (bf16[4,96,1728]{2,1,0:T(8,128)(2,1)}, bf16[4,96,1728]{2,1,0:T(8,128)(2,1)}, u32[]{:S(2)}, u32[]{:S(2)}) collective-permute-start(bf16[4,96,1728]{2,1,0:T(8,128)(2,1)} %collective-permute-done.28.refs_0_.refs_2_), channel_id=1, source_target_pairs={{0,16},{4,12},{8,24},{12,4},{16,0},{20,28},{24,8},{28,20},{1,17},{... | collective-permute-start | bytes 3981320 | tf_op jit(solution)/shard_map/ppermute | solution.py:47
  174.0 30.4 %collective-permute-start.34 = (bf16[4,96,1728]{2,1,0:T(8,128)(2,1)S(1)}, bf16[4,96,1728]{2,1,0:T(8,128)(2,1)S(1)}, u32[]{:S(2)}, u32[]{:S(2)}) collective-permute-start(bf16[4,96,1728]{2,1,0:T(8,128)(2,1)S(1)} %pad_maximum_fusion.refs_1_), channel_id=1, source_target_pairs={{0,4},{4,0},{8,12},{12,8},{16,20},{20,16},{24,28},{28,24},{1,5},{5... | collective-permute-start | bytes 3981320 | tf_op jit(solution)/shard_map/ppermute | solution.py:42
  248.0 66.4 %collective-permute-start.42 = (bf16[384,6912]{1,0:T(8,128)(2,1)}, bf16[384,6912]{1,0:T(8,128)(2,1)}, u32[]{:S(2)}, u32[]{:S(2)}) collective-permute-start(bf16[384,6912]{1,0:T(8,128)(2,1)} %get-tuple-element.72), channel_id=1, source_target_pairs={{0,4},{4,0},{8,12},{12,8},{16,20},{20,16},{24,28},{28,24},{1,5},{5... | collective-permute-start | bytes 15925256 | tf_op jit(solution)/shard_map/ppermute | solution.py:42
  324.6 32.3 %collective-permute-start.45 = (bf16[192,6912]{1,0:T(8,128)(2,1)}, bf16[192,6912]{1,0:T(8,128)(2,1)}, u32[]{:S(2)}, u32[]{:S(2)}) collective-permute-start(bf16[192,6912]{1,0:T(8,128)(2,1)} %get-tuple-element.79), channel_id=1, source_target_pairs={{0,8},{4,20},{8,0},{12,28},{16,24},{20,4},{24,16},{28,12},{1,9},{5... | collective-permute-start | bytes 7962632 | tf_op jit(solution)/shard_map/ppermute | solution.py:47
  325.9 65.6 %collective-permute-start.38 = (bf16[256,768]{1,0:T(8,128)(2,1)S(1)}, bf16[256,768]{1,0:T(8,128)(2,1)}, u32[]{:S(2)}, u32[]{:S(2)}) collective-permute-start(bf16[256,768]{1,0:T(8,128)(2,1)S(1)} %get-tuple-element.168.refs_1_), channel_id=1, source_target_pairs={{0,0},{4,1},{2,2},{6,3},{1,4},{5,5},{3,6},{7,7},{8,8},{12,9},{10,1... | collective-permute-start | bytes 1179656 | tf_op jit(solution)/shard_map/ppermute | solution.py:529
  327.3 64.2 %collective-permute-start.39 = (bf16[256,768]{1,0:T(8,128)(2,1)S(1)}, bf16[256,768]{1,0:T(8,128)(2,1)}, u32[]{:S(2)}, u32[]{:S(2)}) collective-permute-start(bf16[256,768]{1,0:T(8,128)(2,1)S(1)} %get-tuple-element.167), channel_id=1, source_target_pairs={{2,0},{6,1},{0,2},{4,3},{3,4},{7,5},{1,6},{5,7},{10,8},{14,9},{8,1... | collective-permute-start | bytes 1179656 | tf_op jit(solution)/shard_map/ppermute | solution.py:529
  349.4 46.5 %collective-permute-start.49 = (bf16[640,768]{1,0:T(8,128)(2,1)S(1)}, bf16[640,768]{1,0:T(8,128)(2,1)}, u32[]{:S(2)}, u32[]{:S(2)}) collective-permute-start(bf16[640,768]{1,0:T(8,128)(2,1)S(1)} %get-tuple-element.83), channel_id=1, source_target_pairs={{2,0},{6,1},{0,2},{4,3},{3,4},{7,5},{1,6},{5,7},{10,8},{14,9},{8,1... | collective-permute-start | bytes 2949128 | tf_op jit(solution)/shard_map/ppermute | solution.py:529
  350.0 45.8 %collective-permute-start.48 = (bf16[640,768]{1,0:T(8,128)(2,1)S(1)}, bf16[640,768]{1,0:T(8,128)(2,1)}, u32[]{:S(2)}, u32[]{:S(2)}) collective-permute-start(bf16[640,768]{1,0:T(8,128)(2,1)S(1)} %get-tuple-element.78.refs_0_), channel_id=1, source_target_pairs={{0,0},{4,1},{2,2},{6,3},{1,4},{5,5},{3,6},{7,7},{8,8},{12,9},{10,1... | collective-permute-start | bytes 2949128 | tf_op jit(solution)/shard_map/ppermute | solution.py:529
  391.5 34.3 %collective-permute-start.51 = (bf16[384,3840]{1,0:T(8,128)(2,1)}, bf16[384,3840]{1,0:T(8,128)(2,1)}, u32[]{:S(2)}, u32[]{:S(2)}) collective-permute-start(bf16[384,3840]{1,0:T(8,128)(2,1)} %get-tuple-element.88), channel_id=1, source_target_pairs={{0,4},{4,0},{8,12},{12,8},{16,20},{20,16},{24,28},{28,24},{1,5},{5... | collective-permute-start | bytes 8847368 | tf_op jit(solution)/shard_map/ppermute | solution.py:42
  413.4 46.4 %collective-permute-start.47 = (bf16[256,768]{1,0:T(8,128)(2,1)}, bf16[256,768]{1,0:T(8,128)(2,1)}, u32[]{:S(2)}, u32[]{:S(2)}) collective-permute-start(bf16[256,768]{1,0:T(8,128)(2,1)} %get-tuple-element.163), channel_id=1, source_target_pairs={{2,0},{6,1},{0,2},{4,3},{3,4},{7,5},{1,6},{5,7},{10,8},{14,9},{8,1... | collective-permute-start | bytes 1179656 | tf_op jit(solution)/shard_map/ppermute | solution.py:529
  413.6 46.2 %collective-permute-start.46 = (bf16[256,768]{1,0:T(8,128)(2,1)}, bf16[256,768]{1,0:T(8,128)(2,1)}, u32[]{:S(2)}, u32[]{:S(2)}) collective-permute-start(bf16[256,768]{1,0:T(8,128)(2,1)} %get-tuple-element.164), channel_id=1, source_target_pairs={{0,0},{4,1},{2,2},{6,3},{1,4},{5,5},{3,6},{7,7},{8,8},{12,9},{10,1... | collective-permute-start | bytes 1179656 | tf_op jit(solution)/shard_map/ppermute | solution.py:529
  421.3 44.7 %all-to-all-start.2 = ((bf16[4,96,1728]{2,1,0:T(8,128)(2,1)}), bf16[4,96,1728]{2,1,0:T(8,128)(2,1)}, u32[]{:S(2)}, u32[]{:S(2)}) async-start(bf16[4,96,1728]{2,1,0:T(8,128)(2,1)} %sum_far.3.refs_0_.refs_1_), calls=%async_computation.2 | async-start | bytes 2752512 | tf_op jit(solution)/shard_map/all_to_all | solution.py:418
  (117 other events, 1555.9 us)

commit v4 on v3

--- a/solution.py
+++ b/solution.py
@@ -14,8 +14,8 @@
 BF = jnp.bfloat16
 F32 = jnp.float32
 MIB = 1024 * 1024
-TOOK = {'assemble': 1, 'self_forward': 1, 'self_backward': 1, 'weight_grads': 0.5, 'sum_keys': 1, 'rows_back': 1, 'sum_far': 1, 'spread': 1, 'pick_with_ids': 1, 'pick': 1, 'join': 1, 'window_bias': 1, 'cross_forward': 1, 'cross_backward': 1, 'bucket_sums': 1, 'sum_cores': 1, 'sum_paths': 2, 'feed_forward': 1, 'norm_back': 1, 'stack': 1, 'project': 1}
-OPT = {'T': 0, 'Q': 1, 'R': 0, 'S': 0, 'A': 0, 'B': 1, 'C': 0, 'D': 1, 'E': 0, 'F': 1, 'G': 0, 'H': 0, 'I': 0, 'J': 0, 'K': 0, 'L': 2, 'M': 0, 'N': 0, 'P': 1}
+TOOK = {'assemble': 3, 'self_forward': 1, 'self_backward': 1, 'weight_grads': 0.5, 'sum_keys': 1, 'rows_back': 1, 'sum_far': 1, 'spread': 1, 'pick_with_ids': 1, 'pick': 1, 'join': 1, 'window_bias': 1, 'cross_forward': 1, 'cross_backward': 1, 'bucket_sums': 1, 'sum_cores': 1, 'sum_paths': 2, 'feed_forward': 1, 'norm_back': 1, 'stack': 1, 'project': 1}
+OPT = {'T': 0, 'Q': 1, 'R': 0, 'S': 0, 'A': 0, 'B': 1, 'C': 0, 'D': 1, 'E': 0, 'F': 1, 'G': 0, 'H': 0, 'I': 0, 'J': 0, 'K': 1, 'L': 2, 'M': 0, 'N': 0, 'P': 1}
 
 
 def nn(left, right):

time: 514 us -> 513 us (level)
  waiting for transfers between devices: 95.7 us -> 59.8 us
  starting transfers between devices: 80.3 us -> 110 us
    ppermute x28, starting transfers between devices: 18.4 us -> 41.6 us  [flip(): return lax.ppermute(x, axis, [(i, i ^ bits) for i in range(size)])]
    ppermute x15, waiting for transfers between devices: 17.9 us -> 0.04 us  [two_way(): lax.ppermute(x, 'fsdp', [(i, i ^ (second if i & 1 else first)) for i in r...]
    ppermute x2, waiting for transfers between devices: 24.3 us -> 10.8 us  [gathered(): lax.ppermute(lax.dynamic_index_in_dim(x, r ^ high, 0, keepdims=False), ('...]
    ppermute x6, starting transfers between devices: 10.7 us -> 20 us  [returned(): lax.ppermute(x, ('fsdp', 'tensor'), round_moves(r, True))]
    unnamed x152 -> x158, local copies, waits for them, and re-layouts: 23.6 us -> 25.8 us
  transfers between devices with their start and end apart: 67 -> 67, of which waited for: 11 -> 8; matrix products, arithmetic and copies ran while one was open for 10% -> 11% of each run, Pallas kernels for 42% -> 42%
where the time goes in v4:
time: 513 us; the launch traced here: 503 us
  Pallas kernels  235 us (46%)
  starting transfers between devices  110 us (21%)
  waiting for transfers between devices  59.8 us (12%)
  local copies, waits for them, and re-layouts  39 us (8%)
  matrix products  34.4 us (7%)
  other arithmetic  22.7 us (4%)
    pallas_call x28, Pallas kernels, run(): pl.pallas_call(body, in_specs=[pl.BlockSpec(memory_space=pl.ANY)] * count...  235 us
    ppermute x28, starting transfers between devices, flip(): return lax.ppermute(x, axis, [(i, i ^ bits) for i in range(size)])  41.6 us
    ppermute x9, waiting for transfers between devices, shift(): return lax.ppermute(x, axis, [(i, (i + by) % size) for i in range(size)])  33.9 us
    unnamed x158, local copies, waits for them, and re-layouts  25.8 us
    dot_general x7, matrix products, nn(): return jnp.dot(left, right, preferred_element_type=F32)  21 us
    ppermute x6, starting transfers between devices, returned(): lax.ppermute(x, ('fsdp', 'tensor'), round_moves(r, True))  20 us
    ppermute x15, starting transfers between devices, two_way(): lax.ppermute(x, 'fsdp', [(i, i ^ (second if i & 1 else first)) for i in r...  15.3 us
    dot_general x8, matrix products, nt(): lax.dot_general(left, right, (((1,), (1,)), ((), ())), preferred_element_...  13.4 us
  transfers between devices with their start and end apart: 67, of which 8 were waited for; matrix products, arithmetic and copies ran while one was open for 11% of the time, Pallas kernels for 42%

profile of v4, /device:TPU:0, one launch (start us, length us, event | category | flops | bytes accessed | tf_op | source)
XLA Modules:
  0.0 503.0 jit_solution(12283034846968262186)
XLA Ops:
  31.4 10.3 %collective-permute-done.6.refs_3_.refs_2_ = bf16[96,960]{1,0:T(8,128)(2,1)S(1)} collective-permute-done((bf16[96,960]{1,0:T(8,128)(2,1)}, bf16[96,960]{1,0:T(8,128)(2,1)S(1)}, u32[]{:S(2)}, u32[]{:S(2)}) %collective-permute-start.6) | collective-permute-done | bytes 184352 | tf_op jit(solution)/shard_map/ppermute | solution.py:37
  43.7 9.1 %window_bias.1.refs_0_.refs_6_.refs_8_ = f32[12,256,256]{2,1,0:T(8,128)} custom-call(f32[3,768]{1,0:T(4,128)} %convert_element_type.94.refs_0_, bf16[96,960]{1,0:T(8,128)(2,1)} %join.3.refs_1_.refs_0_, bf16[96,960]{1,0:T(8,128)(2,1)} %copy-done.45, bf16[96,960]{1,0:T(8,128)(2,1)} %copy-done.44, bf16[96,960]{1,0:T(8,128)(2,1)} %copy-done.43, ...), custom_call_target="tpu_custom_call" | custom-call | flops 9900000256 | bytes 31500000 | tf_op jit(solution)/shard_map/window_bias/pallas_call | solution.py:137
  62.1 5.2 %collective-permute-done.27 = bf16[96,1728]{1,0:T(8,128)(2,1)} collective-permute-done((bf16[96,1728]{1,0:T(8,128)(2,1)}, bf16[96,1728]{1,0:T(8,128)(2,1)}, u32[]{:S(2)}, u32[]{:S(2)}) %collective-permute-start.27) | collective-permute-done | bytes 331808 | tf_op jit(solution)/shard_map/ppermute | solution.py:37
  67.5 18.5 %collective-permute-done.26 = bf16[96,1728]{1,0:T(8,128)(2,1)} collective-permute-done((bf16[96,1728]{1,0:T(8,128)(2,1)}, bf16[96,1728]{1,0:T(8,128)(2,1)}, u32[]{:S(2)}, u32[]{:S(2)}) %collective-permute-start.26) | collective-permute-done | bytes 331808 | tf_op jit(solution)/shard_map/ppermute | solution.py:37
  96.3 23.9 %collective-permute-start.21 = (bf16[4,96,960]{2,1,0:T(8,128)(2,1)S(1)}, bf16[4,96,960]{2,1,0:T(8,128)(2,1)S(1)}, u32[]{:S(2)}, u32[]{:S(2)}) collective-permute-start(bf16[4,96,960]{2,1,0:T(8,128)(2,1)S(1)} %pad_maximum_fusion.2.refs_1_), channel_id=1, source_target_pairs={{0,4},{4,0},{8,12},{12,8},{16,20},{20,16},{24,28},{28,24},{1,5},{5... | collective-permute-start | bytes 2211848 | tf_op jit(solution)/shard_map/ppermute | solution.py:42
  121.6 10.8 %collective-permute-done.31 = bf16[640,768]{1,0:T(8,128)(2,1)} collective-permute-done((bf16[640,768]{1,0:T(8,128)(2,1)S(1)}, bf16[640,768]{1,0:T(8,128)(2,1)}, u32[]{:S(2)}, u32[]{:S(2)}) %collective-permute-start.31) | collective-permute-done | bytes 983072 | tf_op jit(solution)/shard_map/ppermute | solution.py:469
  142.0 5.1 %assemble.4 = (bf16[768,2304]{1,0:T(8,128)(2,1)}, bf16[768,768]{1,0:T(8,128)(2,1)}, bf16[768,768]{1,0:T(8,128)(2,1)}) custom-call(f32[12,256,256]{2,1,0:T(8,128)} %window_bias.1.refs_0_.refs_6_.refs_8_, bf16[4,96,960]{2,1,0:T(8,128)(2,1)S(1)} %pad_maximum_fusion.2.refs_1_, bf16[4,96,960]{2,1,0:T(8,128)(2,1)S(1)} %collective-permute-done.18.refs_2_, ...), custom_call_target="tpu_custom_call" | custom-call | flops 15971999744 | bytes 50820000 | tf_op jit(solution)/shard_map/assemble/pallas_call | solution.py:137
  154.5 12.2 %self_forward.1.refs_7_ = bf16[512,768]{1,0:T(8,128)(2,1)} custom-call(bf16[768,1536]{1,0:T(8,128)(2,1)} %copy-done.30, bf16[512,2304]{1,0:T(8,128)(2,1)} %convolution_convert_fusion.1.refs_1_.refs_2_.refs_3_.refs_4_, bf16[512,2304]{1,0:T(8,128)(2,1)} %convolution_convert_fusion.1.refs_1_.refs_2_.refs_3_.refs_4_, ...), custom_call_target="tpu_custom_call" | custom-call | flops 13200000000 | bytes 42000000 | tf_op jit(solution)/shard_map/self_forward/pallas_call | solution.py:137
  175.2 26.3 %cross_forward.1 = (bf16[512,768]{1,0:T(8,128)(2,1)S(1)}, f32[512,768]{1,0:T(8,128)S(1)}, f32[6,8,512]{2,1,0:T(8,128)S(1)}) custom-call(bf16[4,96,1728]{2,1,0:T(8,128)(2,1)} %collective-permute-done.28.refs_0_.refs_2_, bf16[4,96,1728]{2,1,0:T(8,128)(2,1)S(1)} %collective-permute-done.29.refs_1_.refs_3_, ...), custom_call_target="tpu_custom_call" | custom-call | flops 28600000512 | bytes 91000000 | tf_op jit(solution)/shard_map/cross_forward/pallas_call | solution.py:137
  204.0 7.7 %assemble.5 = (bf16[768,3072]{1,0:T(8,128)(2,1)}, bf16[768,3072]{1,0:T(8,128)(2,1)}, bf16[768,768]{1,0:T(8,128)(2,1)S(1)}) custom-call(bf16[512,768]{1,0:T(8,128)(2,1)S(1)} %get-tuple-element.62.refs_0_.refs_6_, bf16[4,96,1728]{2,1,0:T(8,128)(2,1)S(1)} %pad_maximum_fusion.refs_1_, bf16[4,96,1728]{2,1,0:T(8,128)(2,1)} %collective-permute-done.28.refs_0_.refs_2_, ...), custom_call_target="tpu_custom_call" | custom-call | flops 26109599744 | bytes 83076000 | tf_op jit(solution)/shard_map/assemble/pallas_call | solution.py:137
  220.6 5.8 %fusion.6.refs_4_ = bf16[512,3072]{1,0:T(8,128)(2,1)S(1)} fusion(f32[512,3072]{1,0:T(8,128)S(1)} %get-tuple-element.193, bf16[512,768]{1,0:T(8,128)(2,1)S(1)} %constant_dynamic-update-slice_fusion.2.refs_2_, bf16[768,3072]{1,0:T(8,128)(2,1)S(1)} %bitcast.90), kind=kOutput, calls=%fused_computation.10 | convolution fusion | flops 2445803520 | bytes 14942208 | tf_op jit(solution)/shard_map/dot_general | solution.py:22
  233.6 13.4 %weight_grads.3 = (bf16[384,6912]{1,0:T(8,128)(2,1)}, bf16[384,6912]{1,0:T(8,128)(2,1)}) custom-call(bf16[512,768]{1,0:T(8,128)(2,1)S(1)} %convolution_convert_fusion.3.refs_0_.refs_3_, bf16[512,768]{1,0:T(8,128)(2,1)S(1)} %multiply_convert_fusion.1.refs_1_, bf16[512,768]{1,0:T(8,128)(2,1)S(1)} %constant_dynamic-update-slice_fusion.2.refs_2_, ...), custom_call_target="tpu_custom_call" | custom-call | flops 6929999872 | bytes 22050000 | tf_op jit(solution)/shard_map/weight_grads/pallas_call | solution.py:137
  247.5 65.4 %cross_backward.1 = (bf16[512,768]{1,0:T(8,128)(2,1)S(1)}, f32[1280,768]{1,0:T(8,128)}, f32[1280,768]{1,0:T(8,128)}, bf16[1280,768]{1,0:T(8,128)(2,1)}, bf16[1280,768]{1,0:T(8,128)(2,1)}) custom-call(bf16[384,6912]{1,0:T(8,128)(2,1)} %get-tuple-element.68.refs_0_.refs_1_, bf16[256,768]{1,0:T(8,128)(2,1)S(1)} %get-tuple-element.168.refs_1_, ...), custom_call_target="tpu_custom_call" | custom-call | flops 68200001536 | bytes 217000000 | tf_op jit(solution)/shard_map/cross_backward/pallas_call | solution.py:137
  313.4 8.7 %sum_cores.3 = (bf16[192,6912]{1,0:T(8,128)(2,1)S(1)}, bf16[192,6912]{1,0:T(8,128)(2,1)}) custom-call(bf16[512,768]{1,0:T(8,128)(2,1)S(1)} %get-tuple-element.71.refs_0_.refs_8_, bf16[384,6912]{1,0:T(8,128)(2,1)} %get-tuple-element.68.refs_0_.refs_1_, bf16[384,6912]{1,0:T(8,128)(2,1)} %collective-permute-done.42.refs_2_), custom_call_target="tpu_custom_call" | custom-call | flops 9732096000 | bytes 30965760 | tf_op jit(solution)/shard_map/sum_cores/pallas_call | solution.py:137
  333.1 6.7 %sum_keys.1.refs_0_.refs_2_ = bf16[1280,1536]{1,0:T(8,128)(2,1)} custom-call(bf16[192,6912]{1,0:T(8,128)(2,1)} %copy-done.27, f32[1280,768]{1,0:T(8,128)} %get-tuple-element.74.refs_1_, f32[1280,768]{1,0:T(8,128)} %get-tuple-element.75.refs_2_, bf16[1280,768]{1,0:T(8,128)(2,1)} %copy-done.63, bf16[1280,768]{1,0:T(8,128)(2,1)} %collective-permute-done.44.refs_4_), custom_call_target="tpu_custom_call" | custom-call | flops 6600000000 | bytes 21000000 | tf_op jit(solution)/shard_map/sum_keys/pallas_call | solution.py:137
  339.8 6.8 %rows_back.1 = (bf16[640,768]{1,0:T(8,128)(2,1)}, bf16[640,768]{1,0:T(8,128)(2,1)}) custom-call(bf16[1280,1536]{1,0:T(8,128)(2,1)} %sum_keys.1.refs_0_.refs_2_, bf16[768,1536]{1,0:T(8,128)(2,1)S(1)} %copy-done.31), custom_call_target="tpu_custom_call" | custom-call | flops 6600000000 | bytes 21000000 | tf_op jit(solution)/shard_map/rows_back/pallas_call | solution.py:137
  346.9 8.9 %collective-permute-start.48 = (bf16[640,768]{1,0:T(8,128)(2,1)}, bf16[640,768]{1,0:T(8,128)(2,1)}, u32[]{:S(2)}, u32[]{:S(2)}) collective-permute-start(bf16[640,768]{1,0:T(8,128)(2,1)} %get-tuple-element.78.refs_0_), channel_id=1, source_target_pairs={{0,0},{4,1},{2,2},{6,3},{1,4},{5,5},{3,6},{7,7},{8,8},{12,9},{10,1... | collective-permute-start | bytes 2949128 | tf_op jit(solution)/shard_map/ppermute | solution.py:529
  355.8 18.1 %self_backward.1 = (bf16[512,768]{1,0:T(8,128)(2,1)}, bf16[512,768]{1,0:T(8,128)(2,1)}, bf16[512,768]{1,0:T(8,128)(2,1)}, f32[12,256,256]{2,1,0:T(8,128)}) custom-call(bf16[640,768]{1,0:T(8,128)(2,1)} %get-tuple-element.78.refs_0_, bf16[192,6912]{1,0:T(8,128)(2,1)} %collective-permute-done.45.refs_1_.refs_2_, ...), custom_call_target="tpu_custom_call" | custom-call | flops 19800000512 | bytes 63000000 | tf_op jit(solution)/shard_map/self_backward/pallas_call | solution.py:137
  375.0 6.2 %sum_paths.3 = (f32[96,6912]{1,0:T(8,128)S(1)}, bf16[96,6912]{1,0:T(8,128)(2,1)S(1)}) custom-call(bf16[512,768]{1,0:T(8,128)(2,1)S(1)} %copy-done.17, bf16[192,6912]{1,0:T(8,128)(2,1)} %copy-done.27, bf16[192,6912]{1,0:T(8,128)(2,1)} %collective-permute-done.45.refs_1_.refs_2_), custom_call_target="tpu_custom_call" | custom-call | flops 9732096000 | bytes 30965760 | tf_op jit(solution)/shard_map/sum_paths/pallas_call | solution.py:137
  382.7 7.8 %weight_grads.4 = (bf16[384,3840]{1,0:T(8,128)(2,1)}, bf16[384,3840]{1,0:T(8,128)(2,1)}) custom-call(f32[96,6912]{1,0:T(8,128)} %copy-done.21, bf16[512,768]{1,0:T(8,128)(2,1)S(1)} %copy-done.7, bf16[512,768]{1,0:T(8,128)(2,1)S(1)} %get-tuple-element.153.refs_2_, bf16[512,768]{1,0:T(8,128)(2,1)S(1)} %copy-done.9, bf16[512,768]{1,0:T(8,128)(2,1)S(1)} %copy-done.17, ...), custom_call_target="tpu_custom_call" | custom-call | flops 3849999872 | bytes 12250000 | tf_op jit(solution)/shard_map/weight_grads/pallas_call | solution.py:137
  397.7 6.8 %weight_grads.5 = (bf16[384,1536]{1,0:T(8,128)(2,1)S(1)}, bf16[384,1536]{1,0:T(8,128)(2,1)}) custom-call(bf16[384,3840]{1,0:T(8,128)(2,1)} %get-tuple-element.85.refs_0_.refs_1_, bf16[1280,768]{1,0:T(8,128)(2,1)S(1)} %copy-done.3, bf16[1280,1536]{1,0:T(8,128)(2,1)} %sum_keys.1.refs_0_.refs_2_), custom_call_target="tpu_custom_call" | custom-call | flops 1540000000 | bytes 4900000 | tf_op jit(solution)/shard_map/weight_grads/pallas_call | solution.py:137
  436.7 13.6 %bucket_sums.1.refs_0_ = f32[12,32,256]{2,1,0:T(8,128)} custom-call(bf16[192,1536]{1,0:T(8,128)(2,1)} %copy-done.25, f32[12,256,256]{2,1,0:T(8,128)} %get-tuple-element.92.refs_1_, s32[256,256]{1,0:T(8,128)} %refs_2_.3), custom_call_target="tpu_custom_call" | custom-call | flops 14300000256 | bytes 45500000 | tf_op jit(solution)/shard_map/bucket_sums/pallas_call | solution.py:137
  465.8 5.1 %all-to-all-start.1 = ((bf16[4,96,384]{2,1,0:T(8,128)(2,1)}), bf16[4,96,384]{2,1,0:T(8,128)(2,1)}, u32[]{:S(2)}, u32[]{:S(2)}) async-start(bf16[4,96,384]{2,1,0:T(8,128)(2,1)} %sum_far.5), calls=%async_computation.1 | async-start | bytes 589824 | tf_op jit(solution)/shard_map/all_to_all | solution.py:418
  490.2 11.7 %all-to-all-done = bf16[4,96,960]{2,1,0:T(8,128)(2,1)S(1)} async-done(((bf16[4,96,960]{2,1,0:T(8,128)(2,1)}), bf16[4,96,960]{2,1,0:T(8,128)(2,1)S(1)}, u32[]{:S(2)}, u32[]{:S(2)}) %all-to-all-start) | async-done | bytes 737312 | tf_op jit(solution)/shard_map/all_to_all | solution.py:418
  (381 shorter events, 187.3 us)
Async XLA Ops:
  25.3 30.5 %collective-permute-start = (bf16[272,768]{1,0:T(8,128)(2,1)}, bf16[272,768]{1,0:T(8,128)(2,1)S(1)}, u32[]{:S(2)}, u32[]{:S(2)}) collective-permute-start(bf16[272,768]{1,0:T(8,128)(2,1)} %get-tuple-element.57), channel_id=1, source_target_pairs={{0,0},{1,4},{2,2},{3,6},{4,1},{5,5},{6,3},{7,7},{8,8},{9,12},{10,1... | collective-permute-start | bytes 1253384 | tf_op jit(solution)/shard_map/ppermute | solution.py:508
  27.0 28.9 %collective-permute-start.1 = (bf16[272,768]{1,0:T(8,128)(2,1)}, bf16[272,768]{1,0:T(8,128)(2,1)S(1)}, u32[]{:S(2)}, u32[]{:S(2)}) collective-permute-start(bf16[272,768]{1,0:T(8,128)(2,1)} %get-tuple-element.58), channel_id=1, source_target_pairs={{0,2},{1,6},{2,0},{3,4},{4,3},{5,7},{6,1},{7,5},{8,10},{9,14},{10,... | collective-permute-start | bytes 1253384 | tf_op jit(solution)/shard_map/ppermute | solution.py:508
  28.9 28.5 %collective-permute-start.14 = (bf16[4,96,384]{2,1,0:T(8,128)(2,1)S(1)}, bf16[4,96,384]{2,1,0:T(8,128)(2,1)S(1)}, u32[]{:S(2)}, u32[]{:S(2)}) collective-permute-start(bf16[4,96,384]{2,1,0:T(8,128)(2,1)S(1)} %pad_maximum_fusion.4.refs_1_), channel_id=1, source_target_pairs={{0,4},{4,0},{8,12},{12,8},{16,20},{20,16},{24,28},{28,24},{1,5},{5... | collective-permute-start | bytes 884744 | tf_op jit(solution)/shard_map/ppermute | solution.py:42
  55.9 30.1 %collective-permute-start.26 = (bf16[96,1728]{1,0:T(8,128)(2,1)}, bf16[96,1728]{1,0:T(8,128)(2,1)}, u32[]{:S(2)}, u32[]{:S(2)}) collective-permute-start(bf16[96,1728]{1,0:T(8,128)(2,1)} %join.5), channel_id=1, source_target_pairs={{0,2},{1,3},{2,0},{3,1},{4,6},{5,7},{6,4},{7,5},{8,10},{9,11},{10,... | collective-permute-start | bytes 995336 | tf_op jit(solution)/shard_map/ppermute | solution.py:37
  57.4 35.0 %collective-permute-start.18 = (bf16[4,96,960]{2,1,0:T(8,128)(2,1)S(1)}, bf16[4,96,960]{2,1,0:T(8,128)(2,1)S(1)}, u32[]{:S(2)}, u32[]{:S(2)}) collective-permute-start(bf16[4,96,960]{2,1,0:T(8,128)(2,1)S(1)} %pad_maximum_fusion.2.refs_1_), channel_id=1, source_target_pairs={{0,8},{4,20},{8,0},{12,28},{16,24},{20,4},{24,16},{28,12},{1,9},{5... | collective-permute-start | bytes 2211848 | tf_op jit(solution)/shard_map/ppermute | solution.py:47
  87.1 45.3 %collective-permute-start.31 = (bf16[640,768]{1,0:T(8,128)(2,1)S(1)}, bf16[640,768]{1,0:T(8,128)(2,1)}, u32[]{:S(2)}, u32[]{:S(2)}) collective-permute-start(bf16[640,768]{1,0:T(8,128)(2,1)S(1)} %copy-done.38), channel_id=1, source_target_pairs={{0,2},{1,6},{2,0},{3,4},{4,3},{5,7},{6,1},{7,5},{8,10},{9,14},{10,... | collective-permute-start | bytes 2949128 | tf_op jit(solution)/shard_map/ppermute | solution.py:469
  91.2 30.2 %collective-permute-start.19 = (bf16[4,96,960]{2,1,0:T(8,128)(2,1)S(1)}, bf16[4,96,960]{2,1,0:T(8,128)(2,1)S(1)}, u32[]{:S(2)}, u32[]{:S(2)}) collective-permute-start(bf16[4,96,960]{2,1,0:T(8,128)(2,1)S(1)} %pad_maximum_fusion.2.refs_1_), channel_id=1, source_target_pairs={{0,16},{4,12},{8,24},{12,4},{16,0},{20,28},{24,8},{28,20},{1,17},{... | collective-permute-start | bytes 2211848 | tf_op jit(solution)/shard_map/ppermute | solution.py:47
  92.4 47.7 %collective-permute-start.28 = (bf16[4,96,1728]{2,1,0:T(8,128)(2,1)S(1)}, bf16[4,96,1728]{2,1,0:T(8,128)(2,1)}, u32[]{:S(2)}, u32[]{:S(2)}) collective-permute-start(bf16[4,96,1728]{2,1,0:T(8,128)(2,1)S(1)} %pad_maximum_fusion.refs_1_), channel_id=1, source_target_pairs={{0,8},{4,20},{8,0},{12,28},{16,24},{20,4},{24,16},{28,12},{1,9},{5... | collective-permute-start | bytes 3981320 | tf_op jit(solution)/shard_map/ppermute | solution.py:47
  92.9 39.4 %collective-permute-start.20 = (bf16[4,96,960]{2,1,0:T(8,128)(2,1)S(1)}, bf16[4,96,960]{2,1,0:T(8,128)(2,1)S(1)}, u32[]{:S(2)}, u32[]{:S(2)}) collective-permute-start(bf16[4,96,960]{2,1,0:T(8,128)(2,1)S(1)} %collective-permute-done.18.refs_2_), channel_id=1, source_target_pairs={{0,16},{4,12},{8,24},{12,4},{16,0},{20,28},{24,8},{28,20},{1,17},{... | collective-permute-start | bytes 2211848 | tf_op jit(solution)/shard_map/ppermute | solution.py:47
  96.3 42.6 %collective-permute-start.21 = (bf16[4,96,960]{2,1,0:T(8,128)(2,1)S(1)}, bf16[4,96,960]{2,1,0:T(8,128)(2,1)S(1)}, u32[]{:S(2)}, u32[]{:S(2)}) collective-permute-start(bf16[4,96,960]{2,1,0:T(8,128)(2,1)S(1)} %pad_maximum_fusion.2.refs_1_), channel_id=1, source_target_pairs={{0,4},{4,0},{8,12},{12,8},{16,20},{20,16},{24,28},{28,24},{1,5},{5... | collective-permute-start | bytes 2211848 | tf_op jit(solution)/shard_map/ppermute | solution.py:42
  138.9 34.5 %collective-permute-start.29 = (bf16[4,96,1728]{2,1,0:T(8,128)(2,1)S(1)}, bf16[4,96,1728]{2,1,0:T(8,128)(2,1)S(1)}, u32[]{:S(2)}, u32[]{:S(2)}) collective-permute-start(bf16[4,96,1728]{2,1,0:T(8,128)(2,1)S(1)} %pad_maximum_fusion.refs_1_), channel_id=1, source_target_pairs={{0,16},{4,12},{8,24},{12,4},{16,0},{20,28},{24,8},{28,20},{1,17},{... | collective-permute-start | bytes 3981320 | tf_op jit(solution)/shard_map/ppermute | solution.py:47
  140.1 35.1 %collective-permute-start.32 = (bf16[1280,1536]{1,0:T(8,128)(2,1)}, bf16[1280,1536]{1,0:T(8,128)(2,1)}, u32[]{:S(2)}, u32[]{:S(2)}) collective-permute-start(bf16[1280,1536]{1,0:T(8,128)(2,1)} %convolution_convert_fusion.refs_3_.refs_4_.refs_6_.refs_7_), channel_id=1, source_target_pairs={{0,4},{4,0},{8,12},{12,8},{16,20},{20,16},{24,28},{28,24},{1,5},{5... | collective-permute-start | bytes 11796488 | tf_op jit(solution)/shard_map/ppermute | solution.py:42
  140.1 35.0 %collective-permute-start.33 = (bf16[4,96,1728]{2,1,0:T(8,128)(2,1)}, bf16[4,96,1728]{2,1,0:T(8,128)(2,1)}, u32[]{:S(2)}, u32[]{:S(2)}) collective-permute-start(bf16[4,96,1728]{2,1,0:T(8,128)(2,1)} %collective-permute-done.28.refs_0_.refs_2_), channel_id=1, source_target_pairs={{0,16},{4,12},{8,24},{12,4},{16,0},{20,28},{24,8},{28,20},{1,17},{... | collective-permute-start | bytes 3981320 | tf_op jit(solution)/shard_map/ppermute | solution.py:47
  171.4 30.1 %collective-permute-start.34 = (bf16[4,96,1728]{2,1,0:T(8,128)(2,1)S(1)}, bf16[4,96,1728]{2,1,0:T(8,128)(2,1)S(1)}, u32[]{:S(2)}, u32[]{:S(2)}) collective-permute-start(bf16[4,96,1728]{2,1,0:T(8,128)(2,1)S(1)} %pad_maximum_fusion.refs_1_), channel_id=1, source_target_pairs={{0,4},{4,0},{8,12},{12,8},{16,20},{20,16},{24,28},{28,24},{1,5},{5... | collective-permute-start | bytes 3981320 | tf_op jit(solution)/shard_map/ppermute | solution.py:42
  173.4 28.1 %collective-permute-start.35 = (bf16[4,96,1728]{2,1,0:T(8,128)(2,1)}, bf16[4,96,1728]{2,1,0:T(8,128)(2,1)S(1)}, u32[]{:S(2)}, u32[]{:S(2)}) collective-permute-start(bf16[4,96,1728]{2,1,0:T(8,128)(2,1)} %collective-permute-done.28.refs_0_.refs_2_), channel_id=1, source_target_pairs={{0,4},{4,0},{8,12},{12,8},{16,20},{20,16},{24,28},{28,24},{1,5},{5... | collective-permute-start | bytes 3981320 | tf_op jit(solution)/shard_map/ppermute | solution.py:42
  247.0 66.4 %collective-permute-start.42 = (bf16[384,6912]{1,0:T(8,128)(2,1)}, bf16[384,6912]{1,0:T(8,128)(2,1)}, u32[]{:S(2)}, u32[]{:S(2)}) collective-permute-start(bf16[384,6912]{1,0:T(8,128)(2,1)} %get-tuple-element.72), channel_id=1, source_target_pairs={{0,4},{4,0},{8,12},{12,8},{16,20},{20,16},{24,28},{28,24},{1,5},{5... | collective-permute-start | bytes 15925256 | tf_op jit(solution)/shard_map/ppermute | solution.py:42
  322.1 33.7 %collective-permute-start.45 = (bf16[192,6912]{1,0:T(8,128)(2,1)}, bf16[192,6912]{1,0:T(8,128)(2,1)}, u32[]{:S(2)}, u32[]{:S(2)}) collective-permute-start(bf16[192,6912]{1,0:T(8,128)(2,1)} %get-tuple-element.79), channel_id=1, source_target_pairs={{0,8},{4,20},{8,0},{12,28},{16,24},{20,4},{24,16},{28,12},{1,9},{5... | collective-permute-start | bytes 7962632 | tf_op jit(solution)/shard_map/ppermute | solution.py:47
  323.5 67.0 %collective-permute-start.38 = (bf16[256,768]{1,0:T(8,128)(2,1)S(1)}, bf16[256,768]{1,0:T(8,128)(2,1)}, u32[]{:S(2)}, u32[]{:S(2)}) collective-permute-start(bf16[256,768]{1,0:T(8,128)(2,1)S(1)} %get-tuple-element.168.refs_1_), channel_id=1, source_target_pairs={{0,0},{4,1},{2,2},{6,3},{1,4},{5,5},{3,6},{7,7},{8,8},{12,9},{10,1... | collective-permute-start | bytes 1179656 | tf_op jit(solution)/shard_map/ppermute | solution.py:529
  324.9 65.6 %collective-permute-start.39 = (bf16[256,768]{1,0:T(8,128)(2,1)}, bf16[256,768]{1,0:T(8,128)(2,1)}, u32[]{:S(2)}, u32[]{:S(2)}) collective-permute-start(bf16[256,768]{1,0:T(8,128)(2,1)} %get-tuple-element.167), channel_id=1, source_target_pairs={{2,0},{6,1},{0,2},{4,3},{3,4},{7,5},{1,6},{5,7},{10,8},{14,9},{8,1... | collective-permute-start | bytes 1179656 | tf_op jit(solution)/shard_map/ppermute | solution.py:529
  346.6 46.4 %collective-permute-start.49 = (bf16[640,768]{1,0:T(8,128)(2,1)}, bf16[640,768]{1,0:T(8,128)(2,1)}, u32[]{:S(2)}, u32[]{:S(2)}) collective-permute-start(bf16[640,768]{1,0:T(8,128)(2,1)} %get-tuple-element.83), channel_id=1, source_target_pairs={{2,0},{6,1},{0,2},{4,3},{3,4},{7,5},{1,6},{5,7},{10,8},{14,9},{8,1... | collective-permute-start | bytes 2949128 | tf_op jit(solution)/shard_map/ppermute | solution.py:529
  346.9 46.1 %collective-permute-start.48 = (bf16[640,768]{1,0:T(8,128)(2,1)}, bf16[640,768]{1,0:T(8,128)(2,1)}, u32[]{:S(2)}, u32[]{:S(2)}) collective-permute-start(bf16[640,768]{1,0:T(8,128)(2,1)} %get-tuple-element.78.refs_0_), channel_id=1, source_target_pairs={{0,0},{4,1},{2,2},{6,3},{1,4},{5,5},{3,6},{7,7},{8,8},{12,9},{10,1... | collective-permute-start | bytes 2949128 | tf_op jit(solution)/shard_map/ppermute | solution.py:529
  410.3 49.2 %collective-permute-start.47 = (bf16[256,768]{1,0:T(8,128)(2,1)}, bf16[256,768]{1,0:T(8,128)(2,1)}, u32[]{:S(2)}, u32[]{:S(2)}) collective-permute-start(bf16[256,768]{1,0:T(8,128)(2,1)} %get-tuple-element.163), channel_id=1, source_target_pairs={{2,0},{6,1},{0,2},{4,3},{3,4},{7,5},{1,6},{5,7},{10,8},{14,9},{8,1... | collective-permute-start | bytes 1179656 | tf_op jit(solution)/shard_map/ppermute | solution.py:529
  412.5 46.9 %collective-permute-start.46 = (bf16[256,768]{1,0:T(8,128)(2,1)}, bf16[256,768]{1,0:T(8,128)(2,1)}, u32[]{:S(2)}, u32[]{:S(2)}) collective-permute-start(bf16[256,768]{1,0:T(8,128)(2,1)} %get-tuple-element.164), channel_id=1, source_target_pairs={{0,0},{4,1},{2,2},{6,3},{1,4},{5,5},{3,6},{7,7},{8,8},{12,9},{10,1... | collective-permute-start | bytes 1179656 | tf_op jit(solution)/shard_map/ppermute | solution.py:529
  426.0 39.8 %all-to-all-start.2 = ((bf16[4,96,1728]{2,1,0:T(8,128)(2,1)}), bf16[4,96,1728]{2,1,0:T(8,128)(2,1)}, u32[]{:S(2)}, u32[]{:S(2)}) async-start(bf16[4,96,1728]{2,1,0:T(8,128)(2,1)} %sum_far.3.refs_1_), calls=%async_computation.2 | async-start | bytes 2752512 | tf_op jit(solution)/shard_map/all_to_all | solution.py:418
  (120 other events, 1488.5 us)
